TPU v7x, 32 devices: a whole 2x2x4 slice. The times are simulated.
32 devices in a mesh: px: 4 (over z), py: 8 (over y, x, core).
Axes of the slice: x: 2, y: 2, z: 4, core: 2. Of those that a mesh axis runs over, the one named last changes fastest.
Arguments:
- positions: float32 [8192, 3, 128], P(('px', 'py')), may hold values from 1 to 254, as said below
- strength: float32 [8192, 128], P(('px', 'py')), may hold values from -6 to 6
- destination: int32 [8192, 1], P(('px', 'py')), may hold values from 0 to 31; in each aligned block of 256 rows (0 to 255, 256 to 511, ...) at most 16 rows name the same one
- tile_index: int32 [8192], P(('px', 'py')), may hold values from 0 to 63
- particle_count: int32 [8192], P(('px', 'py')), may hold values from 1 to 128, 786432 in all
Outputs:
- spectrum: float32 [2, 512, 512, 256], P(None, 'px', 'py')
Inputs may be any that keep to these rules, and one draw needn't show every extreme that they name: `destination`: among the 256 rows of one device no pencil is named more than 16 times; pencil index is i_px * 8 + i_py. `positions`: component 0 lies in [1, 14], component 1 in [1, 6], component 2 in [1, 254].
All inputs are finite; a program needn't handle non-finite values. No bound on the sum of `particle_count` on one device may be relied on, other than what follows from the above.
Results may differ from a plain program's by a relative error of at most 0.0003.
Values sent between devices are 32-bit elements; how exact they have to be, the bound alone decides.
No kernel may reach another device: no remote copies, remote signals or barrier semaphores. Data moves between devices by JAX's collectives and lax.ppermute only.
A program may use at most 192 MiB of HBM per device.

v0:
```python
import math

import jax
import jax.numpy as jnp
import numpy as np
from jax import lax
from jax.sharding import PartitionSpec as P

NX = 512
NY = 512
NZ = 256
BX = 16
BY = 8


def spline_weight(offset):
    distance = jnp.abs(offset)
    inner_part = 1.0 - 2.5 * distance * distance + 1.5 * distance * distance * distance
    outer_part = 0.5 * (2.0 - distance) * (2.0 - distance) * (1.0 - distance)
    return jnp.where(distance < 1.0, inner_part, jnp.where(distance < 2.0, outer_part, 0.0))


def row_blocks(coords, weights):
    row_count = coords.shape[0]
    row_width = coords.shape[2]
    along_x = spline_weight(coords[:, 0, :, None] - jnp.arange(BX).astype(coords.dtype))
    along_y = spline_weight(coords[:, 1, :, None] - jnp.arange(BY).astype(coords.dtype))
    along_z = spline_weight(coords[:, 2, :, None] - jnp.arange(NZ).astype(coords.dtype))
    planar = weights[:, :, None, None] * along_x[:, :, :, None] * along_y[:, :, None, :]
    planar = planar.reshape(row_count, row_width, BX * BY)
    return jnp.einsum("rpa,rpz->raz", planar, along_z, precision=lax.Precision.HIGHEST)


def reverse_digits(value, levels):
    result = 0
    for position in range(levels):
        result = result * 2 + (value >> position & 1)
    return result


def ordered_table(devices, length):
    levels = devices.bit_length() - 1
    local_len = length // devices
    freq_list = np.array(
        [
            reverse_digits(owner_idx, levels) + devices * within
            for owner_idx in range(devices)
            for within in range(local_len)
        ],
        dtype=np.int32,
    )
    freqs = jnp.asarray(freq_list)
    cells = jnp.arange(length, dtype=jnp.int32)
    angle = 2.0 * math.pi / length * (freqs[:, None] * cells[None, :] % length).astype(jnp.float32)
    return (jnp.cos(angle), jnp.sin(angle))


def local(positions, strength, destination, tile_index, particle_count):
    highest = lax.Precision.HIGHEST
    row_total = positions.shape[0]
    row_width = positions.shape[2]
    rows_x = lax.axis_size("px")
    cols_y = lax.axis_size("py")
    devices = rows_x * cols_y
    capacity = max(2, 2 * row_total // devices)
    slot_total = devices * capacity
    alive_mask = jnp.arange(row_width, dtype=jnp.int32)[None, :] < particle_count[:, None]
    strength_live = jnp.where(alive_mask, strength, jnp.zeros_like(strength))
    target = destination[:, 0]
    hit_table = (target[:, None] == jnp.arange(devices, dtype=jnp.int32)[None, :]).astype(jnp.int32)
    earlier = jnp.cumsum(hit_table, axis=0) - hit_table
    ranking = jnp.sum(earlier * hit_table, axis=1)
    slot_of = target * capacity + ranking
    send_coords = jnp.zeros((slot_total, 3, row_width), positions.dtype).at[slot_of].set(positions)
    send_weights = jnp.zeros((slot_total, row_width), strength.dtype).at[slot_of].set(strength_live)
    send_tiles = jnp.full((slot_total,), -1, jnp.int32).at[slot_of].set(tile_index)
    got_coords, got_weights, got_tiles = (
        lax.all_to_all(send_coords, ("px", "py"), split_axis=0, concat_axis=0, tiled=True),
        lax.all_to_all(send_weights, ("px", "py"), split_axis=0, concat_axis=0, tiled=True),
        lax.all_to_all(send_tiles, ("px", "py"), split_axis=0, concat_axis=0, tiled=True),
    )
    width_x = NX // rows_x
    width_y = NY // cols_y
    across_x = width_x // BX
    across_y = width_y // BY
    tile_count = across_x * across_y
    group_rows = 64
    tile_ids = jnp.arange(tile_count, dtype=jnp.int32)

    def deposit(carried, number):
        first_row = number * group_rows
        coords = lax.dynamic_slice_in_dim(got_coords, first_row, group_rows, 0)
        weights = lax.dynamic_slice_in_dim(got_weights, first_row, group_rows, 0)
        places = lax.dynamic_slice_in_dim(got_tiles, first_row, group_rows, 0)
        member = (tile_ids[:, None] == places[None, :]).astype(jnp.float32)
        blocks = row_blocks(coords, weights)
        return (carried + jnp.einsum("tg,gaz->taz", member, blocks, precision=highest), None)

    initial = jnp.zeros((tile_count, BX * BY, NZ), jnp.float32)
    tile_sums, _ = lax.scan(deposit, initial, jnp.arange(slot_total // group_rows, dtype=jnp.int32))
    vort_field = (
        tile_sums.reshape(across_x, across_y, BX, BY, NZ)
        .transpose(0, 2, 1, 3, 4)
        .reshape(width_x, width_y, NZ)
    )
    norm_scale = 1.0 / math.sqrt(NX * NY)
    plane_len = NZ // devices
    outgoing = (
        vort_field.reshape(width_x, width_y, devices, plane_len)
        .transpose(2, 3, 0, 1)
        .reshape(devices, plane_len, width_x * width_y)
    )
    arrived = lax.all_to_all(outgoing, ("px", "py"), split_axis=0, concat_axis=0, tiled=True)
    planes = (
        arrived.reshape(rows_x, cols_y, plane_len, width_x, width_y)
        .transpose(2, 0, 3, 1, 4)
        .reshape(plane_len, NX, NY)
    )
    cos_x, sin_x = ordered_table(rows_x, NX)
    cos_y, sin_y = ordered_table(cols_y, NY)
    half_real = jnp.einsum("kx,zxy->zky", cos_x, planes, precision=highest)
    half_imag = -jnp.einsum("kx,zxy->zky", sin_x, planes, precision=highest)
    full_real = jnp.einsum("ly,zky->zkl", cos_y, half_real, precision=highest) + jnp.einsum(
        "ly,zky->zkl", sin_y, half_imag, precision=highest
    )
    full_imag = jnp.einsum("ly,zky->zkl", cos_y, half_imag, precision=highest) - jnp.einsum(
        "ly,zky->zkl", sin_y, half_real, precision=highest
    )

    def to_pencils(values):
        return (
            values.reshape(plane_len, rows_x, width_x, cols_y, width_y)
            .transpose(1, 3, 0, 2, 4)
            .reshape(devices, plane_len, width_x * width_y)
        )

    back_real, back_imag = (
        lax.all_to_all(
            to_pencils(full_real), ("px", "py"), split_axis=0, concat_axis=0, tiled=True
        ),
        lax.all_to_all(
            to_pencils(full_imag), ("px", "py"), split_axis=0, concat_axis=0, tiled=True
        ),
    )

    def to_field(values):
        return values.reshape(NZ, width_x, width_y).transpose(1, 2, 0)

    return jnp.stack([to_field(back_real), to_field(back_imag)]) * norm_scale


def solution(mesh):
    placed = (
        P(("px", "py"), None, None),
        P(("px", "py"), None),
        P(("px", "py"), None),
        P(("px", "py")),
        P(("px", "py")),
    )
    return jax.shard_map(
        local, mesh=mesh, in_specs=placed, out_specs=P(None, "px", "py", None), check_vma=False
    )
```

profile of v0, /device:TPU:17, one launch (start us, length us, event | category | flops | bytes accessed | tf_op | source)
XLA Modules:
  0.0 1230.3 jit_solution(11362761812831487968)
XLA Ops:
  13.8 25.9 %scatter_fusion = f32[512,3,128]{2,1,0:T(4,128)} fusion(f32[512,3,128]{2,1,0:T(4,128)} %broadcast_in_dim.34, s32[256]{0:T(256)S(1)} %bitcast.125, f32[256,3,128]{2,1,0:T(4,128)S(1)} %copy.63), kind=kCustom, calls=%fused_computation.2 | custom fusion | bytes 1180672 | tf_op jit(solution)/shard_map/scatter | solution.py:74
  47.8 22.7 %all-to-all-done.2 = f32[512,3,128]{2,1,0:T(4,128)S(1)} async-done(((f32[512,3,128]{2,1,0:T(4,128)}), f32[512,3,128]{2,1,0:T(4,128)S(1)}, u32[]{:S(2)}, u32[]{:S(2)}) %all-to-all-start.2) | async-done | bytes 786464 | tf_op jit(solution)/shard_map/all_to_all | solution.py:78
  84.1 248.7 %while.11 = (s32[]{:T(128)}, f32[64,128,256]{2,0,1:T(8,128)}, s32[8]{0:T(128)S(1)}, s32[512]{0:T(512)S(1)}, f32[512,128]{1,0:T(8,128)S(1)}, /*index=5*/f32[512,3...) while((s32[]{:T(128)}, f32[64,128,256]{2,0,1:T(8,128)}, ...), condition=%wide.region_7.8_spmd.clone, body=%wide.region_6.7_spmd.clone.sunk | while | flops 4878503936 | bytes 94244080 | solution.py:100
  86.5 13.2 %fusion.152 = f32[64,128,256]{2,1,0:T(8,128)S(1)} fusion(f32[256]{0:T(256)S(1)} %iota_convert_fusion.6, f32[64,128]{1,0:T(8,128)S(1)} %get-tuple-element.145, f32[64,128,8]{1,2,0:T(8,128)S(1)} %fusion.150, f32[64,128,16]{1,2,0:T(8,128)S(1)} %fusion.151), kind=kOutput, calls=%fused_computation.10.clone.1 | convolution fusion | flops 3260022784 | bytes 9208832 | tf_op jit(solution)/shard_map/while/body/eval_jaxpr/rpa,rpz->raz/dot_general | solution.py:31
  99.7 10.9 select_add_fusion.2
  116.1 13.2 %fusion.152 = f32[64,128,256]{2,1,0:T(8,128)S(1)} fusion(f32[256]{0:T(256)S(1)} %iota_convert_fusion.6, f32[64,128]{1,0:T(8,128)S(1)} %get-tuple-element.145, f32[64,128,8]{1,2,0:T(8,128)S(1)} %fusion.150, f32[64,128,16]{1,2,0:T(8,128)S(1)} %fusion.151), kind=kOutput, calls=%fused_computation.10.clone.1 | convolution fusion | flops 3260022784 | bytes 9208832 | tf_op jit(solution)/shard_map/while/body/eval_jaxpr/rpa,rpz->raz/dot_general | solution.py:31
  129.3 10.9 select_add_fusion.2
  145.7 13.2 %fusion.152 = f32[64,128,256]{2,1,0:T(8,128)S(1)} fusion(f32[256]{0:T(256)S(1)} %iota_convert_fusion.6, f32[64,128]{1,0:T(8,128)S(1)} %get-tuple-element.145, f32[64,128,8]{1,2,0:T(8,128)S(1)} %fusion.150, f32[64,128,16]{1,2,0:T(8,128)S(1)} %fusion.151), kind=kOutput, calls=%fused_computation.10.clone.1 | convolution fusion | flops 3260022784 | bytes 9208832 | tf_op jit(solution)/shard_map/while/body/eval_jaxpr/rpa,rpz->raz/dot_general | solution.py:31
  158.9 10.9 select_add_fusion.2
  175.3 13.2 %fusion.152 = f32[64,128,256]{2,1,0:T(8,128)S(1)} fusion(f32[256]{0:T(256)S(1)} %iota_convert_fusion.6, f32[64,128]{1,0:T(8,128)S(1)} %get-tuple-element.145, f32[64,128,8]{1,2,0:T(8,128)S(1)} %fusion.150, f32[64,128,16]{1,2,0:T(8,128)S(1)} %fusion.151), kind=kOutput, calls=%fused_computation.10.clone.1 | convolution fusion | flops 3260022784 | bytes 9208832 | tf_op jit(solution)/shard_map/while/body/eval_jaxpr/rpa,rpz->raz/dot_general | solution.py:31
  188.5 10.9 select_add_fusion.2
  204.9 13.2 %fusion.152 = f32[64,128,256]{2,1,0:T(8,128)S(1)} fusion(f32[256]{0:T(256)S(1)} %iota_convert_fusion.6, f32[64,128]{1,0:T(8,128)S(1)} %get-tuple-element.145, f32[64,128,8]{1,2,0:T(8,128)S(1)} %fusion.150, f32[64,128,16]{1,2,0:T(8,128)S(1)} %fusion.151), kind=kOutput, calls=%fused_computation.10.clone.1 | convolution fusion | flops 3260022784 | bytes 9208832 | tf_op jit(solution)/shard_map/while/body/eval_jaxpr/rpa,rpz->raz/dot_general | solution.py:31
  218.1 10.9 select_add_fusion.2
  234.5 13.2 %fusion.152 = f32[64,128,256]{2,1,0:T(8,128)S(1)} fusion(f32[256]{0:T(256)S(1)} %iota_convert_fusion.6, f32[64,128]{1,0:T(8,128)S(1)} %get-tuple-element.145, f32[64,128,8]{1,2,0:T(8,128)S(1)} %fusion.150, f32[64,128,16]{1,2,0:T(8,128)S(1)} %fusion.151), kind=kOutput, calls=%fused_computation.10.clone.1 | convolution fusion | flops 3260022784 | bytes 9208832 | tf_op jit(solution)/shard_map/while/body/eval_jaxpr/rpa,rpz->raz/dot_general | solution.py:31
  247.8 10.9 select_add_fusion.2
  264.1 13.2 %fusion.152 = f32[64,128,256]{2,1,0:T(8,128)S(1)} fusion(f32[256]{0:T(256)S(1)} %iota_convert_fusion.6, f32[64,128]{1,0:T(8,128)S(1)} %get-tuple-element.145, f32[64,128,8]{1,2,0:T(8,128)S(1)} %fusion.150, f32[64,128,16]{1,2,0:T(8,128)S(1)} %fusion.151), kind=kOutput, calls=%fused_computation.10.clone.1 | convolution fusion | flops 3260022784 | bytes 9208832 | tf_op jit(solution)/shard_map/while/body/eval_jaxpr/rpa,rpz->raz/dot_general | solution.py:31
  277.4 10.9 select_add_fusion.2
  293.7 13.2 %fusion.152 = f32[64,128,256]{2,1,0:T(8,128)S(1)} fusion(f32[256]{0:T(256)S(1)} %iota_convert_fusion.6, f32[64,128]{1,0:T(8,128)S(1)} %get-tuple-element.145, f32[64,128,8]{1,2,0:T(8,128)S(1)} %fusion.150, f32[64,128,16]{1,2,0:T(8,128)S(1)} %fusion.151), kind=kOutput, calls=%fused_computation.10.clone.1 | convolution fusion | flops 3260022784 | bytes 9208832 | tf_op jit(solution)/shard_map/while/body/eval_jaxpr/rpa,rpz->raz/dot_general | solution.py:31
  307.0 10.9 select_add_fusion.2
  332.7 27.8 %copy.65 = f32[8,8,16,8,256]{2,0,4,3,1:T(8,128)} copy(f32[8,8,16,8,256]{4,1,0,3,2:T(8,128)} %bitcast.113) | data formatting | bytes 16777216 | tf_op jit(solution)/shard_map/reshape | solution.py:102
  360.5 41.7 %reshape_reshape.3 = f32[128,64,32,8]{0,3,2,1:T(8,128)} reshape(f32[8,16,8,8,256]{1,0,4,3,2:T(8,128)} %bitcast.9) | data formatting | bytes 16777216 | tf_op jit(solution)/shard_map/reshape;reshape | solution.py:109
  402.2 12.3 %copy.66 = f32[32,8,128,64]{3,2,1,0:T(8,128)} copy(f32[32,8,128,64]{2,1,0,3:T(8,128)} %bitcast.115) | data formatting | bytes 16777216 | tf_op jit(solution)/shard_map/transpose | solution.py:110
  414.5 14.7 %reshape.120 = f32[32,8,8192]{2,1,0:T(8,128)} reshape(f32[32,8,128,64]{3,2,1,0:T(8,128)} %copy.66) | data formatting | bytes 16777216 | tf_op jit(solution)/shard_map/reshape | solution.py:111
  429.3 188.0 %all_to_all.44 = f32[32,8,8192]{2,1,0:T(8,128)} all-to-all(f32[32,8,8192]{2,1,0:T(8,128)} %reshape.120), channel_id=1, replica_groups=mesh['px'=4,'py'=8] {'px','py'}, dimensions={0} | all-to-all | bytes 16777216 | tf_op jit(solution)/shard_map/all_to_all | solution.py:113
  617.2 14.2 %reshape.121 = f32[4,8,8,128,64]{4,3,2,1,0:T(8,128)} reshape(f32[32,8,8192]{2,1,0:T(8,128)} %all_to_all.44) | data formatting | bytes 16777216 | tf_op jit(solution)/shard_map/reshape | solution.py:115
  631.4 14.5 %copy.67 = f32[8,4,128,8,64]{2,1,4,3,0:T(4,128)} copy(f32[8,4,128,8,64]{4,2,0,3,1:T(8,128)} %bitcast.114) | data formatting | bytes 16777216 | tf_op jit(solution)/shard_map/transpose | solution.py:116
  645.9 10.3 reshape.122
  656.2 24.2 %fusion.80 = f32[8,512,512]{2,1,0:T(8,128)S(1)} fusion(f32[8,512,512]{1,2,0:T(8,128)} %reshape.122, s32[512]{0:T(512)S(1)} %copy-done.5), kind=kOutput, calls=%fused_computation.99 | convolution fusion | flops 12888571904 | bytes 16779264 | tf_op jit(solution)/shard_map/kx,zxy->zky/dot_general | solution.py:122
  680.5 17.5 %fusion.84 = f32[8,512,512]{2,1,0:T(8,128)S(1)} fusion(f32[8,512,512]{1,2,0:T(8,128)S(1)} %copy-done.3, s32[512]{0:T(512)S(1)} %copy-done.5), kind=kOutput, calls=%fused_computation.103 | convolution fusion | flops 12888571904 | bytes 16779264 | tf_op jit(solution)/shard_map/kx,zxy->zky/dot_general | solution.py:121
  698.0 35.4 %fusion.58 = f32[8,512,512]{2,1,0:T(8,128)S(1)} fusion(f32[8,512,512]{2,1,0:T(8,128)S(1)} %fusion.80, s32[512]{0:T(512)S(1)} %copy-done.4), kind=kOutput, calls=%fused_computation.75 | convolution fusion | flops 12890669056 | bytes 16779264 | tf_op jit(solution)/shard_map/ly,zky->zkl/dot_general | solution.py:123
  733.4 31.6 %fusion.66 = f32[8,512,512]{2,1,0:T(8,128)} fusion(f32[8,512,512]{2,1,0:T(8,128)S(1)} %fusion.58, f32[8,512,512]{2,1,0:T(8,128)S(1)} %fusion.84, s32[512]{0:T(512)S(1)} %copy-done.4), kind=kOutput, calls=%fused_computation.83 | convolution fusion | flops 12890669056 | bytes 25167872 | tf_op jit(solution)/shard_map/ly,zky->zkl/dot_general | solution.py:123
  765.0 9.1 copy.70
  774.2 9.9 reshape.123
  784.1 13.8 %copy.71 = f32[4,8,8,128,64]{4,3,2,1,0:T(8,128)} copy(f32[4,8,8,128,64]{3,0,4,1,2:T(4,128)} %bitcast.116) | data formatting | bytes 16777216 | tf_op jit(solution)/shard_map/transpose | solution.py:133
  797.8 14.7 %reshape.124 = f32[32,8,8192]{2,1,0:T(8,128)} reshape(f32[4,8,8,128,64]{4,3,2,1,0:T(8,128)} %copy.71) | data formatting | bytes 16777216 | tf_op jit(solution)/shard_map/reshape | solution.py:134
  817.6 35.9 %fusion.56 = f32[8,512,512]{2,1,0:T(8,128)S(1)} fusion(f32[8,512,512]{2,1,0:T(8,128)} %copy-done.2, s32[512]{0:T(512)S(1)} %copy-done.4), kind=kOutput, calls=%fused_computation.73 | convolution fusion | flops 12890669056 | bytes 16779264 | tf_op jit(solution)/shard_map/ly,zky->zkl/dot_general | solution.py:126
  853.5 37.3 %fusion.69 = f32[8,512,512]{2,1,0:T(8,128)} fusion(f32[8,512,512]{2,1,0:T(8,128)S(1)} %fusion.56, f32[8,512,512]{2,1,0:T(8,128)} %copy-done.1, s32[512]{0:T(512)S(1)} %copy-done.4), kind=kOutput, calls=%fused_computation.84 | convolution fusion | flops 12890669056 | bytes 25167872 | tf_op jit(solution)/shard_map/ly,zky->zkl/dot_general | solution.py:126
  890.8 9.1 copy.75
  899.9 9.9 reshape.126
  909.9 13.8 %copy.76 = f32[4,8,8,128,64]{4,3,2,1,0:T(8,128)} copy(f32[4,8,8,128,64]{3,0,4,1,2:T(4,128)} %bitcast.117) | data formatting | bytes 16777216 | tf_op jit(solution)/shard_map/transpose | solution.py:133
  923.6 14.8 %reshape.127 = f32[32,8,8192]{2,1,0:T(8,128)} reshape(f32[4,8,8,128,64]{4,3,2,1,0:T(8,128)} %copy.76) | data formatting | bytes 16777216 | tf_op jit(solution)/shard_map/reshape | solution.py:134
  938.4 61.7 %all-to-all-done.4 = f32[32,8,8192]{2,1,0:T(8,128)} async-done(((f32[32,8,8192]{2,1,0:T(8,128)}), f32[32,8,8192]{2,1,0:T(8,128)}, u32[]{:S(2)}, u32[]{:S(2)}) %all-to-all-start.4) | async-done | bytes 8388640 | tf_op jit(solution)/shard_map/all_to_all | solution.py:138
  1007.3 14.2 %reshape.125 = f32[256,128,64]{2,1,0:T(8,128)} reshape(f32[32,8,8192]{2,1,0:T(8,128)} %all-to-all-done.4) | data formatting | bytes 16777216 | tf_op jit(solution)/shard_map/reshape | solution.py:147
  1021.5 14.1 %copy.72 = f32[256,128,64]{0,2,1:T(8,128)} copy(f32[256,128,64]{2,1,0:T(8,128)} %reshape.125) | data formatting | bytes 16777216 | tf_op jit(solution)/shard_map/reshape | solution.py:147
  1035.5 154.4 %all-to-all-done.5 = f32[32,8,8192]{2,1,0:T(8,128)} async-done(((f32[32,8,8192]{2,1,0:T(8,128)}), f32[32,8,8192]{2,1,0:T(8,128)}, u32[]{:S(2)}, u32[]{:S(2)}) %all-to-all-start.5) | async-done | bytes 8388640 | tf_op jit(solution)/shard_map/all_to_all | solution.py:141
  1189.9 14.2 %reshape.128 = f32[256,128,64]{2,1,0:T(8,128)} reshape(f32[32,8,8192]{2,1,0:T(8,128)} %all-to-all-done.5) | data formatting | bytes 16777216 | tf_op jit(solution)/shard_map/reshape | solution.py:147
  1204.1 14.1 %copy.77 = f32[256,128,64]{0,2,1:T(8,128)} copy(f32[256,128,64]{2,1,0:T(8,128)} %reshape.128) | data formatting | bytes 16777216 | tf_op jit(solution)/shard_map/reshape | solution.py:147
  1218.1 12.0 maximum_multiply_fusion
  (163 shorter events, 85.6 us)
Async XLA Ops:
  5.2 34.5 %all-to-all-start = ((s32[32,16,1]{1,2,0:T(1,128)}), s32[32,16,1]{1,2,0:T(1,128)S(1)}, u32[]{:S(2)}, u32[]{:S(2)}) async-start(s32[32,16,1]{1,2,0:T(1,128)} %bitcast.5), calls=%async_computation | async-start | bytes 32768 | tf_op jit(solution)/shard_map/all_to_all | solution.py:80
  39.7 30.8 %all-to-all-start.2 = ((f32[512,3,128]{2,1,0:T(4,128)}), f32[512,3,128]{2,1,0:T(4,128)S(1)}, u32[]{:S(2)}, u32[]{:S(2)}) async-start(f32[512,3,128]{2,1,0:T(4,128)} %scatter_fusion), calls=%async_computation.2 | async-start | bytes 2097152 | tf_op jit(solution)/shard_map/all_to_all | solution.py:78
  70.5 13.6 %all-to-all-start.1 = ((f32[32,16,128]{2,1,0:T(8,128)}), f32[32,16,128]{2,1,0:T(8,128)S(1)}, u32[]{:S(2)}, u32[]{:S(2)}) async-start(f32[32,16,128]{2,1,0:T(8,128)} %bitcast.6), calls=%async_computation.1 | async-start | bytes 524288 | tf_op jit(solution)/shard_map/all_to_all | solution.py:79
  85.8 13.9 %slice-start = ((s8[8388608]{0:T(1024)(128)(4,1)}), s8[4194304]{0:T(1024)(128)(4,1)S(1)}, s32[]{:S(2)}) async-start(s8[8388608]{0:T(1024)(128)(4,1)} %bitcast.111), calls=%async_computation.6 | async-start | bytes 8388608 | tf_op jit(solution)/shard_map/while
  86.4 13.3 %slice-start.1 = ((s8[8388608]{0:T(1024)(128)(4,1)}), s8[4194304]{0:T(1024)(128)(4,1)S(1)}, s32[]{:S(2)}) async-start(s8[8388608]{0:T(1024)(128)(4,1)} %bitcast.111), calls=%async_computation.7 | async-start | bytes 8388608 | tf_op jit(solution)/shard_map/while
  110.6 3.4 copy-start
  115.4 13.9 %slice-start = ((s8[8388608]{0:T(1024)(128)(4,1)}), s8[4194304]{0:T(1024)(128)(4,1)S(1)}, s32[]{:S(2)}) async-start(s8[8388608]{0:T(1024)(128)(4,1)} %bitcast.111), calls=%async_computation.6 | async-start | bytes 8388608 | tf_op jit(solution)/shard_map/while
  116.0 13.3 %slice-start.1 = ((s8[8388608]{0:T(1024)(128)(4,1)}), s8[4194304]{0:T(1024)(128)(4,1)S(1)}, s32[]{:S(2)}) async-start(s8[8388608]{0:T(1024)(128)(4,1)} %bitcast.111), calls=%async_computation.7 | async-start | bytes 8388608 | tf_op jit(solution)/shard_map/while
  140.2 3.4 copy-start
  145.0 13.9 %slice-start = ((s8[8388608]{0:T(1024)(128)(4,1)}), s8[4194304]{0:T(1024)(128)(4,1)S(1)}, s32[]{:S(2)}) async-start(s8[8388608]{0:T(1024)(128)(4,1)} %bitcast.111), calls=%async_computation.6 | async-start | bytes 8388608 | tf_op jit(solution)/shard_map/while
  145.7 13.3 %slice-start.1 = ((s8[8388608]{0:T(1024)(128)(4,1)}), s8[4194304]{0:T(1024)(128)(4,1)S(1)}, s32[]{:S(2)}) async-start(s8[8388608]{0:T(1024)(128)(4,1)} %bitcast.111), calls=%async_computation.7 | async-start | bytes 8388608 | tf_op jit(solution)/shard_map/while
  169.9 3.4 copy-start
  174.6 13.9 %slice-start = ((s8[8388608]{0:T(1024)(128)(4,1)}), s8[4194304]{0:T(1024)(128)(4,1)S(1)}, s32[]{:S(2)}) async-start(s8[8388608]{0:T(1024)(128)(4,1)} %bitcast.111), calls=%async_computation.6 | async-start | bytes 8388608 | tf_op jit(solution)/shard_map/while
  175.3 13.3 %slice-start.1 = ((s8[8388608]{0:T(1024)(128)(4,1)}), s8[4194304]{0:T(1024)(128)(4,1)S(1)}, s32[]{:S(2)}) async-start(s8[8388608]{0:T(1024)(128)(4,1)} %bitcast.111), calls=%async_computation.7 | async-start | bytes 8388608 | tf_op jit(solution)/shard_map/while
  199.5 3.4 copy-start
  204.2 13.9 %slice-start = ((s8[8388608]{0:T(1024)(128)(4,1)}), s8[4194304]{0:T(1024)(128)(4,1)S(1)}, s32[]{:S(2)}) async-start(s8[8388608]{0:T(1024)(128)(4,1)} %bitcast.111), calls=%async_computation.6 | async-start | bytes 8388608 | tf_op jit(solution)/shard_map/while
  204.9 13.3 %slice-start.1 = ((s8[8388608]{0:T(1024)(128)(4,1)}), s8[4194304]{0:T(1024)(128)(4,1)S(1)}, s32[]{:S(2)}) async-start(s8[8388608]{0:T(1024)(128)(4,1)} %bitcast.111), calls=%async_computation.7 | async-start | bytes 8388608 | tf_op jit(solution)/shard_map/while
  229.1 3.4 copy-start
  233.8 13.9 %slice-start = ((s8[8388608]{0:T(1024)(128)(4,1)}), s8[4194304]{0:T(1024)(128)(4,1)S(1)}, s32[]{:S(2)}) async-start(s8[8388608]{0:T(1024)(128)(4,1)} %bitcast.111), calls=%async_computation.6 | async-start | bytes 8388608 | tf_op jit(solution)/shard_map/while
  234.5 13.3 %slice-start.1 = ((s8[8388608]{0:T(1024)(128)(4,1)}), s8[4194304]{0:T(1024)(128)(4,1)S(1)}, s32[]{:S(2)}) async-start(s8[8388608]{0:T(1024)(128)(4,1)} %bitcast.111), calls=%async_computation.7 | async-start | bytes 8388608 | tf_op jit(solution)/shard_map/while
  258.7 3.4 copy-start
  263.4 13.9 %slice-start = ((s8[8388608]{0:T(1024)(128)(4,1)}), s8[4194304]{0:T(1024)(128)(4,1)S(1)}, s32[]{:S(2)}) async-start(s8[8388608]{0:T(1024)(128)(4,1)} %bitcast.111), calls=%async_computation.6 | async-start | bytes 8388608 | tf_op jit(solution)/shard_map/while
  264.1 13.3 %slice-start.1 = ((s8[8388608]{0:T(1024)(128)(4,1)}), s8[4194304]{0:T(1024)(128)(4,1)S(1)}, s32[]{:S(2)}) async-start(s8[8388608]{0:T(1024)(128)(4,1)} %bitcast.111), calls=%async_computation.7 | async-start | bytes 8388608 | tf_op jit(solution)/shard_map/while
  288.3 3.4 copy-start
  293.1 13.9 %slice-start = ((s8[8388608]{0:T(1024)(128)(4,1)}), s8[4194304]{0:T(1024)(128)(4,1)S(1)}, s32[]{:S(2)}) async-start(s8[8388608]{0:T(1024)(128)(4,1)} %bitcast.111), calls=%async_computation.6 | async-start | bytes 8388608 | tf_op jit(solution)/shard_map/while
  293.7 13.3 %slice-start.1 = ((s8[8388608]{0:T(1024)(128)(4,1)}), s8[4194304]{0:T(1024)(128)(4,1)S(1)}, s32[]{:S(2)}) async-start(s8[8388608]{0:T(1024)(128)(4,1)} %bitcast.111), calls=%async_computation.7 | async-start | bytes 8388608 | tf_op jit(solution)/shard_map/while
  317.9 3.4 copy-start
  645.9 10.3 copy-start.5
  656.2 24.2 %copy-start.3 = (f32[8,512,512]{1,2,0:T(8,128)S(1)}, f32[8,512,512]{1,2,0:T(8,128)}, u32[]{:S(2)}) copy-start(f32[8,512,512]{1,2,0:T(8,128)} %reshape.122) | copy-start | bytes 25165828
  680.5 17.5 %copy-start.2 = (f32[8,512,512]{2,1,0:T(8,128)}, f32[8,512,512]{2,1,0:T(8,128)S(1)}, u32[]{:S(2)}) copy-start(f32[8,512,512]{2,1,0:T(8,128)S(1)} %fusion.80) | copy-start | bytes 25165828
  680.5 17.5 %copy-start.4 = (s32[512]{0:T(512)S(1)}, s32[512]{0:T(512)}, u32[]{:S(2)}) copy-start(s32[512]{0:T(512)} %constant.78.clone) | copy-start | bytes 6148
  698.0 35.4 %copy-start.1 = (f32[8,512,512]{2,1,0:T(8,128)}, f32[8,512,512]{2,1,0:T(8,128)S(1)}, u32[]{:S(2)}) copy-start(f32[8,512,512]{2,1,0:T(8,128)S(1)} %fusion.84) | copy-start | bytes 25165828
  812.6 187.5 %all-to-all-start.4 = ((f32[32,8,8192]{2,1,0:T(8,128)}), f32[32,8,8192]{2,1,0:T(8,128)}, u32[]{:S(2)}, u32[]{:S(2)}) async-start(f32[32,8,8192]{2,1,0:T(8,128)} %reshape.124), calls=%async_computation.4 | async-start | bytes 16777216 | tf_op jit(solution)/shard_map/all_to_all | solution.py:138
  1000.0 189.9 %all-to-all-start.5 = ((f32[32,8,8192]{2,1,0:T(8,128)}), f32[32,8,8192]{2,1,0:T(8,128)}, u32[]{:S(2)}, u32[]{:S(2)}) async-start(f32[32,8,8192]{2,1,0:T(8,128)} %reshape.127), calls=%async_computation.5 | async-start | bytes 16777216 | tf_op jit(solution)/shard_map/all_to_all | solution.py:141
where the time goes:
time: 1240 us; the launch traced here: 1230 us
  matrix products  375 us (30%)
  local copies, waits for them, and re-layouts  351 us (28%)
  waiting for transfers between devices  246 us (20%)
  blocking collectives  188 us (15%)
  starting transfers between devices  29.2 us (2%)
  other arithmetic  22.8 us (2%)
  loops' own time  17.6 us (1%)
    all_to_all x1, blocking collectives, local(): lax.all_to_all(outgoing, ('px', 'py'), split_axis=0, concat_axis=0, tiled...  188 us
    all_to_all x1, waiting for transfers between devices, local(): lax.all_to_all(to_pencils(full_imag), ('px', 'py'), split_axis=0, concat_...  154 us
    dot_general x8, matrix products, row_blocks(): jnp.einsum('rpa,rpz->raz', planar, along_z, precision=lax.Precision.HIGHEST)  106 us
    dot_general x8, matrix products, deposit(): jnp.einsum('tg,gaz->taz', member, blocks, precision=highest)  87.3 us
    all_to_all x1, waiting for transfers between devices, local(): lax.all_to_all(to_pencils(full_real), ('px', 'py'), split_axis=0, concat_...  61.7 us
    reshape x4, local copies, waits for them, and re-layouts, to_field(): return values.reshape(NZ, width_x, width_y).transpose(1, 2, 0)  56.5 us
    another operation x1, local copies, waits for them, and re-layouts, local(): vort_field.reshape(width_x, width_y, devices, plane_len)  41.7 us
    dot_general x1, matrix products, local(): jnp.einsum('ly,zky->zkl', sin_y, half_real, precision=highest)  37.3 us
  transfers between devices with their start and end apart: 5, of which 4 were waited for; matrix products, arithmetic and copies ran while one was open for 15% of the time, Pallas kernels for 0%

commit v1 on v0

v1 whole, which is shorter than its diff:
```python
import functools
import math

import jax
import jax.numpy as jnp
from jax import lax
from jax.experimental import pallas as pl
from jax.experimental.pallas import tpu as pltpu
from jax.sharding import PartitionSpec as P

NX = 512
NY = 512
NZ = 256
BX = 16
BY = 8
BF = jnp.bfloat16
VMEM = 56 << 20


def spline(offset):
    a = jnp.abs(offset)
    b = jnp.maximum(2.0 - a, 0.0)
    inner = (1.5 * a - 2.5) * (a * a) + 1.0
    outer = (b * b) * (0.5 * b - 0.5)
    return jnp.where(a < 1.0, inner, outer)


def split(v):
    hi = v.astype(BF)
    return hi, (v - hi.astype(jnp.float32)).astype(BF)


def dot_nt(a, b):
    return lax.dot_general(a, b, (((1,), (1,)), ((), ())), preferred_element_type=jnp.float32)


def dot(a, b):
    return jnp.dot(a, b, preferred_element_type=jnp.float32)


def fill(x, y, z, w, part, planar_hi, planar_lo, depth_hi, depth_lo):
    width = x.shape[1]
    ix = lax.broadcasted_iota(jnp.int32, (BX, width), 0).astype(jnp.float32)
    iy = lax.broadcasted_iota(jnp.int32, (BY, width), 0).astype(jnp.float32)
    lanes = slice(part * width, (part + 1) * width)
    wx = spline(x - ix)
    wy = spline(y - iy) * w
    for i in range(0, BX, 2):
        hi, lo = split(jnp.concatenate([wx[i : i + 1] * wy, wx[i + 1 : i + 2] * wy], 0))
        planar_hi[i * BY : (i + 2) * BY, lanes] = hi
        planar_lo[i * BY : (i + 2) * BY, lanes] = lo
    q0 = jnp.floor((z - 1.0) * 0.0625)
    zr = z - 16.0 * q0
    first_hi, first_lo = split(spline(zr - ix))
    next_hi, next_lo = split(spline(zr - 16.0 - ix))
    block = jnp.broadcast_to(q0, (16, width)).astype(BF)
    zero = jnp.zeros((16, width), BF)
    before = None
    for q in range(NZ // 16):
        here = block == BF(q)
        hi, lo = zero, zero
        if before is not None:
            hi, lo = jnp.where(before, next_hi, hi), jnp.where(before, next_lo, lo)
        depth_hi[q * 16 : q * 16 + 16, lanes] = jnp.where(here, first_hi, hi)
        depth_lo[q * 16 : q * 16 + 16, lanes] = jnp.where(here, first_lo, lo)
        before = here


def deposit_kernel(start, order, data, coef, own, other, acc, *bufs, classes, ch, first):
    tile = (first + pl.program_id(0)) * pl.num_programs(1) + pl.program_id(1)
    width = data.shape[1] // 4
    acc[...] = jnp.zeros_like(acc)
    starts = [start[tile * classes + c] for c in range(classes + 1)]
    bounds = [jnp.int32(0)]
    for c in range(classes):
        bounds.append(bounds[-1] + (starts[c + 1] - starts[c] + ch - 1) // ch)
    total = bounds[classes]
    sets = (bufs[:4], bufs[4:])

    def place(i):
        c, base, s, e = jnp.int32(0), bounds[0], starts[0], starts[1]
        for k in range(1, classes):
            past = i >= bounds[k]
            c = jnp.where(past, k, c)
            base = jnp.where(past, bounds[k], base)
            s = jnp.where(past, starts[k], s)
            e = jnp.where(past, starts[k + 1], e)
        return c, s + (i - base) * ch, e

    def make(i, which):
        _, j0, e = place(i)
        for u in range(ch):
            entry = order[jnp.minimum(j0 + u, order.shape[0] - 1)]
            sign = jnp.where(j0 + u < e, (1 - 2 * (entry & 1)).astype(jnp.float32), 0.0)
            row = data[pl.ds(entry >> 1, 1), :]
            x, y, z, w = (row[:, k * width : (k + 1) * width] for k in range(4))
            fill(x, y, z, w * sign, u, *sets[which])

    def multiply(i, which):
        c, _, _ = place(i)
        planar_hi, planar_lo, depth_hi, depth_lo = (r[...] for r in sets[which])
        both = dot_nt(jnp.concatenate([planar_hi, planar_lo], 0), depth_hi)
        cells = planar_hi.shape[0]
        acc[c] += both[:cells] + both[cells:] + dot_nt(planar_hi, depth_lo)

    make(jnp.int32(0), 0)

    def step(k, _):
        multiply(2 * k, 0)
        make(2 * k + 1, 1)
        multiply(2 * k + 1, 1)
        make(2 * k + 2, 0)
        return 0

    lax.fori_loop(0, (total + 1) // 2, step, 0)
    for k, ref in ((0, own), (2, other)):
        for m in range(2):
            v = coef[(k + m) * classes] * acc[0]
            for c in range(1, classes):
                v = v + coef[(k + m) * classes + c] * acc[c]
            ref[m] = v.reshape(BX, BY, NZ)


def deposit(start, order, data, coef, first, tiles_x, tiles_y, classes, ch):
    rows, lanes = data.shape
    width = lanes // 4
    spec = lambda: pl.BlockSpec((2, BX, BY, NZ), lambda i, j, *_: (0, i, j, 0))
    shape = jax.ShapeDtypeStruct((2, tiles_x * BX, tiles_y * BY, NZ), jnp.float32)
    buffers = [
        pltpu.VMEM((BX * BY, ch * width), BF),
        pltpu.VMEM((BX * BY, ch * width), BF),
        pltpu.VMEM((NZ, ch * width), BF),
        pltpu.VMEM((NZ, ch * width), BF),
    ]
    flops = 6 * rows * BX * BY * NZ * width * tiles_x // 8
    return pl.pallas_call(
        functools.partial(deposit_kernel, classes=classes, ch=ch, first=first),
        grid_spec=pltpu.PrefetchScalarGridSpec(
            num_scalar_prefetch=2,
            grid=(tiles_x, tiles_y),
            in_specs=[
                pl.BlockSpec((rows, lanes), lambda i, j, *_: (0, 0), pipeline_mode=pl.Buffered(1)),
                pl.BlockSpec(memory_space=pltpu.SMEM),
            ],
            out_specs=[spec(), spec()],
            scratch_shapes=[pltpu.VMEM((classes, BX * BY, NZ), jnp.float32)] + buffers + buffers,
        ),
        out_shape=[shape, shape],
        compiler_params=pltpu.CompilerParams(vmem_limit_bytes=VMEM),
        cost_estimate=pl.CostEstimate(flops=flops, bytes_accessed=rows * lanes * 4, transcendentals=0),
    )(start, order, data, coef)


def y_kernel(m2, ml, own, other, out):
    wide = own.shape[2]

    def one(i, _):
        u = jnp.concatenate([own[0, i] + other[0, i], own[1, i] + other[1, i]], 0)
        hi, lo = split(u)
        r = dot(m2[...], jnp.concatenate([hi, lo], 0)) + dot(ml[...], hi)
        out[0, i] = r[:wide]
        out[1, i] = r[wide:]
        return 0

    lax.fori_loop(0, own.shape[1], one, 0, unroll=4)


def y_pass(matrix, own, other):
    hi, lo = matrix
    both = jnp.concatenate([hi, hi], 1)
    _, x, y, z = own.shape
    spec = lambda: pl.BlockSpec((2, BX, y, z), lambda i: (0, i, 0, 0))
    whole = lambda m: pl.BlockSpec(m.shape, lambda i: (0, 0))
    return pl.pallas_call(
        y_kernel,
        grid=(x // BX,),
        in_specs=[whole(both), whole(lo), spec(), spec()],
        out_specs=spec(),
        out_shape=jax.ShapeDtypeStruct(own.shape, jnp.float32),
        compiler_params=pltpu.CompilerParams(vmem_limit_bytes=VMEM),
    )(both, lo, own, other)


def x_kernel(mh, ml, *refs):
    ins, out = refs[:-1], refs[-1]
    wide = out.shape[1]
    for k in range(out.shape[2]):
        hi, lo = split(jnp.concatenate([r[c, :, k, :] for c in range(2) for r in ins], 0))
        r = dot(mh[...], hi) + dot(ml[...], hi) + dot(mh[...], lo)
        out[0, :, k, :] = r[:wide]
        out[1, :, k, :] = r[wide:]


def x_pass(matrix, chunks):
    hi, lo = matrix
    _, _, y, z = chunks[0].shape
    x = sum(c.shape[1] for c in chunks)
    spec = lambda n: pl.BlockSpec((2, n, 8, z), lambda i: (0, 0, i, 0))
    whole = pl.BlockSpec(hi.shape, lambda i: (0, 0))
    return pl.pallas_call(
        x_kernel,
        grid=(y // 8,),
        in_specs=[whole, whole] + [spec(c.shape[1]) for c in chunks],
        out_specs=spec(x),
        out_shape=jax.ShapeDtypeStruct((2, x, y, z), jnp.float32),
        compiler_params=pltpu.CompilerParams(vmem_limit_bytes=VMEM),
    )(hi, lo, *chunks)


def dft_matrix(first, step, cells, total, scale):
    i = jnp.arange(cells, dtype=jnp.int32)
    angle = (2.0 * math.pi / total) * ((first + step * i)[:, None] * i[None, :] % total).astype(jnp.float32)
    c, s = jnp.cos(angle) * scale, jnp.sin(angle) * scale
    m = jnp.concatenate([jnp.concatenate([c, s], 1), jnp.concatenate([-s, c], 1)], 0)
    hi = lax.reduce_precision(m, 8, 7)
    return hi.astype(BF), (m - hi).astype(BF)


def reverse_digits(value, levels):
    result = 0
    for position in range(levels):
        result = result * 2 + ((value >> position) & 1)
    return result


def local(positions, strength, destination, tile_index, particle_count):
    rows, _, width = positions.shape
    n_px, n_py = lax.axis_size("px"), lax.axis_size("py")
    me_x, me_y = lax.axis_index("px"), lax.axis_index("py")
    width_x, width_y = NX // n_px, NY // n_py
    tiles_x, tiles_y = width_x // BX, width_y // BY
    tiles = tiles_x * tiles_y
    assert n_py >= 2 * n_px
    classes = n_py // 2
    res_x = reverse_digits(me_x, n_px.bit_length() - 1)
    res_y = reverse_digits(me_y, n_py.bit_length() - 1)
    side = me_y & 1
    low_y = res_y % classes

    alive = jnp.arange(width, dtype=jnp.int32)[None, :] < particle_count[:, None]
    live = jnp.where(alive, strength, jnp.zeros_like(strength))
    packed = jnp.concatenate([positions.reshape(rows, 3 * width), live], 1)
    info = destination[:, 0] * tiles + tile_index
    groups = [list(range(0, n_py, 2)), list(range(1, n_py, 2))]

    def gather(v):
        v = lax.all_gather(v, "px", tiled=True)
        return lax.all_gather(v, "py", axis_index_groups=groups, tiled=True)

    info = gather(info)
    data = gather(packed)
    total = info.shape[0]

    pencil, tile = info // tiles, info % tiles
    at_x, at_y = pencil // n_py, pencil % n_py
    k = (res_x * at_x * (n_py // n_px) + low_y * at_y) % n_py
    half = k % classes
    group = tile * classes + (half - (half & 1)) + (at_y & 1)
    number = jnp.arange(total, dtype=jnp.int32)
    code = group * (2 * total) + number * 2 + (k >= classes).astype(jnp.int32)
    code = lax.sort(code)
    edges = jnp.arange(tiles * classes + 1, dtype=jnp.int32) * (2 * total)
    start = jnp.sum((code[None, :] < edges[:, None]).astype(jnp.int32), axis=1)
    order = code % (2 * total)

    c = jnp.arange(classes, dtype=jnp.int32)
    odd = c & 1
    exponent = jnp.where(low_y % 2 == 1, c, c - odd).astype(jnp.float32) * (2.0 * math.pi / n_py)
    flip = lambda s: (1 - 2 * (odd * s)).astype(jnp.float32)
    real, imag = jnp.cos(exponent), -jnp.sin(exponent)
    coef = jnp.concatenate([real * flip(side), imag * flip(side), real * flip(1 - side), imag * flip(1 - side)])

    matrix_y = dft_matrix(res_y, n_py, width_y, NY, 1.0 / math.sqrt(NX * NY))
    matrix_x = dft_matrix(res_x, n_px, width_x, NX, 1.0)
    swap = [(i, i ^ 1) for i in range(n_py)]
    parts = 4
    each = tiles_x // parts
    halves = []
    for i in range(parts):
        own, other = deposit(start, order, data, coef, i * each, each, tiles_y, classes, 4)
        halves.append((own, lax.ppermute(other, "py", swap)))
    return x_pass(matrix_x, [y_pass(matrix_y, own, got) for own, got in halves])


def solution(mesh):
    placed = (
        P(("px", "py"), None, None),
        P(("px", "py"), None),
        P(("px", "py"), None),
        P(("px", "py")),
        P(("px", "py")),
    )
    return jax.shard_map(
        local, mesh=mesh, in_specs=placed, out_specs=P(None, "px", "py", None), check_vma=False
    )
```

time: 1240 us -> 691 us (0.56)
  Pallas kernels: 0 us -> 525 us
  matrix products: 375 us -> 0 us
  local copies, waits for them, and re-layouts: 351 us -> 3.31 us
  blocking collectives: 188 us -> 11.6 us
  waiting for transfers between devices: 246 us -> 115 us
  starting transfers between devices: 29.2 us -> 7.28 us
  loops' own time: 17.6 us -> 0 us
  between operations: 0.39 us -> 13.5 us
    pallas_call x0 -> x9, Pallas kernels: none -> 525 us  [the longest x4 481 us: deposit(): pl.pallas_call(functools.partial(deposit_kernel, classes=classes, ch=ch,...]
    dot_general x22 -> x0, matrix products: 375 us -> none  [the longest x8 106 us: row_blocks(): jnp.einsum('rpa,rpz->raz', planar, along_z, precision=lax.Precision.HIGHEST)]
    all_to_all x5 -> x0, waiting for transfers between devices: 246 us -> none  [the longest x1 154 us: local(): lax.all_to_all(to_pencils(full_imag), ('px', 'py'), split_axis=0, concat_...]
    all_to_all x1 -> x0, blocking collectives: 188 us -> none  [local(): lax.all_to_all(outgoing, ('px', 'py'), split_axis=0, concat_axis=0, tiled...]
    reshape x12 -> x1, local copies, waits for them, and re-layouts: 173 us -> 0.16 us  [local(): packed = jnp.concatenate([positions.reshape(rows, 3 * width), live], 1)]
    all_gather x0 -> x2, waiting for transfers between devices: none -> 115 us  [the longest x1 69.5 us: gather(): return lax.all_gather(v, 'py', axis_index_groups=groups, tiled=True)]
    transpose x4 -> x0, local copies, waits for them, and re-layouts: 54.4 us -> none  [the longest x2 27.5 us: to_pencils(): return values.reshape(plane_len, rows_x, width_x, cols_y, width_y).transp...]
    another operation x2 -> x1, local copies, waits for them, and re-layouts: 41.7 us -> 0.01 us  [the longest x1 41.7 us: local(): vort_field.reshape(width_x, width_y, devices, plane_len)]
  transfers between devices with their start and end apart: 5 -> 6, of which waited for: 4 -> 2; matrix products, arithmetic and copies ran while one was open for 15% -> 2% of each run, Pallas kernels for 0% -> 55%
where the time goes in v1:
time: 691 us; the launch traced here: 688 us
  Pallas kernels  525 us (76%)
  waiting for transfers between devices  115 us (17%)
  between operations  13.5 us (2%)
  other arithmetic  12.9 us (2%)
  blocking collectives  11.6 us (2%)
  starting transfers between devices  7.28 us (1%)
    pallas_call x4, Pallas kernels, deposit(): pl.pallas_call(functools.partial(deposit_kernel, classes=classes, ch=ch,...  481 us
    all_gather x1, waiting for transfers between devices, gather(): return lax.all_gather(v, 'py', axis_index_groups=groups, tiled=True)  69.5 us
    all_gather x1, waiting for transfers between devices, gather(): v = lax.all_gather(v, 'px', tiled=True)  45.8 us
    pallas_call x4, Pallas kernels, y_pass(): pl.pallas_call(y_kernel, grid=(x // BX,), in_specs=[whole(both), whole(lo...  24.5 us
    pallas_call x1, Pallas kernels, x_pass(): pl.pallas_call(x_kernel, grid=(y // 8,), in_specs=[whole, whole] + [spec(...  19.5 us
  transfers between devices with their start and end apart: 6, of which 2 were waited for; matrix products, arithmetic and copies ran while one was open for 2% of the time, Pallas kernels for 55%

profile of v1, /device:TPU:17, one launch (start us, length us, event | category | flops | bytes accessed | tf_op | source)
XLA Modules:
  0.0 688.5 jit_solution(1227535487675187639)
XLA Ops:
  6.5 0.0 copy-start.2
  6.5 0.0 copy-start.1
  6.5 0.0 all-gather.4.cloned.1.call-start
  6.5 1.2 copy.11
  7.7 0.2 copy.12
  7.9 1.0 fusion.1
  8.9 0.8 pad_maximum_fusion
  9.8 0.0 all-gather.4.cloned.1.call-update
  9.8 0.0 all-gather.6.cloned.1.call-start
  9.8 45.8 %all-gather.4.cloned.1.call-done = f32[1024,512]{1,0:T(8,128)} async-done(((f32[256,512]{1,0:T(8,128)}), f32[1024,512]{1,0:T(8,128)}) %all-gather.4.cloned.1.call-update) | async-done | bytes 2097168 | tf_op jit(solution)/shard_map/all_gather | solution.py:247
  55.6 0.0 all-gather.6.cloned.1.call-update
  55.7 0.0 copy-done.2
  55.7 0.0 copy-done.1
  55.7 5.5 all-gather
  61.2 6.1 all_gather.13
  67.3 0.1 fusion.23
  67.4 5.8 sort.14
  73.2 0.1 fusion.47
  73.2 0.7 pad_maximum_fusion.2.coef
  73.9 1.2 convert_reduce_fusion.start
  75.1 0.6 add_select_fusion.2.order
  75.7 69.5 %all-gather.6.cloned.1.call-done.data = f32[4096,512]{1,0:T(8,128)} async-done(((f32[1024,512]{1,0:T(8,128)}), f32[4096,512]{1,0:T(8,128)}) %all-gather.6.cloned.1.call-update) | async-done | bytes 8388624 | tf_op jit(solution)/shard_map/all_gather | solution.py:248
  145.2 119.2 %shard_map.57 = (f32[2,32,64,256]{3,2,1,0:T(8,128)}, f32[2,32,64,256]{3,2,1,0:T(8,128)}) custom-call(s32[257]{0:T(512)} %convert_reduce_fusion.start, s32[4096]{0:T(1024)} %add_select_fusion.2.order, f32[4096,512]{1,0:T(8,128)} %all-gather.6.cloned.1.call-done.data, f32[16]{0:T(128)} %pad_maximum_fusion.2.coef), custom_call_target="tpu_custom_call" | custom-call | flops 25769803776 | bytes 8388608 | tf_op jit(solution)/shard_map/pallas_call | solution.py:136
  264.4 3.7 collective-permute-start.1
  268.1 120.7 %shard_map.59 = (f32[2,32,64,256]{3,2,1,0:T(8,128)}, f32[2,32,64,256]{3,2,1,0:T(8,128)}) custom-call(s32[257]{0:T(512)} %convert_reduce_fusion.start, s32[4096]{0:T(1024)} %add_select_fusion.2.order, f32[4096,512]{1,0:T(8,128)} %all-gather.6.cloned.1.call-done.data, f32[16]{0:T(128)} %pad_maximum_fusion.2.coef), custom_call_target="tpu_custom_call" | custom-call | flops 25769803776 | bytes 8388608 | tf_op jit(solution)/shard_map/pallas_call | solution.py:136
  388.8 3.0 collective-permute-start.2
  391.8 120.8 %shard_map.61 = (f32[2,32,64,256]{3,2,1,0:T(8,128)}, f32[2,32,64,256]{3,2,1,0:T(8,128)}) custom-call(s32[257]{0:T(512)} %convert_reduce_fusion.start, s32[4096]{0:T(1024)} %add_select_fusion.2.order, f32[4096,512]{1,0:T(8,128)} %all-gather.6.cloned.1.call-done.data, f32[16]{0:T(128)} %pad_maximum_fusion.2.coef), custom_call_target="tpu_custom_call" | custom-call | flops 25769803776 | bytes 8388608 | tf_op jit(solution)/shard_map/pallas_call | solution.py:136
  512.6 0.0 collective-permute-start.3
  512.6 119.9 %shard_map.55 = (f32[2,32,64,256]{3,2,1,0:T(8,128)}, f32[2,32,64,256]{3,2,1,0:T(8,128)}) custom-call(s32[257]{0:T(512)} %convert_reduce_fusion.start, s32[4096]{0:T(1024)} %add_select_fusion.2.order, f32[4096,512]{1,0:T(8,128)} %all-gather.6.cloned.1.call-done.data, f32[16]{0:T(128)} %pad_maximum_fusion.2.coef), custom_call_target="tpu_custom_call" | custom-call | flops 25769803776 | bytes 8388608 | tf_op jit(solution)/shard_map/pallas_call | solution.py:136
  632.5 0.5 collective-permute-start
  633.0 0.2 sine_multiply_fusion
  633.2 0.7 fusion.2
  633.9 0.6 pad_maximum_fusion.1.m2
  634.6 0.3 fusion.14
  634.9 0.7 fusion
  635.7 0.0 collective-permute-done.1.other
  635.7 6.2 shard_map.58.refs_1_
  641.9 0.0 collective-permute-done.2.other
  641.9 6.1 shard_map.60.refs_2_
  648.0 0.0 collective-permute-done.3.other
  648.0 0.0 copy-start
  648.0 2.0 copy-done
  649.9 6.1 shard_map.62.refs_3_
  656.0 0.0 collective-permute-done.other
  656.0 6.1 shard_map.56.refs_0_
  662.2 19.5 %shard_map.63 = f32[2,128,64,256]{3,2,1,0:T(8,128)} custom-call(bf16[256,256]{1,0:T(8,128)(2,1)} %get-tuple-element.25.mh, bf16[256,256]{1,0:T(8,128)(2,1)} %get-tuple-element.24.ml, f32[2,32,64,256]{3,2,1,0:T(8,128)} %shard_map.56.refs_0_, f32[2,32,64,256]{3,2,1,0:T(8,128)} %shard_map.58.refs_1_, f32[2,32,64,256]{3,2,1,0:T(8,128)} %shard_map.60.refs_2_, ...), custom_call_target="tpu_custom_call" | custom-call | tf_op jit(solution)/shard_map/pallas_call | solution.py:200
  (7 shorter events, 0.1 us)
Async XLA Ops:
  6.5 49.1 %copy-start.2 = (s32[256,1]{0,1:T(1,128)S(1)}, s32[256,1]{0,1:T(1,128)}, u32[]{:S(2)}) copy-start(s32[256,1]{0,1:T(1,128)} %param.7) | copy-start | bytes 3076
  6.5 49.1 %copy-start.1 = (s32[256]{0:T(256)S(1)}, s32[256]{0:T(256)}, u32[]{:S(2)}) copy-start(s32[256]{0:T(256)} %param.8) | copy-start | bytes 3076
  6.5 49.1 %all-gather.4.cloned.1.call-start = ((), (), s32[]{:S(2)}) async-start(), calls=%async_computation | async-start | bytes 2621440 | tf_op jit(solution)/shard_map/all_gather | solution.py:247
  9.8 135.4 %all-gather.6.cloned.1.call-start = ((), (), s32[]{:S(2)}) async-start(), calls=%async_computation.1 | async-start | bytes 10485760 | tf_op jit(solution)/shard_map/all_gather | solution.py:248
  264.4 371.3 %collective-permute-start.1 = (f32[2,32,64,256]{3,2,1,0:T(8,128)}, f32[2,32,64,256]{3,2,1,0:T(8,128)}, u32[]{:S(2)}, u32[]{:S(2)}) collective-permute-start(f32[2,32,64,256]{3,2,1,0:T(8,128)} %get-tuple-element.19), channel_id=1, source_target_pairs={{0,1},{1,0},{2,3},{3,2},{4,5},{5,4},{6,7},{7,6},{8,9},{9,8},{10,11... | collective-permute-start | bytes 12582920 | tf_op jit(solution)/shard_map/ppermute | solution.py:281
  388.8 253.1 %collective-permute-start.2 = (f32[2,32,64,256]{3,2,1,0:T(8,128)}, f32[2,32,64,256]{3,2,1,0:T(8,128)}, u32[]{:S(2)}, u32[]{:S(2)}) collective-permute-start(f32[2,32,64,256]{3,2,1,0:T(8,128)} %get-tuple-element.21), channel_id=1, source_target_pairs={{0,1},{1,0},{2,3},{3,2},{4,5},{5,4},{6,7},{7,6},{8,9},{9,8},{10,11... | collective-permute-start | bytes 12582920 | tf_op jit(solution)/shard_map/ppermute | solution.py:281
  512.6 135.4 %collective-permute-start.3 = (f32[2,32,64,256]{3,2,1,0:T(8,128)}, f32[2,32,64,256]{3,2,1,0:T(8,128)S(1)}, u32[]{:S(2)}, u32[]{:S(2)}) collective-permute-start(f32[2,32,64,256]{3,2,1,0:T(8,128)} %get-tuple-element.23), channel_id=1, source_target_pairs={{0,1},{1,0},{2,3},{3,2},{4,5},{5,4},{6,7},{7,6},{8,9},{9,8},{10,11... | collective-permute-start | bytes 12582920 | tf_op jit(solution)/shard_map/ppermute | solution.py:281
  632.5 23.6 %collective-permute-start = (f32[2,32,64,256]{3,2,1,0:T(8,128)}, f32[2,32,64,256]{3,2,1,0:T(8,128)}, u32[]{:S(2)}, u32[]{:S(2)}) collective-permute-start(f32[2,32,64,256]{3,2,1,0:T(8,128)} %get-tuple-element.17), channel_id=1, source_target_pairs={{0,1},{1,0},{2,3},{3,2},{4,5},{5,4},{6,7},{7,6},{8,9},{9,8},{10,11... | collective-permute-start | bytes 12582920 | tf_op jit(solution)/shard_map/ppermute | solution.py:281
  648.0 2.0 copy-start
Sparse Core Ops, SparseCore 0:
  9.9 45.6 all-gather.3
  57.4 87.7 all-gather.5

commit v2 on v1

--- a/solution.py
+++ b/solution.py
@@ -15,6 +15,10 @@
 BY = 8
 BF = jnp.bfloat16
 VMEM = 56 << 20
+STEP_ROWS = 4
+PAIR = 2
+DEPTH = 6
+LANES = 128
 
 
 def spline(offset):
@@ -28,10 +32,6 @@
 def split(v):
     hi = v.astype(BF)
     return hi, (v - hi.astype(jnp.float32)).astype(BF)
-
-
-def dot_nt(a, b):
-    return lax.dot_general(a, b, (((1,), (1,)), ((), ())), preferred_element_type=jnp.float32)
 
 
 def dot(a, b):
@@ -50,45 +50,32 @@
         planar_hi[i * BY : (i + 2) * BY, lanes] = hi
         planar_lo[i * BY : (i + 2) * BY, lanes] = lo
     q0 = jnp.floor((z - 1.0) * 0.0625)
-    zr = z - 16.0 * q0
-    first_hi, first_lo = split(spline(zr - ix))
-    next_hi, next_lo = split(spline(zr - 16.0 - ix))
-    block = jnp.broadcast_to(q0, (16, width)).astype(BF)
-    zero = jnp.zeros((16, width), BF)
-    before = None
-    for q in range(NZ // 16):
-        here = block == BF(q)
-        hi, lo = zero, zero
-        if before is not None:
-            hi, lo = jnp.where(before, next_hi, hi), jnp.where(before, next_lo, lo)
-        depth_hi[q * 16 : q * 16 + 16, lanes] = jnp.where(here, first_hi, hi)
-        depth_lo[q * 16 : q * 16 + 16, lanes] = jnp.where(here, first_lo, lo)
-        before = here
-
-
-def deposit_kernel(start, order, data, coef, own, other, acc, *bufs, classes, ch, first):
-    tile = (first + pl.program_id(0)) * pl.num_programs(1) + pl.program_id(1)
+    away = (z - 16.0 * q0) - ix
+    far = away > 8.0
+    hi, lo = split(spline(jnp.where(far, away - 16.0, away)))
+    block = jnp.where(far, q0 + 1.0, q0).astype(BF)
+    spread = lambda v: jnp.concatenate([v] * (LANES // 16), 0).T
+    hi, lo, block = spread(hi), spread(lo), spread(block)
+    zero = jnp.zeros((width, LANES), BF)
+    column_block = (lax.broadcasted_iota(jnp.int32, (width, LANES), 1) // 16).astype(jnp.float32)
+    for t in range(NZ // LANES):
+        here = block == (column_block + float(t * (LANES // 16))).astype(BF)
+        depth_hi[lanes, t * LANES : (t + 1) * LANES] = jnp.where(here, hi, zero)
+        depth_lo[lanes, t * LANES : (t + 1) * LANES] = jnp.where(here, lo, zero)
+
+
+def deposit_kernel(
+    groups_of, firsts, ends, order, span, coef, *refs, classes, ch, depth, first, blocks
+):
+    parts, (own, other, acc, data, arrived), bufs = refs[:blocks], refs[blocks : blocks + 5], refs[blocks + 5 :]
+    tile = pl.program_id(0) * pl.num_programs(1) + pl.program_id(1)
     width = data.shape[1] // 4
-    acc[...] = jnp.zeros_like(acc)
-    starts = [start[tile * classes + c] for c in range(classes + 1)]
-    bounds = [jnp.int32(0)]
-    for c in range(classes):
-        bounds.append(bounds[-1] + (starts[c + 1] - starts[c] + ch - 1) // ch)
-    total = bounds[classes]
-    sets = (bufs[:4], bufs[4:])
-
-    def place(i):
-        c, base, s, e = jnp.int32(0), bounds[0], starts[0], starts[1]
-        for k in range(1, classes):
-            past = i >= bounds[k]
-            c = jnp.where(past, k, c)
-            base = jnp.where(past, bounds[k], base)
-            s = jnp.where(past, starts[k], s)
-            e = jnp.where(past, starts[k + 1], e)
-        return c, s + (i - base) * ch, e
-
-    def make(i, which):
-        _, j0, e = place(i)
+    base = first * pl.num_programs(1) * classes
+    sets = [bufs[4 * k : 4 * k + 4] for k in range(depth)]
+
+    def make(t, which):
+        t = jnp.minimum(t, groups_of.shape[0] - 1)
+        j0, e = firsts[t], ends[t]
         for u in range(ch):
             entry = order[jnp.minimum(j0 + u, order.shape[0] - 1)]
             sign = jnp.where(j0 + u < e, (1 - 2 * (entry & 1)).astype(jnp.float32), 0.0)
@@ -96,59 +83,102 @@
             x, y, z, w = (row[:, k * width : (k + 1) * width] for k in range(4))
             fill(x, y, z, w * sign, u, *sets[which])
 
-    def multiply(i, which):
-        c, _, _ = place(i)
+    def multiply(t, which, stop):
+        g = jnp.where(t < stop, groups_of[jnp.minimum(t, groups_of.shape[0] - 1)] - base, acc.shape[0] - 1)
         planar_hi, planar_lo, depth_hi, depth_lo = (r[...] for r in sets[which])
-        both = dot_nt(jnp.concatenate([planar_hi, planar_lo], 0), depth_hi)
         cells = planar_hi.shape[0]
-        acc[c] += both[:cells] + both[cells:] + dot_nt(planar_hi, depth_lo)
-
-    make(jnp.int32(0), 0)
-
-    def step(k, _):
-        multiply(2 * k, 0)
-        make(2 * k + 1, 1)
-        multiply(2 * k + 1, 1)
-        make(2 * k + 2, 0)
-        return 0
-
-    lax.fori_loop(0, (total + 1) // 2, step, 0)
+        v = acc[g]
+        for u in range(0, ch, PAIR):
+            lanes = slice(u * width, (u + PAIR) * width)
+            both = dot(jnp.concatenate([planar_hi[:, lanes], planar_lo[:, lanes]], 0), depth_hi[lanes])
+            v = v + (both[:cells] + both[cells:] + dot(planar_hi[:, lanes], depth_lo[lanes]))
+        acc[g] = v
+
+    @pl.when(tile == 0)
+    def _():
+        copies, at = [], 0
+        for k, part in enumerate(parts):
+            rows = part.shape[0]
+            copies.append(pltpu.make_async_copy(part, data.at[at : at + rows], arrived.at[k]))
+            at += rows
+        for copy in copies:
+            copy.start()
+
+        def clear(i, _):
+            acc[i] = jnp.zeros(acc.shape[1:], jnp.float32)
+            return 0
+
+        lax.fori_loop(0, acc.shape[0], clear, 0)
+        for copy in copies:
+            copy.wait()
+        begin, stop = span[first], span[first + pl.num_programs(0)]
+        for k in range(depth):
+            make(begin + k, k)
+
+        def step(i, _):
+            for k in range(depth):
+                t = begin + i * depth + k
+                multiply(t, k, stop)
+                make(t + depth, k)
+            return 0
+
+        lax.fori_loop(0, (stop - begin + depth - 1) // depth, step, 0)
+
     for k, ref in ((0, own), (2, other)):
         for m in range(2):
-            v = coef[(k + m) * classes] * acc[0]
+            v = coef[(k + m) * classes] * acc[tile * classes]
             for c in range(1, classes):
-                v = v + coef[(k + m) * classes + c] * acc[c]
+                v = v + coef[(k + m) * classes + c] * acc[tile * classes + c]
             ref[m] = v.reshape(BX, BY, NZ)
 
 
-def deposit(start, order, data, coef, first, tiles_x, tiles_y, classes, ch):
-    rows, lanes = data.shape
+def deposit(plan, blocks, coef, first, tiles_x, tiles_y, classes, ch, depth):
+    rows, lanes = sum(b.shape[0] for b in blocks), blocks[0].shape[1]
     width = lanes // 4
     spec = lambda: pl.BlockSpec((2, BX, BY, NZ), lambda i, j, *_: (0, i, j, 0))
     shape = jax.ShapeDtypeStruct((2, tiles_x * BX, tiles_y * BY, NZ), jnp.float32)
     buffers = [
         pltpu.VMEM((BX * BY, ch * width), BF),
         pltpu.VMEM((BX * BY, ch * width), BF),
-        pltpu.VMEM((NZ, ch * width), BF),
-        pltpu.VMEM((NZ, ch * width), BF),
+        pltpu.VMEM((ch * width, NZ), BF),
+        pltpu.VMEM((ch * width, NZ), BF),
     ]
     flops = 6 * rows * BX * BY * NZ * width * tiles_x // 8
     return pl.pallas_call(
-        functools.partial(deposit_kernel, classes=classes, ch=ch, first=first),
+        functools.partial(deposit_kernel, classes=classes, ch=ch, depth=depth, first=first, blocks=len(blocks)),
         grid_spec=pltpu.PrefetchScalarGridSpec(
-            num_scalar_prefetch=2,
+            num_scalar_prefetch=5,
             grid=(tiles_x, tiles_y),
-            in_specs=[
-                pl.BlockSpec((rows, lanes), lambda i, j, *_: (0, 0), pipeline_mode=pl.Buffered(1)),
-                pl.BlockSpec(memory_space=pltpu.SMEM),
-            ],
+            in_specs=[pl.BlockSpec(memory_space=pltpu.SMEM)] + [pl.BlockSpec(memory_space=pl.ANY)] * len(blocks),
             out_specs=[spec(), spec()],
-            scratch_shapes=[pltpu.VMEM((classes, BX * BY, NZ), jnp.float32)] + buffers + buffers,
+            scratch_shapes=[
+                pltpu.VMEM((tiles_x * tiles_y * classes + 1, BX * BY, NZ), jnp.float32),
+                pltpu.VMEM((rows, lanes), jnp.float32),
+                pltpu.SemaphoreType.DMA((len(blocks),)),
+            ]
+            + buffers * depth,
         ),
         out_shape=[shape, shape],
         compiler_params=pltpu.CompilerParams(vmem_limit_bytes=VMEM),
         cost_estimate=pl.CostEstimate(flops=flops, bytes_accessed=rows * lanes * 4, transcendentals=0),
-    )(start, order, data, coef)
+    )(*plan, coef, *blocks)
+
+
+def make_plan(code, radix, group_count, span_groups, ch):
+    total = code.shape[0]
+    edges = jnp.arange(group_count + 1, dtype=jnp.int32) * radix
+    start = jnp.sum((code[None, :] < edges[:, None]).astype(jnp.int32), axis=1)
+    steps = (start[1:] - start[:-1] + ch - 1) // ch
+    before = jnp.sum(jnp.where(jnp.tri(group_count, k=-1, dtype=jnp.bool_), steps[None, :], 0), axis=1)
+    after = before + steps
+    t = jnp.arange(total // ch + group_count, dtype=jnp.int32)[:, None]
+    mine = (before[None, :] <= t) & (t < after[None, :])
+    pick = lambda v: jnp.sum(jnp.where(mine, v, 0), axis=1)
+    group = pick(jnp.arange(group_count, dtype=jnp.int32)[None, :])
+    first = pick(start[None, :-1] + (t - before[None, :]) * ch)
+    end = pick(jnp.broadcast_to(start[None, 1:], mine.shape))
+    span = jnp.concatenate([before[::span_groups], after[-1:]])
+    return group, first, end, code % radix, span
 
 
 def y_kernel(m2, ml, own, other, out):
@@ -223,6 +253,23 @@
     return result
 
 
+def gather_rows(v, tail, n_px, n_py, side):
+    rows = v.shape[0] - tail
+    if n_py != 8:
+        groups = [list(range(0, n_py, 2)), list(range(1, n_py, 2))]
+        got = lax.all_gather(lax.all_gather(v, "px", tiled=True), "py", axis_index_groups=groups, tiled=True)
+        return [got], got.reshape(-1, rows + tail, v.shape[1])[:, rows:]
+    flip = lambda u, axis, n, m: lax.ppermute(u, axis, [(i, i ^ m) for i in range(n)])
+    half = rows // 2
+    blocks, tails = [], []
+    for u in [v] + [flip(v, "px", n_px, m) for m in range(1, n_px)]:
+        one, two = flip(u, "py", n_py, 2), flip(u, "py", n_py, 4)
+        rest = flip(two[half:], "py", n_py, 2)
+        blocks += [u, one, two, flip(one[:half], "py", n_py, 4), rest]
+        tails += [u[rows:], one[rows:], two[rows:], rest[rows - half :]]
+    return blocks, jnp.stack(tails)
+
+
 def local(positions, strength, destination, tile_index, particle_count):
     rows, _, width = positions.shape
     n_px, n_py = lax.axis_size("px"), lax.axis_size("py")
@@ -240,28 +287,21 @@
     alive = jnp.arange(width, dtype=jnp.int32)[None, :] < particle_count[:, None]
     live = jnp.where(alive, strength, jnp.zeros_like(strength))
     packed = jnp.concatenate([positions.reshape(rows, 3 * width), live], 1)
-    info = destination[:, 0] * tiles + tile_index
-    groups = [list(range(0, n_py, 2)), list(range(1, n_py, 2))]
-
-    def gather(v):
-        v = lax.all_gather(v, "px", tiled=True)
-        return lax.all_gather(v, "py", axis_index_groups=groups, tiled=True)
-
-    info = gather(info)
-    data = gather(packed)
-    total = info.shape[0]
+    info = (destination[:, 0] * tiles + tile_index).astype(jnp.float32)
+    tail = -(-rows // (4 * width) // 8) * 8
+    info = jnp.pad(info, (0, tail * 4 * width - rows)).reshape(tail, 4 * width)
+    blocks, tails = gather_rows(jnp.concatenate([packed, info], 0), tail, n_px, n_py, me_y & 1)
+    info = tails.reshape(tails.shape[0], -1)[:, :rows].astype(jnp.int32)
+    number = jnp.arange(info.shape[0], dtype=jnp.int32)[:, None] * (rows + tail) + jnp.arange(rows, dtype=jnp.int32)
+    radix = 2 * info.shape[0] * (rows + tail)
 
     pencil, tile = info // tiles, info % tiles
     at_x, at_y = pencil // n_py, pencil % n_py
     k = (res_x * at_x * (n_py // n_px) + low_y * at_y) % n_py
     half = k % classes
     group = tile * classes + (half - (half & 1)) + (at_y & 1)
-    number = jnp.arange(total, dtype=jnp.int32)
-    code = group * (2 * total) + number * 2 + (k >= classes).astype(jnp.int32)
-    code = lax.sort(code)
-    edges = jnp.arange(tiles * classes + 1, dtype=jnp.int32) * (2 * total)
-    start = jnp.sum((code[None, :] < edges[:, None]).astype(jnp.int32), axis=1)
-    order = code % (2 * total)
+    code = group * radix + number * 2 + (k >= classes).astype(jnp.int32)
+    plan = make_plan(lax.sort(code.reshape(-1)), radix, tiles * classes, tiles_y * classes, STEP_ROWS)
 
     c = jnp.arange(classes, dtype=jnp.int32)
     odd = c & 1
@@ -273,11 +313,10 @@
     matrix_y = dft_matrix(res_y, n_py, width_y, NY, 1.0 / math.sqrt(NX * NY))
     matrix_x = dft_matrix(res_x, n_px, width_x, NX, 1.0)
     swap = [(i, i ^ 1) for i in range(n_py)]
-    parts = 4
-    each = tiles_x // parts
+    last = max(1, tiles_x // 4)
     halves = []
-    for i in range(parts):
-        own, other = deposit(start, order, data, coef, i * each, each, tiles_y, classes, 4)
+    for first, each in ((0, tiles_x - last), (tiles_x - last, last)):
+        own, other = deposit(plan, blocks, coef, first, each, tiles_y, classes, STEP_ROWS, DEPTH)
         halves.append((own, lax.ppermute(other, "py", swap)))
     return x_pass(matrix_x, [y_pass(matrix_y, own, got) for own, got in halves])
 

time: 691 us -> 501 us (0.73)
  Pallas kernels: 525 us -> 364 us
  waiting for transfers between devices: 115 us -> 85.1 us
  starting transfers between devices: 7.28 us -> 23.3 us
  between operations: 13.5 us -> 0.45 us
  blocking collectives: 11.6 us -> 0 us
  local copies, waits for them, and re-layouts: 3.31 us -> 10.5 us
    pallas_call x4 -> x2, Pallas kernels: 481 us -> 322 us  [deposit(): pl.pallas_call(functools.partial(deposit_kernel, classes=classes, ch=ch,...]
    all_gather x2 -> x0, waiting for transfers between devices: 115 us -> none  [the longest x1 69.5 us: gather(): return lax.all_gather(v, 'py', axis_index_groups=groups, tiled=True)]
    ppermute x0 -> x19, waiting for transfers between devices: none -> 80.8 us  [gather_rows(): lax.ppermute(u, axis, [(i, i ^ m) for i in range(n)])]
    ppermute x0 -> x19, starting transfers between devices: none -> 19.8 us  [gather_rows(): lax.ppermute(u, axis, [(i, i ^ m) for i in range(n)])]
    all_gather x2 -> x0, blocking collectives: 11.6 us -> none  [the longest x1 6.08 us: gather(): return lax.all_gather(v, 'py', axis_index_groups=groups, tiled=True)]
    pallas_call x4 -> x2, Pallas kernels: 24.5 us -> 22.3 us  [y_pass(): pl.pallas_call(y_kernel, grid=(x // BX,), in_specs=[whole(both), whole(lo...]
  transfers between devices with their start and end apart: 6 -> 21, of which waited for: 2 -> 11; matrix products, arithmetic and copies ran while one was open for 2% -> 4% of each run, Pallas kernels for 55% -> 18%
where the time goes in v2:
time: 501 us; the launch traced here: 498 us
  Pallas kernels  364 us (73%)
  waiting for transfers between devices  85.1 us (17%)
  starting transfers between devices  23.3 us (5%)
  other arithmetic  14.9 us (3%)
  local copies, waits for them, and re-layouts  10.5 us (2%)
    pallas_call x2, Pallas kernels, deposit(): pl.pallas_call(functools.partial(deposit_kernel, classes=classes, ch=ch,...  322 us
    ppermute x19, waiting for transfers between devices, gather_rows(): lax.ppermute(u, axis, [(i, i ^ m) for i in range(n)])  80.8 us
    pallas_call x2, Pallas kernels, y_pass(): pl.pallas_call(y_kernel, grid=(x // BX,), in_specs=[whole(both), whole(lo...  22.3 us
    ppermute x19, starting transfers between devices, gather_rows(): lax.ppermute(u, axis, [(i, i ^ m) for i in range(n)])  19.8 us
    pallas_call x1, Pallas kernels, x_pass(): pl.pallas_call(x_kernel, grid=(y // 8,), in_specs=[whole, whole] + [spec(...  19.4 us
  transfers between devices with their start and end apart: 21, of which 11 were waited for; matrix products, arithmetic and copies ran while one was open for 4% of the time, Pallas kernels for 18%

profile of v2, /device:TPU:17, one launch (start us, length us, event | category | flops | bytes accessed | tf_op | source)
XLA Modules:
  0.0 498.5 jit_solution(2947967641417308795)
XLA Ops:
  0.0 0.7 broadcast_multiply_fusion
  0.7 0.7 add_convert_fusion
  1.4 1.2 copy.9
  2.9 1.4 collective-permute-start.3
  4.4 1.3 collective-permute-start.11
  5.7 1.2 collective-permute-start.1
  6.9 1.2 collective-permute-start
  8.8 9.2 %collective-permute-done.1.refs_2_ = f32[264,512]{1,0:T(8,128)S(1)} collective-permute-done((f32[264,512]{1,0:T(8,128)S(1)}, f32[264,512]{1,0:T(8,128)S(1)}, u32[]{:S(2)}, u32[]{:S(2)}) %collective-permute-start.1) | collective-permute-done | bytes 540704 | tf_op jit(solution)/shard_map/ppermute | solution.py:262
  18.0 1.3 collective-permute-start.2
  19.3 6.2 %collective-permute-done.3.refs_5_ = f32[264,512]{1,0:T(8,128)} collective-permute-done((f32[264,512]{1,0:T(8,128)S(1)}, f32[264,512]{1,0:T(8,128)}, u32[]{:S(2)}, u32[]{:S(2)}) %collective-permute-start.3) | collective-permute-done | bytes 540704 | tf_op jit(solution)/shard_map/ppermute | solution.py:262
  25.5 1.2 collective-permute-start.5
  26.8 0.8 slice_bitcast_fusion.11
  27.8 1.2 collective-permute-start.9
  29.0 0.8 slice_bitcast_fusion.7
  29.8 22.2 %collective-permute-done.11.refs_15_ = f32[264,512]{1,0:T(8,128)} collective-permute-done((f32[264,512]{1,0:T(8,128)S(1)}, f32[264,512]{1,0:T(8,128)}, u32[]{:S(2)}, u32[]{:S(2)}) %collective-permute-start.11) | collective-permute-done | bytes 540704 | tf_op jit(solution)/shard_map/ppermute | solution.py:262
  52.0 0.7 slice_bitcast_fusion.3
  52.7 0.7 slice_bitcast_fusion.14
  53.5 1.0 slice.134
  54.5 1.3 collective-permute-start.15
  56.0 1.2 collective-permute-start.4
  57.6 1.3 collective-permute-start.12
  58.9 13.2 %collective-permute-done.13.refs_17_ = f32[264,512]{1,0:T(8,128)S(1)} collective-permute-done((f32[264,512]{1,0:T(8,128)}, f32[264,512]{1,0:T(8,128)S(1)}, u32[]{:S(2)}, u32[]{:S(2)}) %collective-permute-start.13) | collective-permute-done | bytes 540704 | tf_op jit(solution)/shard_map/ppermute | solution.py:262
  72.1 1.2 collective-permute-start.6
  73.8 5.5 %collective-permute-done.8.refs_11_ = f32[264,512]{1,0:T(8,128)S(1)} collective-permute-done((f32[264,512]{1,0:T(8,128)}, f32[264,512]{1,0:T(8,128)S(1)}, u32[]{:S(2)}, u32[]{:S(2)}) %collective-permute-start.8) | collective-permute-done | bytes 540704 | tf_op jit(solution)/shard_map/ppermute | solution.py:262
  79.2 1.2 collective-permute-start.14
  80.5 10.4 %collective-permute-done.12.refs_16_ = f32[264,512]{1,0:T(8,128)S(1)} collective-permute-done((f32[264,512]{1,0:T(8,128)}, f32[264,512]{1,0:T(8,128)S(1)}, u32[]{:S(2)}, u32[]{:S(2)}) %collective-permute-start.12) | collective-permute-done | bytes 540704 | tf_op jit(solution)/shard_map/ppermute | solution.py:262
  91.0 1.3 collective-permute-start.16
  92.4 4.4 collective-permute-done.6.refs_9_
  96.8 1.2 collective-permute-start.17
  98.1 4.7 collective-permute-done.10.refs_14_
  102.8 1.2 collective-permute-start.18
  104.0 4.7 collective-permute-done.14.refs_19_
  108.8 0.6 copy-done.14
  109.9 5.8 %sort.14 = (s32[4096]{0:T(1024)S(1)}, s32[4096]{0:T(1024)}) sort(s32[4096]{0:T(1024)S(1)} %bitcast.83, s32[4096]{0:T(1024)S(1)} %iota.67), dimensions={0}, to_apply=%region_0.1 | sort | flops 49152 | bytes 65536 | tf_op jit(solution)/shard_map/sort | solution.py:304
  116.7 0.6 add_select_fusion.2.order
  117.9 1.2 pad_add_fusion.span
  119.1 1.5 select_reduce_fusion
  120.7 0.6 copy-done.15
  121.7 241.3 %shard_map.55 = (f32[2,96,64,256]{3,2,1,0:T(8,128)}, f32[2,96,64,256]{3,2,1,0:T(8,128)}) custom-call(s32[1280]{0:T(1024)} %get-tuple-element.18.groups_of, s32[1280]{0:T(1024)} %get-tuple-element.17.firsts, s32[1280]{0:T(1024)} %get-tuple-element.16.ends, s32[4096]{0:T(1024)} %add_select_fusion.2.order, s32[9]{0:T(128)} %pad_add_fusion.span, ...), custom_call_target="tpu_custom_call" | custom-call | flops 79725330432 | bytes 8650752 | tf_op jit(solution)/shard_map/pallas_call | solution.py:147
  363.1 81.1 %shard_map.57 = (f32[2,32,64,256]{3,2,1,0:T(8,128)}, f32[2,32,64,256]{3,2,1,0:T(8,128)}) custom-call(s32[1280]{0:T(1024)} %get-tuple-element.18.groups_of, s32[1280]{0:T(1024)} %get-tuple-element.17.firsts, s32[1280]{0:T(1024)} %get-tuple-element.16.ends, s32[4096]{0:T(1024)} %add_select_fusion.2.order, s32[9]{0:T(128)} %pad_add_fusion.span, ...), custom_call_target="tpu_custom_call" | custom-call | flops 26575110144 | bytes 8650752 | tf_op jit(solution)/shard_map/pallas_call | solution.py:147
  444.3 3.5 collective-permute-start.20
  448.0 0.7 fusion.3
  449.6 0.7 fusion.1
  450.3 4.4 collective-permute-done.20.other
  454.7 2.1 copy-done
  456.8 6.1 %shard_map.58.refs_1_ = f32[2,32,64,256]{3,2,1,0:T(8,128)} custom-call(bf16[128,256]{1,0:T(8,128)(2,1)} %pad_maximum_fusion.1.m2, bf16[128,128]{1,0:T(8,128)(2,1)} %get-tuple-element.21.ml, f32[2,32,64,256]{3,2,1,0:T(8,128)} %get-tuple-element.14.own, f32[2,32,64,256]{3,2,1,0:T(8,128)} %copy-done), custom_call_target="tpu_custom_call" | custom-call | tf_op jit(solution)/shard_map/pallas_call | solution.py:204
  462.9 16.1 %shard_map.56.refs_0_ = f32[2,96,64,256]{3,2,1,0:T(8,128)} custom-call(bf16[128,256]{1,0:T(8,128)(2,1)} %pad_maximum_fusion.1.m2, bf16[128,128]{1,0:T(8,128)(2,1)} %get-tuple-element.21.ml, f32[2,96,64,256]{3,2,1,0:T(8,128)} %get-tuple-element.12.own, f32[2,96,64,256]{3,2,1,0:T(8,128)} %collective-permute-done.19.other), custom_call_target="tpu_custom_call" | custom-call | tf_op jit(solution)/shard_map/pallas_call | solution.py:204
  479.1 19.4 %shard_map.59 = f32[2,128,64,256]{3,2,1,0:T(8,128)} custom-call(bf16[256,256]{1,0:T(8,128)(2,1)} %get-tuple-element.20.mh, bf16[256,256]{1,0:T(8,128)(2,1)} %get-tuple-element.19.ml, f32[2,96,64,256]{3,2,1,0:T(8,128)} %shard_map.56.refs_0_, f32[2,32,64,256]{3,2,1,0:T(8,128)} %shard_map.58.refs_1_), custom_call_target="tpu_custom_call" | custom-call | tf_op jit(solution)/shard_map/pallas_call | solution.py:230
  (109 shorter events, 6.3 us)
Async XLA Ops:
  0.0 2.8 copy-start.9
  0.0 2.8 copy-start.10
  2.9 70.4 %copy-start.1 = (f32[264,512]{1,0:T(8,128)}, f32[264,512]{1,0:T(8,128)S(1)}, u32[]{:S(2)}) copy-start(f32[264,512]{1,0:T(8,128)S(1)} %pad_maximum_fusion.refs_0_) | copy-start | bytes 1622020
  2.9 22.6 %collective-permute-start.3 = (f32[264,512]{1,0:T(8,128)S(1)}, f32[264,512]{1,0:T(8,128)}, u32[]{:S(2)}, u32[]{:S(2)}) collective-permute-start(f32[264,512]{1,0:T(8,128)S(1)} %pad_maximum_fusion.refs_0_), channel_id=1, source_target_pairs={{0,8},{8,0},{16,24},{24,16},{1,9},{9,1},{17,25},{25,17},{2,10},{10... | collective-permute-start | bytes 1622024 | tf_op jit(solution)/shard_map/ppermute | solution.py:262
  4.3 23.5 %collective-permute-start.7 = (f32[264,512]{1,0:T(8,128)S(1)}, f32[264,512]{1,0:T(8,128)}, u32[]{:S(2)}, u32[]{:S(2)}) collective-permute-start(f32[264,512]{1,0:T(8,128)S(1)} %pad_maximum_fusion.refs_0_), channel_id=1, source_target_pairs={{0,16},{8,24},{16,0},{24,8},{1,17},{9,25},{17,1},{25,9},{2,18},{10... | collective-permute-start | bytes 1622024 | tf_op jit(solution)/shard_map/ppermute | solution.py:262
  4.4 47.6 %collective-permute-start.11 = (f32[264,512]{1,0:T(8,128)S(1)}, f32[264,512]{1,0:T(8,128)}, u32[]{:S(2)}, u32[]{:S(2)}) collective-permute-start(f32[264,512]{1,0:T(8,128)S(1)} %pad_maximum_fusion.refs_0_), channel_id=1, source_target_pairs={{0,24},{8,16},{16,8},{24,0},{1,25},{9,17},{17,9},{25,1},{2,26},{10... | collective-permute-start | bytes 1622024 | tf_op jit(solution)/shard_map/ppermute | solution.py:262
  5.7 12.4 %collective-permute-start.1 = (f32[264,512]{1,0:T(8,128)S(1)}, f32[264,512]{1,0:T(8,128)S(1)}, u32[]{:S(2)}, u32[]{:S(2)}) collective-permute-start(f32[264,512]{1,0:T(8,128)S(1)} %pad_maximum_fusion.refs_0_), channel_id=1, source_target_pairs={{0,4},{1,5},{2,6},{3,7},{4,0},{5,1},{6,2},{7,3},{8,12},{9,13},{10,... | collective-permute-start | bytes 1622024 | tf_op jit(solution)/shard_map/ppermute | solution.py:262
  6.9 45.8 %collective-permute-start = (f32[264,512]{1,0:T(8,128)S(1)}, f32[264,512]{1,0:T(8,128)}, u32[]{:S(2)}, u32[]{:S(2)}) collective-permute-start(f32[264,512]{1,0:T(8,128)S(1)} %pad_maximum_fusion.refs_0_), channel_id=1, source_target_pairs={{0,2},{1,3},{2,0},{3,1},{4,6},{5,7},{6,4},{7,5},{8,10},{9,11},{10,... | collective-permute-start | bytes 1622024 | tf_op jit(solution)/shard_map/ppermute | solution.py:262
  18.0 55.4 %copy-start.2 = (f32[264,512]{1,0:T(8,128)}, f32[264,512]{1,0:T(8,128)S(1)}, u32[]{:S(2)}) copy-start(f32[264,512]{1,0:T(8,128)S(1)} %collective-permute-done.1.refs_2_) | copy-start | bytes 1622020
  18.0 38.0 %collective-permute-start.2 = (f32[136,512]{1,0:T(8,128)S(1)}, f32[136,512]{1,0:T(8,128)S(1)}, u32[]{:S(2)}, u32[]{:S(2)}) collective-permute-start(f32[136,512]{1,0:T(8,128)S(1)} %slice.116), channel_id=1, source_target_pairs={{0,2},{1,3},{2,0},{3,1},{4,6},{5,7},{6,4},{7,5},{8,10},{9,11},{10,... | collective-permute-start | bytes 835592 | tf_op jit(solution)/shard_map/ppermute | solution.py:262
  25.5 31.8 %collective-permute-start.5 = (f32[264,512]{1,0:T(8,128)}, f32[264,512]{1,0:T(8,128)S(1)}, u32[]{:S(2)}, u32[]{:S(2)}) collective-permute-start(f32[264,512]{1,0:T(8,128)} %collective-permute-done.3.refs_5_), channel_id=1, source_target_pairs={{0,4},{1,5},{2,6},{3,7},{4,0},{5,1},{6,2},{7,3},{8,12},{9,13},{10,... | collective-permute-start | bytes 1622024 | tf_op jit(solution)/shard_map/ppermute | solution.py:262
  27.8 29.9 %collective-permute-start.9 = (f32[264,512]{1,0:T(8,128)}, f32[264,512]{1,0:T(8,128)S(1)}, u32[]{:S(2)}, u32[]{:S(2)}) collective-permute-start(f32[264,512]{1,0:T(8,128)} %collective-permute-done.7.refs_10_), channel_id=1, source_target_pairs={{0,4},{1,5},{2,6},{3,7},{4,0},{5,1},{6,2},{7,3},{8,12},{9,13},{10,... | collective-permute-start | bytes 1622024 | tf_op jit(solution)/shard_map/ppermute | solution.py:262
  54.5 66.1 %collective-permute-start.15 = (f32[128,512]{1,0:T(8,128)S(1)}, f32[128,512]{1,0:T(8,128)S(1)}, u32[]{:S(2)}, u32[]{:S(2)}) collective-permute-start(f32[128,512]{1,0:T(8,128)S(1)} %slice.134), channel_id=1, source_target_pairs={{0,4},{1,5},{2,6},{3,7},{4,0},{5,1},{6,2},{7,3},{8,12},{9,13},{10,... | collective-permute-start | bytes 786440 | tf_op jit(solution)/shard_map/ppermute | solution.py:262
  55.8 16.3 %collective-permute-start.13 = (f32[264,512]{1,0:T(8,128)}, f32[264,512]{1,0:T(8,128)S(1)}, u32[]{:S(2)}, u32[]{:S(2)}) collective-permute-start(f32[264,512]{1,0:T(8,128)} %collective-permute-done.11.refs_15_), channel_id=1, source_target_pairs={{0,4},{1,5},{2,6},{3,7},{4,0},{5,1},{6,2},{7,3},{8,12},{9,13},{10,... | collective-permute-start | bytes 1622024 | tf_op jit(solution)/shard_map/ppermute | solution.py:262
  56.0 35.0 %copy-start.11 = (f32[136,512]{1,0:T(8,128)}, f32[136,512]{1,0:T(8,128)S(1)}, u32[]{:S(2)}) copy-start(f32[136,512]{1,0:T(8,128)S(1)} %collective-permute-done.2.refs_4_) | copy-start | bytes 835588
  56.0 17.4 %collective-permute-start.4 = (f32[264,512]{1,0:T(8,128)}, f32[264,512]{1,0:T(8,128)S(1)}, u32[]{:S(2)}, u32[]{:S(2)}) collective-permute-start(f32[264,512]{1,0:T(8,128)} %collective-permute-done.3.refs_5_), channel_id=1, source_target_pairs={{0,2},{1,3},{2,0},{3,1},{4,6},{5,7},{6,4},{7,5},{8,10},{9,11},{10,... | collective-permute-start | bytes 1622024 | tf_op jit(solution)/shard_map/ppermute | solution.py:262
  57.3 35.0 %copy-start.3 = (f32[264,512]{1,0:T(8,128)}, f32[264,512]{1,0:T(8,128)S(1)}, u32[]{:S(2)}) copy-start(f32[264,512]{1,0:T(8,128)S(1)} %collective-permute-done.5.refs_7_) | copy-start | bytes 1622020
  57.3 21.9 %collective-permute-start.8 = (f32[264,512]{1,0:T(8,128)}, f32[264,512]{1,0:T(8,128)S(1)}, u32[]{:S(2)}, u32[]{:S(2)}) collective-permute-start(f32[264,512]{1,0:T(8,128)} %collective-permute-done.7.refs_10_), channel_id=1, source_target_pairs={{0,2},{1,3},{2,0},{3,1},{4,6},{5,7},{6,4},{7,5},{8,10},{9,11},{10,... | collective-permute-start | bytes 1622024 | tf_op jit(solution)/shard_map/ppermute | solution.py:262
  57.6 34.7 %copy-start.4 = (f32[264,512]{1,0:T(8,128)}, f32[264,512]{1,0:T(8,128)S(1)}, u32[]{:S(2)}) copy-start(f32[264,512]{1,0:T(8,128)S(1)} %collective-permute-done.9.refs_12_) | copy-start | bytes 1622020
  57.6 33.2 %collective-permute-start.12 = (f32[264,512]{1,0:T(8,128)}, f32[264,512]{1,0:T(8,128)S(1)}, u32[]{:S(2)}, u32[]{:S(2)}) collective-permute-start(f32[264,512]{1,0:T(8,128)} %collective-permute-done.11.refs_15_), channel_id=1, source_target_pairs={{0,2},{1,3},{2,0},{3,1},{4,6},{5,7},{6,4},{7,5},{8,10},{9,11},{10,... | collective-permute-start | bytes 1622024 | tf_op jit(solution)/shard_map/ppermute | solution.py:262
  72.1 20.2 %copy-start.5 = (f32[264,512]{1,0:T(8,128)}, f32[264,512]{1,0:T(8,128)S(1)}, u32[]{:S(2)}) copy-start(f32[264,512]{1,0:T(8,128)S(1)} %collective-permute-done.13.refs_17_) | copy-start | bytes 1622020
  72.1 24.6 %collective-permute-start.6 = (f32[136,512]{1,0:T(8,128)S(1)}, f32[136,512]{1,0:T(8,128)S(1)}, u32[]{:S(2)}, u32[]{:S(2)}) collective-permute-start(f32[136,512]{1,0:T(8,128)S(1)} %slice.121), channel_id=1, source_target_pairs={{0,2},{1,3},{2,0},{3,1},{4,6},{5,7},{6,4},{7,5},{8,10},{9,11},{10,... | collective-permute-start | bytes 835592 | tf_op jit(solution)/shard_map/ppermute | solution.py:262
  73.4 35.3 %copy-start.6 = (f32[264,512]{1,0:T(8,128)}, f32[264,512]{1,0:T(8,128)S(1)}, u32[]{:S(2)}) copy-start(f32[264,512]{1,0:T(8,128)S(1)} %collective-permute-done.4.refs_6_) | copy-start | bytes 1622020
  73.5 29.3 %collective-permute-start.10 = (f32[136,512]{1,0:T(8,128)S(1)}, f32[136,512]{1,0:T(8,128)S(1)}, u32[]{:S(2)}, u32[]{:S(2)}) collective-permute-start(f32[136,512]{1,0:T(8,128)S(1)} %slice.126), channel_id=1, source_target_pairs={{0,2},{1,3},{2,0},{3,1},{4,6},{5,7},{6,4},{7,5},{8,10},{9,11},{10,... | collective-permute-start | bytes 835592 | tf_op jit(solution)/shard_map/ppermute | solution.py:262
  79.2 29.5 %copy-start.7 = (f32[264,512]{1,0:T(8,128)}, f32[264,512]{1,0:T(8,128)S(1)}, u32[]{:S(2)}) copy-start(f32[264,512]{1,0:T(8,128)S(1)} %collective-permute-done.8.refs_11_) | copy-start | bytes 1622020
  79.2 29.5 %collective-permute-start.14 = (f32[136,512]{1,0:T(8,128)S(1)}, f32[136,512]{1,0:T(8,128)S(1)}, u32[]{:S(2)}, u32[]{:S(2)}) collective-permute-start(f32[136,512]{1,0:T(8,128)S(1)} %slice.131), channel_id=1, source_target_pairs={{0,2},{1,3},{2,0},{3,1},{4,6},{5,7},{6,4},{7,5},{8,10},{9,11},{10,... | collective-permute-start | bytes 835592 | tf_op jit(solution)/shard_map/ppermute | solution.py:262
  90.8 18.0 %copy-start.8 = (f32[264,512]{1,0:T(8,128)}, f32[264,512]{1,0:T(8,128)S(1)}, u32[]{:S(2)}) copy-start(f32[264,512]{1,0:T(8,128)S(1)} %collective-permute-done.12.refs_16_) | copy-start | bytes 1622020
  91.0 29.6 %collective-permute-start.16 = (f32[128,512]{1,0:T(8,128)S(1)}, f32[128,512]{1,0:T(8,128)S(1)}, u32[]{:S(2)}, u32[]{:S(2)}) collective-permute-start(f32[128,512]{1,0:T(8,128)S(1)} %slice.135), channel_id=1, source_target_pairs={{0,4},{1,5},{2,6},{3,7},{4,0},{5,1},{6,2},{7,3},{8,12},{9,13},{10,... | collective-permute-start | bytes 786440 | tf_op jit(solution)/shard_map/ppermute | solution.py:262
  96.8 12.0 %copy-start.12 = (f32[136,512]{1,0:T(8,128)}, f32[136,512]{1,0:T(8,128)S(1)}, u32[]{:S(2)}) copy-start(f32[136,512]{1,0:T(8,128)S(1)} %collective-permute-done.6.refs_9_) | copy-start | bytes 835588
  96.8 23.9 %collective-permute-start.17 = (f32[128,512]{1,0:T(8,128)S(1)}, f32[128,512]{1,0:T(8,128)S(1)}, u32[]{:S(2)}, u32[]{:S(2)}) collective-permute-start(f32[128,512]{1,0:T(8,128)S(1)} %slice.136), channel_id=1, source_target_pairs={{0,4},{1,5},{2,6},{3,7},{4,0},{5,1},{6,2},{7,3},{8,12},{9,13},{10,... | collective-permute-start | bytes 786440 | tf_op jit(solution)/shard_map/ppermute | solution.py:262
  102.8 18.0 %copy-start.13 = (f32[136,512]{1,0:T(8,128)}, f32[136,512]{1,0:T(8,128)S(1)}, u32[]{:S(2)}) copy-start(f32[136,512]{1,0:T(8,128)S(1)} %collective-permute-done.10.refs_14_) | copy-start | bytes 835588
  102.8 17.9 %collective-permute-start.18 = (f32[128,512]{1,0:T(8,128)S(1)}, f32[128,512]{1,0:T(8,128)S(1)}, u32[]{:S(2)}, u32[]{:S(2)}) collective-permute-start(f32[128,512]{1,0:T(8,128)S(1)} %slice.137), channel_id=1, source_target_pairs={{0,4},{1,5},{2,6},{3,7},{4,0},{5,1},{6,2},{7,3},{8,12},{9,13},{10,... | collective-permute-start | bytes 786440 | tf_op jit(solution)/shard_map/ppermute | solution.py:262
  108.7 0.7 copy-start.14
  120.7 0.7 copy-start.15
  120.7 0.8 copy-start.16
  120.7 0.9 copy-start.17
  120.7 1.0 copy-start.18
  363.0 99.9 %collective-permute-start.19 = (f32[2,96,64,256]{3,2,1,0:T(8,128)}, f32[2,96,64,256]{3,2,1,0:T(8,128)}, u32[]{:S(2)}, u32[]{:S(2)}) collective-permute-start(f32[2,96,64,256]{3,2,1,0:T(8,128)} %get-tuple-element.13), channel_id=1, source_target_pairs={{0,1},{1,0},{2,3},{3,2},{4,5},{5,4},{6,7},{7,6},{8,9},{9,8},{10,11... | collective-permute-start | bytes 37748744 | tf_op jit(solution)/shard_map/ppermute | solution.py:320
  444.3 10.5 %collective-permute-start.20 = (f32[2,32,64,256]{3,2,1,0:T(8,128)}, f32[2,32,64,256]{3,2,1,0:T(8,128)S(1)}, u32[]{:S(2)}, u32[]{:S(2)}) collective-permute-start(f32[2,32,64,256]{3,2,1,0:T(8,128)} %get-tuple-element.15), channel_id=1, source_target_pairs={{0,1},{1,0},{2,3},{3,2},{4,5},{5,4},{6,7},{7,6},{8,9},{9,8},{10,11... | collective-permute-start | bytes 12582920 | tf_op jit(solution)/shard_map/ppermute | solution.py:320
  454.7 2.1 copy-start

commit v3 on v2

--- a/solution.py
+++ b/solution.py
@@ -15,9 +15,9 @@
 BY = 8
 BF = jnp.bfloat16
 VMEM = 56 << 20
-STEP_ROWS = 4
+STEP_ROWS = 2
 PAIR = 2
-DEPTH = 6
+DEPTH = 32
 LANES = 128
 
 
@@ -38,17 +38,17 @@
     return jnp.dot(a, b, preferred_element_type=jnp.float32)
 
 
-def fill(x, y, z, w, part, planar_hi, planar_lo, depth_hi, depth_lo):
+def fill(x, y, z, w):
     width = x.shape[1]
     ix = lax.broadcasted_iota(jnp.int32, (BX, width), 0).astype(jnp.float32)
     iy = lax.broadcasted_iota(jnp.int32, (BY, width), 0).astype(jnp.float32)
-    lanes = slice(part * width, (part + 1) * width)
     wx = spline(x - ix)
     wy = spline(y - iy) * w
+    planar_hi, planar_lo, depth_hi, depth_lo = [], [], [], []
     for i in range(0, BX, 2):
         hi, lo = split(jnp.concatenate([wx[i : i + 1] * wy, wx[i + 1 : i + 2] * wy], 0))
-        planar_hi[i * BY : (i + 2) * BY, lanes] = hi
-        planar_lo[i * BY : (i + 2) * BY, lanes] = lo
+        planar_hi.append(hi)
+        planar_lo.append(lo)
     q0 = jnp.floor((z - 1.0) * 0.0625)
     away = (z - 16.0 * q0) - ix
     far = away > 8.0
@@ -60,39 +60,40 @@
     column_block = (lax.broadcasted_iota(jnp.int32, (width, LANES), 1) // 16).astype(jnp.float32)
     for t in range(NZ // LANES):
         here = block == (column_block + float(t * (LANES // 16))).astype(BF)
-        depth_hi[lanes, t * LANES : (t + 1) * LANES] = jnp.where(here, hi, zero)
-        depth_lo[lanes, t * LANES : (t + 1) * LANES] = jnp.where(here, lo, zero)
+        depth_hi.append(jnp.where(here, hi, zero))
+        depth_lo.append(jnp.where(here, lo, zero))
+    return [jnp.concatenate(v, 0) for v in (planar_hi, planar_lo)] + [jnp.concatenate(v, 1) for v in (depth_hi, depth_lo)]
 
 
 def deposit_kernel(
     groups_of, firsts, ends, order, span, coef, *refs, classes, ch, depth, first, blocks
 ):
-    parts, (own, other, acc, data, arrived), bufs = refs[:blocks], refs[blocks : blocks + 5], refs[blocks + 5 :]
+    parts, (own, other, acc, data, arrived) = refs[:blocks], refs[blocks:]
     tile = pl.program_id(0) * pl.num_programs(1) + pl.program_id(1)
     width = data.shape[1] // 4
     base = first * pl.num_programs(1) * classes
-    sets = [bufs[4 * k : 4 * k + 4] for k in range(depth)]
-
-    def make(t, which):
+
+    def multiply(t, stop):
+        live = t < stop
         t = jnp.minimum(t, groups_of.shape[0] - 1)
-        j0, e = firsts[t], ends[t]
-        for u in range(ch):
-            entry = order[jnp.minimum(j0 + u, order.shape[0] - 1)]
-            sign = jnp.where(j0 + u < e, (1 - 2 * (entry & 1)).astype(jnp.float32), 0.0)
-            row = data[pl.ds(entry >> 1, 1), :]
-            x, y, z, w = (row[:, k * width : (k + 1) * width] for k in range(4))
-            fill(x, y, z, w * sign, u, *sets[which])
-
-    def multiply(t, which, stop):
-        g = jnp.where(t < stop, groups_of[jnp.minimum(t, groups_of.shape[0] - 1)] - base, acc.shape[0] - 1)
-        planar_hi, planar_lo, depth_hi, depth_lo = (r[...] for r in sets[which])
-        cells = planar_hi.shape[0]
-        v = acc[g]
+        j0, e = firsts[t], jnp.where(live, ends[t], 0)
+        g = jnp.where(live, groups_of[t] - base, acc.shape[0] - 1)
+        v = None
         for u in range(0, ch, PAIR):
-            lanes = slice(u * width, (u + PAIR) * width)
-            both = dot(jnp.concatenate([planar_hi[:, lanes], planar_lo[:, lanes]], 0), depth_hi[lanes])
-            v = v + (both[:cells] + both[cells:] + dot(planar_hi[:, lanes], depth_lo[lanes]))
-        acc[g] = v
+            made = []
+            for j in range(u, u + PAIR):
+                entry = order[jnp.minimum(j0 + j, order.shape[0] - 1)]
+                sign = jnp.where(j0 + j < e, (1 - 2 * (entry & 1)).astype(jnp.float32), 0.0)
+                row = data[pl.ds(entry >> 1, 1), :]
+                x, y, z, w = (row[:, k * width : (k + 1) * width] for k in range(4))
+                made.append(fill(x, y, z, w * sign))
+            ph, plo = (jnp.concatenate([m[k] for m in made], 1) for k in range(2))
+            dh, dl = (jnp.concatenate([m[k] for m in made], 0) for k in range(2, 4))
+            cells = ph.shape[0]
+            both = dot(jnp.concatenate([ph, plo], 0), dh)
+            p = both[:cells] + both[cells:] + dot(ph, dl)
+            v = p if v is None else v + p
+        acc[g] += v
 
     @pl.when(tile == 0)
     def _():
@@ -112,14 +113,11 @@
         for copy in copies:
             copy.wait()
         begin, stop = span[first], span[first + pl.num_programs(0)]
-        for k in range(depth):
-            make(begin + k, k)
 
         def step(i, _):
             for k in range(depth):
                 t = begin + i * depth + k
-                multiply(t, k, stop)
-                make(t + depth, k)
+                multiply(t, stop)
             return 0
 
         lax.fori_loop(0, (stop - begin + depth - 1) // depth, step, 0)
@@ -137,12 +135,6 @@
     width = lanes // 4
     spec = lambda: pl.BlockSpec((2, BX, BY, NZ), lambda i, j, *_: (0, i, j, 0))
     shape = jax.ShapeDtypeStruct((2, tiles_x * BX, tiles_y * BY, NZ), jnp.float32)
-    buffers = [
-        pltpu.VMEM((BX * BY, ch * width), BF),
-        pltpu.VMEM((BX * BY, ch * width), BF),
-        pltpu.VMEM((ch * width, NZ), BF),
-        pltpu.VMEM((ch * width, NZ), BF),
-    ]
     flops = 6 * rows * BX * BY * NZ * width * tiles_x // 8
     return pl.pallas_call(
         functools.partial(deposit_kernel, classes=classes, ch=ch, depth=depth, first=first, blocks=len(blocks)),
@@ -155,8 +147,7 @@
                 pltpu.VMEM((tiles_x * tiles_y * classes + 1, BX * BY, NZ), jnp.float32),
                 pltpu.VMEM((rows, lanes), jnp.float32),
                 pltpu.SemaphoreType.DMA((len(blocks),)),
-            ]
-            + buffers * depth,
+            ],
         ),
         out_shape=[shape, shape],
         compiler_params=pltpu.CompilerParams(vmem_limit_bytes=VMEM),
@@ -208,6 +199,7 @@
         out_specs=spec(),
         out_shape=jax.ShapeDtypeStruct(own.shape, jnp.float32),
         compiler_params=pltpu.CompilerParams(vmem_limit_bytes=VMEM),
+        cost_estimate=pl.CostEstimate(flops=24 * x * y * y * z, bytes_accessed=24 * x * y * z, transcendentals=0),
     )(both, lo, own, other)
 
 

time: 501 us -> 390 us (0.78)
  Pallas kernels: 364 us -> 253 us
    pallas_call x2, Pallas kernels: 322 us -> 211 us  [deposit(): pl.pallas_call(functools.partial(deposit_kernel, classes=classes, ch=ch,...]
  transfers between devices with their start and end apart: 21 -> 21, of which waited for: 11 -> 11; matrix products, arithmetic and copies ran while one was open for 4% -> 5% of each run, Pallas kernels for 18% -> 16%
where the time goes in v3:
time: 390 us; the launch traced here: 389 us
  Pallas kernels  253 us (65%)
  waiting for transfers between devices  85.5 us (22%)
  starting transfers between devices  23.2 us (6%)
  other arithmetic  16.6 us (4%)
  local copies, waits for them, and re-layouts  10.4 us (3%)
    pallas_call x2, Pallas kernels, deposit(): pl.pallas_call(functools.partial(deposit_kernel, classes=classes, ch=ch,...  211 us
    ppermute x19, waiting for transfers between devices, gather_rows(): lax.ppermute(u, axis, [(i, i ^ m) for i in range(n)])  80.7 us
    pallas_call x2, Pallas kernels, y_pass(): pl.pallas_call(y_kernel, grid=(x // BX,), in_specs=[whole(both), whole(lo...  22.3 us
    ppermute x19, starting transfers between devices, gather_rows(): lax.ppermute(u, axis, [(i, i ^ m) for i in range(n)])  19.8 us
    pallas_call x1, Pallas kernels, x_pass(): pl.pallas_call(x_kernel, grid=(y // 8,), in_specs=[whole, whole] + [spec(...  19.4 us
    unnamed x64, local copies, waits for them, and re-layouts  8 us
  transfers between devices with their start and end apart: 21, of which 11 were waited for; matrix products, arithmetic and copies ran while one was open for 5% of the time, Pallas kernels for 16%

profile of v3, /device:TPU:17, one launch (start us, length us, event | category | flops | bytes accessed | tf_op | source)
XLA Modules:
  0.0 388.7 jit_solution(976215923743708220)
XLA Ops:
  0.0 0.7 broadcast_multiply_fusion
  0.7 0.7 add_convert_fusion
  1.4 1.2 copy.9
  2.7 1.0 fusion.2
  3.8 1.4 collective-permute-start.3
  5.2 1.3 collective-permute-start.11
  6.5 1.2 collective-permute-start.1
  7.7 1.2 collective-permute-start
  9.7 9.2 %collective-permute-done.1.refs_2_ = f32[264,512]{1,0:T(8,128)S(1)} collective-permute-done((f32[264,512]{1,0:T(8,128)S(1)}, f32[264,512]{1,0:T(8,128)S(1)}, u32[]{:S(2)}, u32[]{:S(2)}) %collective-permute-start.1) | collective-permute-done | bytes 540704 | tf_op jit(solution)/shard_map/ppermute | solution.py:254
  18.9 1.3 collective-permute-start.2
  20.2 6.2 %collective-permute-done.3.refs_5_ = f32[264,512]{1,0:T(8,128)} collective-permute-done((f32[264,512]{1,0:T(8,128)S(1)}, f32[264,512]{1,0:T(8,128)}, u32[]{:S(2)}, u32[]{:S(2)}) %collective-permute-start.3) | collective-permute-done | bytes 540704 | tf_op jit(solution)/shard_map/ppermute | solution.py:254
  26.4 1.2 collective-permute-start.5
  27.6 0.8 slice_bitcast_fusion.11
  28.6 1.2 collective-permute-start.9
  29.9 0.8 slice_bitcast_fusion.7
  30.6 22.2 %collective-permute-done.11.refs_15_ = f32[264,512]{1,0:T(8,128)} collective-permute-done((f32[264,512]{1,0:T(8,128)S(1)}, f32[264,512]{1,0:T(8,128)}, u32[]{:S(2)}, u32[]{:S(2)}) %collective-permute-start.11) | collective-permute-done | bytes 540704 | tf_op jit(solution)/shard_map/ppermute | solution.py:254
  52.8 0.7 slice_bitcast_fusion.3
  53.5 0.7 slice_bitcast_fusion.14
  54.4 1.0 slice.134
  55.4 1.3 collective-permute-start.15
  56.9 1.2 collective-permute-start.4
  58.5 1.3 collective-permute-start.12
  59.8 13.2 %collective-permute-done.13.refs_17_ = f32[264,512]{1,0:T(8,128)S(1)} collective-permute-done((f32[264,512]{1,0:T(8,128)}, f32[264,512]{1,0:T(8,128)S(1)}, u32[]{:S(2)}, u32[]{:S(2)}) %collective-permute-start.13) | collective-permute-done | bytes 540704 | tf_op jit(solution)/shard_map/ppermute | solution.py:254
  73.0 1.2 collective-permute-start.6
  74.6 5.5 %collective-permute-done.8.refs_11_ = f32[264,512]{1,0:T(8,128)S(1)} collective-permute-done((f32[264,512]{1,0:T(8,128)}, f32[264,512]{1,0:T(8,128)S(1)}, u32[]{:S(2)}, u32[]{:S(2)}) %collective-permute-start.8) | collective-permute-done | bytes 540704 | tf_op jit(solution)/shard_map/ppermute | solution.py:254
  80.1 1.2 collective-permute-start.14
  81.3 10.4 %collective-permute-done.12.refs_16_ = f32[264,512]{1,0:T(8,128)S(1)} collective-permute-done((f32[264,512]{1,0:T(8,128)}, f32[264,512]{1,0:T(8,128)S(1)}, u32[]{:S(2)}, u32[]{:S(2)}) %collective-permute-start.12) | collective-permute-done | bytes 540704 | tf_op jit(solution)/shard_map/ppermute | solution.py:254
  91.9 1.3 collective-permute-start.16
  93.2 4.4 %collective-permute-done.6.refs_9_ = f32[136,512]{1,0:T(8,128)S(1)} collective-permute-done((f32[136,512]{1,0:T(8,128)S(1)}, f32[136,512]{1,0:T(8,128)S(1)}, u32[]{:S(2)}, u32[]{:S(2)}) %collective-permute-start.6) | collective-permute-done | bytes 278560 | tf_op jit(solution)/shard_map/ppermute | solution.py:254
  97.6 1.2 collective-permute-start.17
  98.9 4.8 %collective-permute-done.10.refs_14_ = f32[136,512]{1,0:T(8,128)S(1)} collective-permute-done((f32[136,512]{1,0:T(8,128)S(1)}, f32[136,512]{1,0:T(8,128)S(1)}, u32[]{:S(2)}, u32[]{:S(2)}) %collective-permute-start.10) | collective-permute-done | bytes 278560 | tf_op jit(solution)/shard_map/ppermute | solution.py:254
  103.7 1.2 collective-permute-start.18
  105.0 4.6 %collective-permute-done.14.refs_19_ = f32[136,512]{1,0:T(8,128)S(1)} collective-permute-done((f32[136,512]{1,0:T(8,128)S(1)}, f32[136,512]{1,0:T(8,128)S(1)}, u32[]{:S(2)}, u32[]{:S(2)}) %collective-permute-start.14) | collective-permute-done | bytes 278560 | tf_op jit(solution)/shard_map/ppermute | solution.py:254
  110.8 5.8 %sort.14 = (s32[4096]{0:T(1024)S(1)}, s32[4096]{0:T(1024)}) sort(s32[4096]{0:T(1024)S(1)} %bitcast.83, s32[4096]{0:T(1024)S(1)} %iota.67), dimensions={0}, to_apply=%region_0.1 | sort | flops 49152 | bytes 65536 | tf_op jit(solution)/shard_map/sort | solution.py:296
  118.1 2.3 select_reduce_fusion
  120.4 1.3 pad_add_fusion.span
  122.4 0.6 copy-done.13
  123.2 154.4 %shard_map.55 = (f32[2,96,64,256]{3,2,1,0:T(8,128)}, f32[2,96,64,256]{3,2,1,0:T(8,128)}) custom-call(s32[2304]{0:T(1024)} %get-tuple-element.18.groups_of, s32[2304]{0:T(1024)} %get-tuple-element.17.firsts, s32[2304]{0:T(1024)} %get-tuple-element.16.ends, s32[4096]{0:T(1024)} %add_select_fusion.2.order, s32[9]{0:T(128)} %pad_add_fusion.span, ...), custom_call_target="tpu_custom_call" | custom-call | flops 79725330432 | bytes 8650752 | tf_op jit(solution)/shard_map/pallas_call | solution.py:139
  277.6 3.4 collective-permute-start.19
  280.9 56.6 %shard_map.57 = (f32[2,32,64,256]{3,2,1,0:T(8,128)}, f32[2,32,64,256]{3,2,1,0:T(8,128)}) custom-call(s32[2304]{0:T(1024)} %get-tuple-element.18.groups_of, s32[2304]{0:T(1024)} %get-tuple-element.17.firsts, s32[2304]{0:T(1024)} %get-tuple-element.16.ends, s32[4096]{0:T(1024)} %add_select_fusion.2.order, s32[9]{0:T(128)} %pad_add_fusion.span, ...), custom_call_target="tpu_custom_call" | custom-call | flops 26575110144 | bytes 8650752 | tf_op jit(solution)/shard_map/pallas_call | solution.py:139
  337.9 0.7 fusion.3
  338.6 0.6 pad_maximum_fusion.1.m2
  339.6 0.7 fusion.1
  340.3 4.7 %collective-permute-done.20.other = f32[2,32,64,256]{3,2,1,0:T(8,128)S(1)} collective-permute-done((f32[2,32,64,256]{3,2,1,0:T(8,128)}, f32[2,32,64,256]{3,2,1,0:T(8,128)S(1)}, u32[]{:S(2)}, u32[]{:S(2)}) %collective-permute-start.20) | collective-permute-done | bytes 4194336 | tf_op jit(solution)/shard_map/ppermute | solution.py:312
  345.0 2.1 copy-done
  347.1 6.1 %shard_map.58.refs_1_ = f32[2,32,64,256]{3,2,1,0:T(8,128)} custom-call(bf16[128,256]{1,0:T(8,128)(2,1)} %pad_maximum_fusion.1.m2, bf16[128,128]{1,0:T(8,128)(2,1)} %get-tuple-element.21.ml, f32[2,32,64,256]{3,2,1,0:T(8,128)} %get-tuple-element.14.own, f32[2,32,64,256]{3,2,1,0:T(8,128)} %copy-done), custom_call_target="tpu_custom_call" | custom-call | flops 805306368 | bytes 12582912 | tf_op jit(solution)/shard_map/pallas_call | solution.py:195
  353.2 16.2 %shard_map.56.refs_0_ = f32[2,96,64,256]{3,2,1,0:T(8,128)} custom-call(bf16[128,256]{1,0:T(8,128)(2,1)} %pad_maximum_fusion.1.m2, bf16[128,128]{1,0:T(8,128)(2,1)} %get-tuple-element.21.ml, f32[2,96,64,256]{3,2,1,0:T(8,128)} %get-tuple-element.12.own, f32[2,96,64,256]{3,2,1,0:T(8,128)} %collective-permute-done.19.other), custom_call_target="tpu_custom_call" | custom-call | flops 2415919104 | bytes 37748736 | tf_op jit(solution)/shard_map/pallas_call | solution.py:195
  369.4 19.4 %shard_map.59 = f32[2,128,64,256]{3,2,1,0:T(8,128)} custom-call(bf16[256,256]{1,0:T(8,128)(2,1)} %get-tuple-element.20.mh, bf16[256,256]{1,0:T(8,128)(2,1)} %get-tuple-element.19.ml, f32[2,96,64,256]{3,2,1,0:T(8,128)} %shard_map.56.refs_0_, f32[2,32,64,256]{3,2,1,0:T(8,128)} %shard_map.58.refs_1_), custom_call_target="tpu_custom_call" | custom-call | tf_op jit(solution)/shard_map/pallas_call | solution.py:222
  (103 shorter events, 6.8 us)
Async XLA Ops:
  3.8 89.4 %copy-start.1 = (f32[264,512]{1,0:T(8,128)}, f32[264,512]{1,0:T(8,128)S(1)}, u32[]{:S(2)}) copy-start(f32[264,512]{1,0:T(8,128)S(1)} %pad_maximum_fusion.refs_0_) | copy-start | bytes 1622020
  3.8 22.6 %collective-permute-start.3 = (f32[264,512]{1,0:T(8,128)S(1)}, f32[264,512]{1,0:T(8,128)}, u32[]{:S(2)}, u32[]{:S(2)}) collective-permute-start(f32[264,512]{1,0:T(8,128)S(1)} %pad_maximum_fusion.refs_0_), channel_id=1, source_target_pairs={{0,8},{8,0},{16,24},{24,16},{1,9},{9,1},{17,25},{25,17},{2,10},{10... | collective-permute-start | bytes 1622024 | tf_op jit(solution)/shard_map/ppermute | solution.py:254
  5.2 23.5 %collective-permute-start.7 = (f32[264,512]{1,0:T(8,128)S(1)}, f32[264,512]{1,0:T(8,128)}, u32[]{:S(2)}, u32[]{:S(2)}) collective-permute-start(f32[264,512]{1,0:T(8,128)S(1)} %pad_maximum_fusion.refs_0_), channel_id=1, source_target_pairs={{0,16},{8,24},{16,0},{24,8},{1,17},{9,25},{17,1},{25,9},{2,18},{10... | collective-permute-start | bytes 1622024 | tf_op jit(solution)/shard_map/ppermute | solution.py:254
  5.2 47.6 %collective-permute-start.11 = (f32[264,512]{1,0:T(8,128)S(1)}, f32[264,512]{1,0:T(8,128)}, u32[]{:S(2)}, u32[]{:S(2)}) collective-permute-start(f32[264,512]{1,0:T(8,128)S(1)} %pad_maximum_fusion.refs_0_), channel_id=1, source_target_pairs={{0,24},{8,16},{16,8},{24,0},{1,25},{9,17},{17,9},{25,1},{2,26},{10... | collective-permute-start | bytes 1622024 | tf_op jit(solution)/shard_map/ppermute | solution.py:254
  6.5 12.4 %collective-permute-start.1 = (f32[264,512]{1,0:T(8,128)S(1)}, f32[264,512]{1,0:T(8,128)S(1)}, u32[]{:S(2)}, u32[]{:S(2)}) collective-permute-start(f32[264,512]{1,0:T(8,128)S(1)} %pad_maximum_fusion.refs_0_), channel_id=1, source_target_pairs={{0,4},{1,5},{2,6},{3,7},{4,0},{5,1},{6,2},{7,3},{8,12},{9,13},{10,... | collective-permute-start | bytes 1622024 | tf_op jit(solution)/shard_map/ppermute | solution.py:254
  7.7 45.8 %collective-permute-start = (f32[264,512]{1,0:T(8,128)S(1)}, f32[264,512]{1,0:T(8,128)}, u32[]{:S(2)}, u32[]{:S(2)}) collective-permute-start(f32[264,512]{1,0:T(8,128)S(1)} %pad_maximum_fusion.refs_0_), channel_id=1, source_target_pairs={{0,2},{1,3},{2,0},{3,1},{4,6},{5,7},{6,4},{7,5},{8,10},{9,11},{10,... | collective-permute-start | bytes 1622024 | tf_op jit(solution)/shard_map/ppermute | solution.py:254
  18.9 74.4 %copy-start.2 = (f32[264,512]{1,0:T(8,128)}, f32[264,512]{1,0:T(8,128)S(1)}, u32[]{:S(2)}) copy-start(f32[264,512]{1,0:T(8,128)S(1)} %collective-permute-done.1.refs_2_) | copy-start | bytes 1622020
  18.9 38.0 %collective-permute-start.2 = (f32[136,512]{1,0:T(8,128)S(1)}, f32[136,512]{1,0:T(8,128)S(1)}, u32[]{:S(2)}, u32[]{:S(2)}) collective-permute-start(f32[136,512]{1,0:T(8,128)S(1)} %slice.116), channel_id=1, source_target_pairs={{0,2},{1,3},{2,0},{3,1},{4,6},{5,7},{6,4},{7,5},{8,10},{9,11},{10,... | collective-permute-start | bytes 835592 | tf_op jit(solution)/shard_map/ppermute | solution.py:254
  26.4 31.8 %collective-permute-start.5 = (f32[264,512]{1,0:T(8,128)}, f32[264,512]{1,0:T(8,128)S(1)}, u32[]{:S(2)}, u32[]{:S(2)}) collective-permute-start(f32[264,512]{1,0:T(8,128)} %collective-permute-done.3.refs_5_), channel_id=1, source_target_pairs={{0,4},{1,5},{2,6},{3,7},{4,0},{5,1},{6,2},{7,3},{8,12},{9,13},{10,... | collective-permute-start | bytes 1622024 | tf_op jit(solution)/shard_map/ppermute | solution.py:254
  28.6 29.9 %collective-permute-start.9 = (f32[264,512]{1,0:T(8,128)}, f32[264,512]{1,0:T(8,128)S(1)}, u32[]{:S(2)}, u32[]{:S(2)}) collective-permute-start(f32[264,512]{1,0:T(8,128)} %collective-permute-done.7.refs_10_), channel_id=1, source_target_pairs={{0,4},{1,5},{2,6},{3,7},{4,0},{5,1},{6,2},{7,3},{8,12},{9,13},{10,... | collective-permute-start | bytes 1622024 | tf_op jit(solution)/shard_map/ppermute | solution.py:254
  55.4 66.9 %collective-permute-start.15 = (f32[128,512]{1,0:T(8,128)S(1)}, f32[128,512]{1,0:T(8,128)S(1)}, u32[]{:S(2)}, u32[]{:S(2)}) collective-permute-start(f32[128,512]{1,0:T(8,128)S(1)} %slice.134), channel_id=1, source_target_pairs={{0,4},{1,5},{2,6},{3,7},{4,0},{5,1},{6,2},{7,3},{8,12},{9,13},{10,... | collective-permute-start | bytes 786440 | tf_op jit(solution)/shard_map/ppermute | solution.py:254
  56.7 16.3 %collective-permute-start.13 = (f32[264,512]{1,0:T(8,128)}, f32[264,512]{1,0:T(8,128)S(1)}, u32[]{:S(2)}, u32[]{:S(2)}) collective-permute-start(f32[264,512]{1,0:T(8,128)} %collective-permute-done.11.refs_15_), channel_id=1, source_target_pairs={{0,4},{1,5},{2,6},{3,7},{4,0},{5,1},{6,2},{7,3},{8,12},{9,13},{10,... | collective-permute-start | bytes 1622024 | tf_op jit(solution)/shard_map/ppermute | solution.py:254
  56.9 65.4 %copy-start.9 = (f32[136,512]{1,0:T(8,128)}, f32[136,512]{1,0:T(8,128)S(1)}, u32[]{:S(2)}) copy-start(f32[136,512]{1,0:T(8,128)S(1)} %collective-permute-done.2.refs_4_) | copy-start | bytes 835588
  56.9 17.4 %collective-permute-start.4 = (f32[264,512]{1,0:T(8,128)}, f32[264,512]{1,0:T(8,128)S(1)}, u32[]{:S(2)}, u32[]{:S(2)}) collective-permute-start(f32[264,512]{1,0:T(8,128)} %collective-permute-done.3.refs_5_), channel_id=1, source_target_pairs={{0,2},{1,3},{2,0},{3,1},{4,6},{5,7},{6,4},{7,5},{8,10},{9,11},{10,... | collective-permute-start | bytes 1622024 | tf_op jit(solution)/shard_map/ppermute | solution.py:254
  58.1 64.2 %copy-start.3 = (f32[264,512]{1,0:T(8,128)}, f32[264,512]{1,0:T(8,128)S(1)}, u32[]{:S(2)}) copy-start(f32[264,512]{1,0:T(8,128)S(1)} %collective-permute-done.5.refs_7_) | copy-start | bytes 1622020
  58.2 21.9 %collective-permute-start.8 = (f32[264,512]{1,0:T(8,128)}, f32[264,512]{1,0:T(8,128)S(1)}, u32[]{:S(2)}, u32[]{:S(2)}) collective-permute-start(f32[264,512]{1,0:T(8,128)} %collective-permute-done.7.refs_10_), channel_id=1, source_target_pairs={{0,2},{1,3},{2,0},{3,1},{4,6},{5,7},{6,4},{7,5},{8,10},{9,11},{10,... | collective-permute-start | bytes 1622024 | tf_op jit(solution)/shard_map/ppermute | solution.py:254
  58.5 33.3 %copy-start.4 = (f32[264,512]{1,0:T(8,128)}, f32[264,512]{1,0:T(8,128)S(1)}, u32[]{:S(2)}) copy-start(f32[264,512]{1,0:T(8,128)S(1)} %collective-permute-done.9.refs_12_) | copy-start | bytes 1622020
  58.5 33.2 %collective-permute-start.12 = (f32[264,512]{1,0:T(8,128)}, f32[264,512]{1,0:T(8,128)S(1)}, u32[]{:S(2)}, u32[]{:S(2)}) collective-permute-start(f32[264,512]{1,0:T(8,128)} %collective-permute-done.11.refs_15_), channel_id=1, source_target_pairs={{0,2},{1,3},{2,0},{3,1},{4,6},{5,7},{6,4},{7,5},{8,10},{9,11},{10,... | collective-permute-start | bytes 1622024 | tf_op jit(solution)/shard_map/ppermute | solution.py:254
  73.0 36.6 %copy-start.5 = (f32[264,512]{1,0:T(8,128)}, f32[264,512]{1,0:T(8,128)S(1)}, u32[]{:S(2)}) copy-start(f32[264,512]{1,0:T(8,128)S(1)} %collective-permute-done.13.refs_17_) | copy-start | bytes 1622020
  73.0 24.6 %collective-permute-start.6 = (f32[136,512]{1,0:T(8,128)S(1)}, f32[136,512]{1,0:T(8,128)S(1)}, u32[]{:S(2)}, u32[]{:S(2)}) collective-permute-start(f32[136,512]{1,0:T(8,128)S(1)} %slice.121), channel_id=1, source_target_pairs={{0,2},{1,3},{2,0},{3,1},{4,6},{5,7},{6,4},{7,5},{8,10},{9,11},{10,... | collective-permute-start | bytes 835592 | tf_op jit(solution)/shard_map/ppermute | solution.py:254
  74.3 35.3 %copy-start.6 = (f32[264,512]{1,0:T(8,128)}, f32[264,512]{1,0:T(8,128)S(1)}, u32[]{:S(2)}) copy-start(f32[264,512]{1,0:T(8,128)S(1)} %collective-permute-done.4.refs_6_) | copy-start | bytes 1622020
  74.3 29.4 %collective-permute-start.10 = (f32[136,512]{1,0:T(8,128)S(1)}, f32[136,512]{1,0:T(8,128)S(1)}, u32[]{:S(2)}, u32[]{:S(2)}) collective-permute-start(f32[136,512]{1,0:T(8,128)S(1)} %slice.126), channel_id=1, source_target_pairs={{0,2},{1,3},{2,0},{3,1},{4,6},{5,7},{6,4},{7,5},{8,10},{9,11},{10,... | collective-permute-start | bytes 835592 | tf_op jit(solution)/shard_map/ppermute | solution.py:254
  80.1 29.5 %copy-start.7 = (f32[264,512]{1,0:T(8,128)}, f32[264,512]{1,0:T(8,128)S(1)}, u32[]{:S(2)}) copy-start(f32[264,512]{1,0:T(8,128)S(1)} %collective-permute-done.8.refs_11_) | copy-start | bytes 1622020
  80.1 29.5 %collective-permute-start.14 = (f32[136,512]{1,0:T(8,128)S(1)}, f32[136,512]{1,0:T(8,128)S(1)}, u32[]{:S(2)}, u32[]{:S(2)}) collective-permute-start(f32[136,512]{1,0:T(8,128)S(1)} %slice.131), channel_id=1, source_target_pairs={{0,2},{1,3},{2,0},{3,1},{4,6},{5,7},{6,4},{7,5},{8,10},{9,11},{10,... | collective-permute-start | bytes 835592 | tf_op jit(solution)/shard_map/ppermute | solution.py:254
  91.7 18.0 %copy-start.8 = (f32[264,512]{1,0:T(8,128)}, f32[264,512]{1,0:T(8,128)S(1)}, u32[]{:S(2)}) copy-start(f32[264,512]{1,0:T(8,128)S(1)} %collective-permute-done.12.refs_16_) | copy-start | bytes 1622020
  91.9 30.4 %collective-permute-start.16 = (f32[128,512]{1,0:T(8,128)S(1)}, f32[128,512]{1,0:T(8,128)}, u32[]{:S(2)}, u32[]{:S(2)}) collective-permute-start(f32[128,512]{1,0:T(8,128)S(1)} %slice.135), channel_id=1, source_target_pairs={{0,4},{1,5},{2,6},{3,7},{4,0},{5,1},{6,2},{7,3},{8,12},{9,13},{10,... | collective-permute-start | bytes 786440 | tf_op jit(solution)/shard_map/ppermute | solution.py:254
  97.6 12.0 %copy-start.10 = (f32[136,512]{1,0:T(8,128)}, f32[136,512]{1,0:T(8,128)S(1)}, u32[]{:S(2)}) copy-start(f32[136,512]{1,0:T(8,128)S(1)} %collective-permute-done.6.refs_9_) | copy-start | bytes 835588
  97.6 24.7 %collective-permute-start.17 = (f32[128,512]{1,0:T(8,128)S(1)}, f32[128,512]{1,0:T(8,128)S(1)}, u32[]{:S(2)}, u32[]{:S(2)}) collective-permute-start(f32[128,512]{1,0:T(8,128)S(1)} %slice.136), channel_id=1, source_target_pairs={{0,4},{1,5},{2,6},{3,7},{4,0},{5,1},{6,2},{7,3},{8,12},{9,13},{10,... | collective-permute-start | bytes 786440 | tf_op jit(solution)/shard_map/ppermute | solution.py:254
  103.7 5.9 %copy-start.11 = (f32[136,512]{1,0:T(8,128)}, f32[136,512]{1,0:T(8,128)S(1)}, u32[]{:S(2)}) copy-start(f32[136,512]{1,0:T(8,128)S(1)} %collective-permute-done.10.refs_14_) | copy-start | bytes 835588
  103.7 18.6 %collective-permute-start.18 = (f32[128,512]{1,0:T(8,128)S(1)}, f32[128,512]{1,0:T(8,128)S(1)}, u32[]{:S(2)}, u32[]{:S(2)}) collective-permute-start(f32[128,512]{1,0:T(8,128)S(1)} %slice.137), channel_id=1, source_target_pairs={{0,4},{1,5},{2,6},{3,7},{4,0},{5,1},{6,2},{7,3},{8,12},{9,13},{10,... | collective-permute-start | bytes 786440 | tf_op jit(solution)/shard_map/ppermute | solution.py:254
  109.6 0.7 copy-start.12
  122.3 0.7 copy-start.13
  122.3 0.8 copy-start.14
  122.3 0.9 copy-start.15
  277.6 75.6 %collective-permute-start.19 = (f32[2,96,64,256]{3,2,1,0:T(8,128)}, f32[2,96,64,256]{3,2,1,0:T(8,128)}, u32[]{:S(2)}, u32[]{:S(2)}) collective-permute-start(f32[2,96,64,256]{3,2,1,0:T(8,128)} %get-tuple-element.13), channel_id=1, source_target_pairs={{0,1},{1,0},{2,3},{3,2},{4,5},{5,4},{6,7},{7,6},{8,9},{9,8},{10,11... | collective-permute-start | bytes 37748744 | tf_op jit(solution)/shard_map/ppermute | solution.py:312
  337.6 7.4 %collective-permute-start.20 = (f32[2,32,64,256]{3,2,1,0:T(8,128)}, f32[2,32,64,256]{3,2,1,0:T(8,128)S(1)}, u32[]{:S(2)}, u32[]{:S(2)}) collective-permute-start(f32[2,32,64,256]{3,2,1,0:T(8,128)} %get-tuple-element.15), channel_id=1, source_target_pairs={{0,1},{1,0},{2,3},{3,2},{4,5},{5,4},{6,7},{7,6},{8,9},{9,8},{10,11... | collective-permute-start | bytes 12582920 | tf_op jit(solution)/shard_map/ppermute | solution.py:312
  345.0 2.1 copy-start

commit v4 on v3

--- a/solution.py
+++ b/solution.py
@@ -3,6 +3,7 @@
 
 import jax
 import jax.numpy as jnp
+import numpy as np
 from jax import lax
 from jax.experimental import pallas as pl
 from jax.experimental.pallas import tpu as pltpu
@@ -122,12 +123,15 @@
 
         lax.fori_loop(0, (stop - begin + depth - 1) // depth, step, 0)
 
-    for k, ref in ((0, own), (2, other)):
-        for m in range(2):
-            v = coef[(k + m) * classes] * acc[tile * classes]
-            for c in range(1, classes):
-                v = v + coef[(k + m) * classes + c] * acc[tile * classes + c]
-            ref[m] = v.reshape(BX, BY, NZ)
+    for m in range(2):
+        even, odd = (
+            functools.reduce(
+                jnp.add, [coef[m * classes + c] * acc[tile * classes + c] for c in range(parity, classes, 2)]
+            )
+            for parity in range(2)
+        )
+        own[m] = (even + odd).reshape(BX, BY, NZ)
+        other[m] = (even - odd).reshape(BX, BY, NZ)
 
 
 def deposit(plan, blocks, coef, first, tiles_x, tiles_y, classes, ch, depth):
@@ -172,61 +176,62 @@
     return group, first, end, code % radix, span
 
 
-def y_kernel(m2, ml, own, other, out):
-    wide = own.shape[2]
-
-    def one(i, _):
-        u = jnp.concatenate([own[0, i] + other[0, i], own[1, i] + other[1, i]], 0)
-        hi, lo = split(u)
-        r = dot(m2[...], jnp.concatenate([hi, lo], 0)) + dot(ml[...], hi)
-        out[0, i] = r[:wide]
-        out[1, i] = r[wide:]
-        return 0
-
-    lax.fori_loop(0, own.shape[1], one, 0, unroll=4)
-
-
-def y_pass(matrix, own, other):
-    hi, lo = matrix
-    both = jnp.concatenate([hi, hi], 1)
-    _, x, y, z = own.shape
-    spec = lambda: pl.BlockSpec((2, BX, y, z), lambda i: (0, i, 0, 0))
-    whole = lambda m: pl.BlockSpec(m.shape, lambda i: (0, 0))
+def transform_kernel(yh, yl, xh, xl, *refs, counts):
+    out, held = refs[-2:]
+    t = pl.program_id(0)
+    wide_y, wide_x = held.shape[2], held.shape[1]
+
+    begin = 0
+    for n, (own, got) in zip(counts, zip(refs[0:-2:2], refs[1:-2:2])):
+
+        @pl.when((t >= begin) & (t < begin + n))
+        def _(own=own, got=got):
+            def one(i, _):
+                u = jnp.concatenate([own[0, i] + got[0, i], own[1, i] + got[1, i]], 0)
+                hi, lo = split(u)
+                r = dot(yh[...], jnp.concatenate([hi, lo], 0)) + dot(yl[...], hi)
+                held[0, t * BX + i] = r[:wide_y]
+                held[1, t * BX + i] = r[wide_y:]
+                return 0
+
+            lax.fori_loop(0, BX, one, 0, unroll=8)
+
+        begin += n
+
+    @pl.when(t >= begin)
+    def _():
+        at = pl.multiple_of((t - begin) * 8, 8)
+        u = jnp.concatenate([jnp.swapaxes(held[c, :, pl.ds(at, 8), :], 0, 1) for c in range(2)], 1)
+        done = []
+        for k in range(8):
+            hi, lo = split(u[k])
+            done.append(dot(xh[...], hi) + dot(xl[...], hi) + dot(xh[...], lo))
+        w = jnp.stack(done)
+        out[0] = jnp.swapaxes(w[:, :wide_x], 0, 1)
+        out[1] = jnp.swapaxes(w[:, wide_x:], 0, 1)
+
+
+def transform(matrix_y, matrix_x, halves):
+    (yh, yl), (xh, xl) = matrix_y, matrix_x
+    yh = jnp.concatenate([yh, yh], 1)
+    _, _, y, z = halves[0][0].shape
+    counts = [own.shape[1] // BX for own, _ in halves]
+    whole = lambda m: pl.BlockSpec(m.shape, lambda t: (0, 0))
+    specs, begin = [], 0
+    for n in counts:
+        spec = pl.BlockSpec((2, BX, y, z), lambda t, n=n, begin=begin: (0, jnp.clip(t - begin, 0, n - 1), 0, 0))
+        specs += [spec, spec]
+        begin += n
+    x = begin * BX
     return pl.pallas_call(
-        y_kernel,
-        grid=(x // BX,),
-        in_specs=[whole(both), whole(lo), spec(), spec()],
-        out_specs=spec(),
-        out_shape=jax.ShapeDtypeStruct(own.shape, jnp.float32),
+        functools.partial(transform_kernel, counts=counts),
+        grid=(begin + y // 8,),
+        in_specs=[whole(yh), whole(yl), whole(xh), whole(xl)] + specs,
+        out_specs=pl.BlockSpec((2, x, 8, z), lambda t: (0, 0, jnp.maximum(t - begin, 0), 0)),
+        out_shape=jax.ShapeDtypeStruct((2, x, y, z), jnp.float32),
+        scratch_shapes=[pltpu.VMEM((2, x, y, z), jnp.float32)],
         compiler_params=pltpu.CompilerParams(vmem_limit_bytes=VMEM),
-        cost_estimate=pl.CostEstimate(flops=24 * x * y * y * z, bytes_accessed=24 * x * y * z, transcendentals=0),
-    )(both, lo, own, other)
-
-
-def x_kernel(mh, ml, *refs):
-    ins, out = refs[:-1], refs[-1]
-    wide = out.shape[1]
-    for k in range(out.shape[2]):
-        hi, lo = split(jnp.concatenate([r[c, :, k, :] for c in range(2) for r in ins], 0))
-        r = dot(mh[...], hi) + dot(ml[...], hi) + dot(mh[...], lo)
-        out[0, :, k, :] = r[:wide]
-        out[1, :, k, :] = r[wide:]
-
-
-def x_pass(matrix, chunks):
-    hi, lo = matrix
-    _, _, y, z = chunks[0].shape
-    x = sum(c.shape[1] for c in chunks)
-    spec = lambda n: pl.BlockSpec((2, n, 8, z), lambda i: (0, 0, i, 0))
-    whole = pl.BlockSpec(hi.shape, lambda i: (0, 0))
-    return pl.pallas_call(
-        x_kernel,
-        grid=(y // 8,),
-        in_specs=[whole, whole] + [spec(c.shape[1]) for c in chunks],
-        out_specs=spec(x),
-        out_shape=jax.ShapeDtypeStruct((2, x, y, z), jnp.float32),
-        compiler_params=pltpu.CompilerParams(vmem_limit_bytes=VMEM),
-    )(hi, lo, *chunks)
+    )(yh, yl, xh, xl, *[v for half in halves for v in half])
 
 
 def dft_matrix(first, step, cells, total, scale):
@@ -245,21 +250,41 @@
     return result
 
 
-def gather_rows(v, tail, n_px, n_py, side):
-    rows = v.shape[0] - tail
-    if n_py != 8:
+def gather_rows(v, tail, n_px, n_py):
+    height = v.shape[0]
+    rows = height - tail
+    line = np.arange(rows, dtype=np.int32)
+    if (n_px, n_py) != (4, 8):
         groups = [list(range(0, n_py, 2)), list(range(1, n_py, 2))]
         got = lax.all_gather(lax.all_gather(v, "px", tiled=True), "py", axis_index_groups=groups, tiled=True)
-        return [got], got.reshape(-1, rows + tail, v.shape[1])[:, rows:]
+        count = n_px * n_py // 2
+        return [got], got.reshape(count, height, v.shape[1])[:, rows:], np.arange(count)[:, None] * height + line
     flip = lambda u, axis, n, m: lax.ppermute(u, axis, [(i, i ^ m) for i in range(n)])
-    half = rows // 2
-    blocks, tails = [], []
-    for u in [v] + [flip(v, "px", n_px, m) for m in range(1, n_px)]:
-        one, two = flip(u, "py", n_py, 2), flip(u, "py", n_py, 4)
-        rest = flip(two[half:], "py", n_py, 2)
-        blocks += [u, one, two, flip(one[:half], "py", n_py, 4), rest]
-        tails += [u[rows:], one[rows:], two[rows:], rest[rows - half :]]
-    return blocks, jnp.stack(tails)
+    across = lambda u, m: flip(u, "py", n_py, m)
+    half, rest = rows // 2, height - rows // 2
+    blocks, tails, places = [], [], []
+
+    def add(u):
+        blocks.append(u)
+        return sum(b.shape[0] for b in blocks[:-1])
+
+    def add_whole(u):
+        places.append(add(u) + line)
+        tails.append(u[rows:])
+
+    columns = [v] + [flip(v, "px", n_px, m) for m in range(1, n_px)]
+    for members in ([0, 1], [2], [3]):
+        one = [across(columns[m], 2) for m in members]
+        two = [across(columns[m], 4) for m in members]
+        upper = across(jnp.concatenate([u[:half] for u in one], 0), 4)
+        lower = across(jnp.concatenate([u[half:] for u in two], 0), 2)
+        for u in [columns[m] for m in members] + one + two:
+            add_whole(u)
+        at_upper, at_lower = add(upper), add(lower)
+        for i in range(len(members)):
+            places.append(np.concatenate([at_upper + i * half + line[:half], at_lower + i * rest + line[: rows - half]]))
+            tails.append(lower[i * rest + rows - half : (i + 1) * rest])
+    return blocks, jnp.stack(tails), np.stack(places)
 
 
 def local(positions, strength, destination, tile_index, particle_count):
@@ -282,10 +307,10 @@
     info = (destination[:, 0] * tiles + tile_index).astype(jnp.float32)
     tail = -(-rows // (4 * width) // 8) * 8
     info = jnp.pad(info, (0, tail * 4 * width - rows)).reshape(tail, 4 * width)
-    blocks, tails = gather_rows(jnp.concatenate([packed, info], 0), tail, n_px, n_py, me_y & 1)
+    blocks, tails, places = gather_rows(jnp.concatenate([packed, info], 0), tail, n_px, n_py)
     info = tails.reshape(tails.shape[0], -1)[:, :rows].astype(jnp.int32)
-    number = jnp.arange(info.shape[0], dtype=jnp.int32)[:, None] * (rows + tail) + jnp.arange(rows, dtype=jnp.int32)
-    radix = 2 * info.shape[0] * (rows + tail)
+    number = jnp.asarray(places, jnp.int32)
+    radix = 2 * sum(b.shape[0] for b in blocks)
 
     pencil, tile = info // tiles, info % tiles
     at_x, at_y = pencil // n_py, pencil % n_py
@@ -298,9 +323,8 @@
     c = jnp.arange(classes, dtype=jnp.int32)
     odd = c & 1
     exponent = jnp.where(low_y % 2 == 1, c, c - odd).astype(jnp.float32) * (2.0 * math.pi / n_py)
-    flip = lambda s: (1 - 2 * (odd * s)).astype(jnp.float32)
-    real, imag = jnp.cos(exponent), -jnp.sin(exponent)
-    coef = jnp.concatenate([real * flip(side), imag * flip(side), real * flip(1 - side), imag * flip(1 - side)])
+    flip = (1 - 2 * (odd * side)).astype(jnp.float32)
+    coef = jnp.concatenate([jnp.cos(exponent) * flip, -jnp.sin(exponent) * flip])
 
     matrix_y = dft_matrix(res_y, n_py, width_y, NY, 1.0 / math.sqrt(NX * NY))
     matrix_x = dft_matrix(res_x, n_px, width_x, NX, 1.0)
@@ -310,7 +334,7 @@
     for first, each in ((0, tiles_x - last), (tiles_x - last, last)):
         own, other = deposit(plan, blocks, coef, first, each, tiles_y, classes, STEP_ROWS, DEPTH)
         halves.append((own, lax.ppermute(other, "py", swap)))
-    return x_pass(matrix_x, [y_pass(matrix_y, own, got) for own, got in halves])
+    return transform(matrix_y, matrix_x, halves)
 
 
 def solution(mesh):

time: 390 us -> 378 us (0.969)
  Pallas kernels: 253 us -> 240 us
    pallas_call x3 -> x1, Pallas kernels: 41.6 us -> 30.8 us  [transform(): pl.pallas_call(functools.partial(transform_kernel, counts=counts), grid=(...]
    ppermute x19 -> x17, waiting for transfers between devices: 80.7 us -> 83.1 us  [gather_rows(): lax.ppermute(u, axis, [(i, i ^ m) for i in range(n)])]
    unnamed x64 -> x63, local copies, waits for them, and re-layouts: 8 us -> 6.28 us
    ppermute x19 -> x17, starting transfers between devices: 19.8 us -> 18.8 us  [gather_rows(): lax.ppermute(u, axis, [(i, i ^ m) for i in range(n)])]
  transfers between devices with their start and end apart: 21 -> 19, of which waited for: 11 -> 11; matrix products, arithmetic and copies ran while one was open for 5% -> 5% of each run, Pallas kernels for 16% -> 16%
where the time goes in v4:
time: 378 us; the launch traced here: 377 us
  Pallas kernels  240 us (63%)
  waiting for transfers between devices  87.8 us (23%)
  starting transfers between devices  23.7 us (6%)
  other arithmetic  16.7 us (4%)
  local copies, waits for them, and re-layouts  8.77 us (2%)
    pallas_call x2, Pallas kernels, deposit(): pl.pallas_call(functools.partial(deposit_kernel, classes=classes, ch=ch,...  209 us
    ppermute x17, waiting for transfers between devices, gather_rows(): lax.ppermute(u, axis, [(i, i ^ m) for i in range(n)])  83.1 us
    pallas_call x1, Pallas kernels, transform(): pl.pallas_call(functools.partial(transform_kernel, counts=counts), grid=(...  30.8 us
    ppermute x17, starting transfers between devices, gather_rows(): lax.ppermute(u, axis, [(i, i ^ m) for i in range(n)])  18.8 us
  transfers between devices with their start and end apart: 19, of which 11 were waited for; matrix products, arithmetic and copies ran while one was open for 5% of the time, Pallas kernels for 16%

profile of v4, /device:TPU:17, one launch (start us, length us, event | category | flops | bytes accessed | tf_op | source)
XLA Modules:
  0.0 376.9 jit_solution(2227380894715951016)
XLA Ops:
  0.0 0.7 broadcast_multiply_fusion
  0.7 0.7 add_convert_fusion
  1.4 1.2 copy.10
  2.7 1.0 fusion.2
  4.0 3.2 collective-permute-start.6
  7.2 1.2 collective-permute-start.3
  8.5 1.2 collective-permute-start.1
  9.7 0.6 pad_maximum_fusion.4.coef
  10.4 29.9 %collective-permute-done.10.refs_13_ = f32[264,512]{1,0:T(8,128)} collective-permute-done((f32[264,512]{1,0:T(8,128)S(1)}, f32[264,512]{1,0:T(8,128)}, u32[]{:S(2)}, u32[]{:S(2)}) %collective-permute-start.10) | collective-permute-done | bytes 540704 | tf_op jit(solution)/shard_map/ppermute | solution.py:262
  40.3 0.7 slice_bitcast_fusion.3
  41.0 1.2 collective-permute-start.12
  42.2 7.7 %collective-permute-done.6.refs_8_ = f32[264,512]{1,0:T(8,128)S(1)} collective-permute-done((f32[264,512]{1,0:T(8,128)S(1)}, f32[264,512]{1,0:T(8,128)S(1)}, u32[]{:S(2)}, u32[]{:S(2)}) %collective-permute-start.6) | collective-permute-done | bytes 540704 | tf_op jit(solution)/shard_map/ppermute | solution.py:262
  49.9 1.2 collective-permute-start.11
  51.1 1.3 collective-permute-start.8
  52.7 0.7 slice_bitcast_fusion.13
  53.6 1.1 slice.134
  55.0 1.2 collective-permute-start.2
  56.2 6.3 %collective-permute-done.11.refs_14_ = f32[264,512]{1,0:T(8,128)S(1)} collective-permute-done((f32[264,512]{1,0:T(8,128)}, f32[264,512]{1,0:T(8,128)S(1)}, u32[]{:S(2)}, u32[]{:S(2)}) %collective-permute-start.11) | collective-permute-done | bytes 540704 | tf_op jit(solution)/shard_map/ppermute | solution.py:262
  62.5 1.2 collective-permute-start.13
  63.8 1.8 collective-permute-done.8.refs_10_
  65.6 1.2 collective-permute-start.16
  66.8 7.3 %collective-permute-done.7.refs_9_ = f32[264,512]{1,0:T(8,128)S(1)} collective-permute-done((f32[264,512]{1,0:T(8,128)S(1)}, f32[264,512]{1,0:T(8,128)S(1)}, u32[]{:S(2)}, u32[]{:S(2)}) %collective-permute-start.7) | collective-permute-done | bytes 540704 | tf_op jit(solution)/shard_map/ppermute | solution.py:262
  74.1 1.2 collective-permute-start.9
  75.4 1.8 collective-permute-done.4.refs_5_
  77.1 1.2 collective-permute-start.15
  78.5 7.2 %collective-permute-done.2.refs_3_ = f32[264,512]{1,0:T(8,128)S(1)} collective-permute-done((f32[264,512]{1,0:T(8,128)S(1)}, f32[264,512]{1,0:T(8,128)S(1)}, u32[]{:S(2)}, u32[]{:S(2)}) %collective-permute-start.2) | collective-permute-done | bytes 540704 | tf_op jit(solution)/shard_map/ppermute | solution.py:262
  85.7 1.2 collective-permute-start.5
  87.2 4.5 %collective-permute-done.13.refs_17_ = f32[136,512]{1,0:T(8,128)S(1)} collective-permute-done((f32[136,512]{1,0:T(8,128)S(1)}, f32[136,512]{1,0:T(8,128)S(1)}, u32[]{:S(2)}, u32[]{:S(2)}) %collective-permute-start.13) | collective-permute-done | bytes 278560 | tf_op jit(solution)/shard_map/ppermute | solution.py:262
  91.7 1.2 collective-permute-start.14
  92.9 4.7 %collective-permute-done.9.refs_12_ = f32[136,512]{1,0:T(8,128)S(1)} collective-permute-done((f32[136,512]{1,0:T(8,128)S(1)}, f32[136,512]{1,0:T(8,128)S(1)}, u32[]{:S(2)}, u32[]{:S(2)}) %collective-permute-start.9) | collective-permute-done | bytes 278560 | tf_op jit(solution)/shard_map/ppermute | solution.py:262
  97.7 11.9 %collective-permute-done.5.refs_7_ = f32[272,512]{1,0:T(8,128)S(1)} collective-permute-done((f32[272,512]{1,0:T(8,128)S(1)}, f32[272,512]{1,0:T(8,128)S(1)}, u32[]{:S(2)}, u32[]{:S(2)}) %collective-permute-start.5) | collective-permute-done | bytes 557088 | tf_op jit(solution)/shard_map/ppermute | solution.py:262
  109.7 0.7 copy-done.10
  110.9 5.8 %sort.14 = (s32[4096]{0:T(1024)S(1)}, s32[4096]{0:T(1024)}) sort(s32[4096]{0:T(1024)S(1)} %bitcast.83, s32[4096]{0:T(1024)S(1)} %iota.57), dimensions={0}, to_apply=%region_0.1 | sort | flops 49152 | bytes 65536 | tf_op jit(solution)/shard_map/sort | solution.py:321
  116.7 0.6 convert_reduce_fusion
  117.6 0.6 slice.109
  118.2 2.3 select_reduce_fusion
  120.5 1.3 pad_add_fusion.span
  121.8 0.6 add_select_fusion.2.order
  122.4 0.7 copy-done.15
  123.1 149.9 %shard_map.64 = (f32[2,96,64,256]{3,2,1,0:T(8,128)}, f32[2,96,64,256]{3,2,1,0:T(8,128)}) custom-call(s32[2304]{0:T(1024)} %get-tuple-element.18.groups_of, s32[2304]{0:T(1024)} %get-tuple-element.17.firsts, s32[2304]{0:T(1024)} %get-tuple-element.16.ends, s32[4096]{0:T(1024)} %add_select_fusion.2.order, s32[9]{0:T(128)} %pad_add_fusion.span, ...), custom_call_target="tpu_custom_call" | custom-call | flops 79725330432 | bytes 8650752 | tf_op jit(solution)/shard_map/pallas_call | solution.py:143
  273.1 4.9 %collective-permute-start.17 = (f32[2,96,64,256]{3,2,1,0:T(8,128)}, f32[2,96,64,256]{3,2,1,0:T(8,128)}, u32[]{:S(2)}, u32[]{:S(2)}) collective-permute-start(f32[2,96,64,256]{3,2,1,0:T(8,128)} %get-tuple-element.13), channel_id=1, source_target_pairs={{0,1},{1,0},{2,3},{3,2},{4,5},{5,4},{6,7},{7,6},{8,9},{9,8},{10,11... | collective-permute-start | bytes 37748744 | tf_op jit(solution)/shard_map/ppermute | solution.py:336
  277.9 58.8 %shard_map.65 = (f32[2,32,64,256]{3,2,1,0:T(8,128)}, f32[2,32,64,256]{3,2,1,0:T(8,128)}) custom-call(s32[2304]{0:T(1024)} %get-tuple-element.18.groups_of, s32[2304]{0:T(1024)} %get-tuple-element.17.firsts, s32[2304]{0:T(1024)} %get-tuple-element.16.ends, s32[4096]{0:T(1024)} %add_select_fusion.2.order, s32[9]{0:T(128)} %pad_add_fusion.span, ...), custom_call_target="tpu_custom_call" | custom-call | flops 26575110144 | bytes 8650752 | tf_op jit(solution)/shard_map/pallas_call | solution.py:143
  337.1 0.7 fusion.3
  337.8 0.6 pad_maximum_fusion.3.yh
  338.7 0.7 fusion.1
  339.5 4.7 %collective-permute-done.18.refs_3_ = f32[2,32,64,256]{3,2,1,0:T(8,128)S(1)} collective-permute-done((f32[2,32,64,256]{3,2,1,0:T(8,128)}, f32[2,32,64,256]{3,2,1,0:T(8,128)S(1)}, u32[]{:S(2)}, u32[]{:S(2)}) %collective-permute-start.18) | collective-permute-done | bytes 4194336 | tf_op jit(solution)/shard_map/ppermute | solution.py:336
  344.2 1.9 copy-done
  346.1 30.8 %shard_map.66 = f32[2,128,64,256]{3,2,1,0:T(8,128)} custom-call(bf16[128,256]{1,0:T(8,128)(2,1)} %pad_maximum_fusion.3.yh, bf16[128,128]{1,0:T(8,128)(2,1)} %get-tuple-element.23.yl, bf16[256,256]{1,0:T(8,128)(2,1)} %get-tuple-element.22.xh, bf16[256,256]{1,0:T(8,128)(2,1)} %get-tuple-element.21.xl, f32[2,96,64,256]{3,2,1,0:T(8,128)} %get-tuple-element.12.refs_0_, ...), custom_call_target="tpu_custom_call" | custom-call | tf_op jit(solution)/shard_map/pallas_call | solution.py:226
  (96 shorter events, 3.1 us)
Async XLA Ops:
  3.8 74.7 %copy-start.1 = (f32[264,512]{1,0:T(8,128)}, f32[264,512]{1,0:T(8,128)S(1)}, u32[]{:S(2)}) copy-start(f32[264,512]{1,0:T(8,128)S(1)} %pad_maximum_fusion.1.refs_0_) | copy-start | bytes 1622020
  3.8 36.5 %collective-permute-start.10 = (f32[264,512]{1,0:T(8,128)S(1)}, f32[264,512]{1,0:T(8,128)}, u32[]{:S(2)}, u32[]{:S(2)}) collective-permute-start(f32[264,512]{1,0:T(8,128)S(1)} %pad_maximum_fusion.1.refs_0_), channel_id=1, source_target_pairs={{0,24},{8,16},{16,8},{24,0},{1,25},{9,17},{17,9},{25,1},{2,26},{10... | collective-permute-start | bytes 1622024 | tf_op jit(solution)/shard_map/ppermute | solution.py:262
  4.0 45.9 %collective-permute-start.6 = (f32[264,512]{1,0:T(8,128)S(1)}, f32[264,512]{1,0:T(8,128)S(1)}, u32[]{:S(2)}, u32[]{:S(2)}) collective-permute-start(f32[264,512]{1,0:T(8,128)S(1)} %pad_maximum_fusion.1.refs_0_), channel_id=1, source_target_pairs={{0,16},{8,24},{16,0},{24,8},{1,17},{9,25},{17,1},{25,9},{2,18},{10... | collective-permute-start | bytes 1622024 | tf_op jit(solution)/shard_map/ppermute | solution.py:262
  7.2 43.9 %collective-permute-start.3 = (f32[264,512]{1,0:T(8,128)S(1)}, f32[264,512]{1,0:T(8,128)S(1)}, u32[]{:S(2)}, u32[]{:S(2)}) collective-permute-start(f32[264,512]{1,0:T(8,128)S(1)} %pad_maximum_fusion.1.refs_0_), channel_id=1, source_target_pairs={{0,4},{1,5},{2,6},{3,7},{4,0},{5,1},{6,2},{7,3},{8,12},{9,13},{10,... | collective-permute-start | bytes 1622024 | tf_op jit(solution)/shard_map/ppermute | solution.py:262
  8.5 44.0 %collective-permute-start.1 = (f32[264,512]{1,0:T(8,128)S(1)}, f32[264,512]{1,0:T(8,128)}, u32[]{:S(2)}, u32[]{:S(2)}) collective-permute-start(f32[264,512]{1,0:T(8,128)S(1)} %pad_maximum_fusion.1.refs_0_), channel_id=1, source_target_pairs={{0,2},{1,3},{2,0},{3,1},{4,6},{5,7},{6,4},{7,5},{8,10},{9,11},{10,... | collective-permute-start | bytes 1622024 | tf_op jit(solution)/shard_map/ppermute | solution.py:262
  9.7 43.8 %collective-permute-start = (f32[264,512]{1,0:T(8,128)S(1)}, f32[264,512]{1,0:T(8,128)S(1)}, u32[]{:S(2)}, u32[]{:S(2)}) collective-permute-start(f32[264,512]{1,0:T(8,128)S(1)} %pad_maximum_fusion.1.refs_0_), channel_id=1, source_target_pairs={{0,8},{8,0},{16,24},{24,16},{1,9},{9,1},{17,25},{25,17},{2,10},{10... | collective-permute-start | bytes 1622024 | tf_op jit(solution)/shard_map/ppermute | solution.py:262
  41.0 14.0 %collective-permute-start.12 = (f32[264,512]{1,0:T(8,128)}, f32[264,512]{1,0:T(8,128)S(1)}, u32[]{:S(2)}, u32[]{:S(2)}) collective-permute-start(f32[264,512]{1,0:T(8,128)} %collective-permute-done.10.refs_13_), channel_id=1, source_target_pairs={{0,4},{1,5},{2,6},{3,7},{4,0},{5,1},{6,2},{7,3},{8,12},{9,13},{10,... | collective-permute-start | bytes 1622024 | tf_op jit(solution)/shard_map/ppermute | solution.py:262
  49.9 72.5 %copy-start.13 = (f32[264,512]{1,0:T(8,128)}, f32[264,512]{1,0:T(8,128)S(1)}, u32[]{:S(2)}) copy-start(f32[264,512]{1,0:T(8,128)S(1)} %collective-permute-done.6.refs_8_) | copy-start | bytes 1622020
  49.9 12.6 %collective-permute-start.11 = (f32[264,512]{1,0:T(8,128)}, f32[264,512]{1,0:T(8,128)S(1)}, u32[]{:S(2)}, u32[]{:S(2)}) collective-permute-start(f32[264,512]{1,0:T(8,128)} %collective-permute-done.10.refs_13_), channel_id=1, source_target_pairs={{0,2},{1,3},{2,0},{3,1},{4,6},{5,7},{6,4},{7,5},{8,10},{9,11},{10,... | collective-permute-start | bytes 1622024 | tf_op jit(solution)/shard_map/ppermute | solution.py:262
  51.1 27.3 %copy-start.2 = (f32[264,512]{1,0:T(8,128)}, f32[264,512]{1,0:T(8,128)S(1)}, u32[]{:S(2)}) copy-start(f32[264,512]{1,0:T(8,128)S(1)} %collective-permute-done.3.refs_4_) | copy-start | bytes 1622020
  51.1 14.4 %collective-permute-start.8 = (f32[264,512]{1,0:T(8,128)S(1)}, f32[264,512]{1,0:T(8,128)S(1)}, u32[]{:S(2)}, u32[]{:S(2)}) collective-permute-start(f32[264,512]{1,0:T(8,128)S(1)} %collective-permute-done.6.refs_8_), channel_id=1, source_target_pairs={{0,4},{1,5},{2,6},{3,7},{4,0},{5,1},{6,2},{7,3},{8,12},{9,13},{10,... | collective-permute-start | bytes 1622024 | tf_op jit(solution)/shard_map/ppermute | solution.py:262
  52.4 21.7 %collective-permute-start.7 = (f32[264,512]{1,0:T(8,128)S(1)}, f32[264,512]{1,0:T(8,128)S(1)}, u32[]{:S(2)}, u32[]{:S(2)}) collective-permute-start(f32[264,512]{1,0:T(8,128)S(1)} %collective-permute-done.6.refs_8_), channel_id=1, source_target_pairs={{0,2},{1,3},{2,0},{3,1},{4,6},{5,7},{6,4},{7,5},{8,10},{9,11},{10,... | collective-permute-start | bytes 1622024 | tf_op jit(solution)/shard_map/ppermute | solution.py:262
  53.5 24.9 %copy-start.14 = (f32[264,512]{1,0:T(8,128)}, f32[264,512]{1,0:T(8,128)S(1)}, u32[]{:S(2)}) copy-start(f32[264,512]{1,0:T(8,128)S(1)} %collective-permute-done.refs_1_) | copy-start | bytes 1622020
  54.7 22.4 %collective-permute-start.4 = (f32[264,512]{1,0:T(8,128)S(1)}, f32[264,512]{1,0:T(8,128)S(1)}, u32[]{:S(2)}, u32[]{:S(2)}) collective-permute-start(f32[264,512]{1,0:T(8,128)S(1)} %collective-permute-done.refs_1_), channel_id=1, source_target_pairs={{0,4},{1,5},{2,6},{3,7},{4,0},{5,1},{6,2},{7,3},{8,12},{9,13},{10,... | collective-permute-start | bytes 1622024 | tf_op jit(solution)/shard_map/ppermute | solution.py:262
  55.0 32.0 %copy-start.3 = (f32[264,512]{1,0:T(8,128)}, f32[264,512]{1,0:T(8,128)S(1)}, u32[]{:S(2)}) copy-start(f32[264,512]{1,0:T(8,128)S(1)} %collective-permute-done.12.refs_15_) | copy-start | bytes 1622020
  55.0 30.7 %collective-permute-start.2 = (f32[264,512]{1,0:T(8,128)S(1)}, f32[264,512]{1,0:T(8,128)S(1)}, u32[]{:S(2)}, u32[]{:S(2)}) collective-permute-start(f32[264,512]{1,0:T(8,128)S(1)} %collective-permute-done.refs_1_), channel_id=1, source_target_pairs={{0,2},{1,3},{2,0},{3,1},{4,6},{5,7},{6,4},{7,5},{8,10},{9,11},{10,... | collective-permute-start | bytes 1622024 | tf_op jit(solution)/shard_map/ppermute | solution.py:262
  62.5 15.8 %copy-start.6 = (f32[264,512]{1,0:T(8,128)}, f32[264,512]{1,0:T(8,128)S(1)}, u32[]{:S(2)}) copy-start(f32[264,512]{1,0:T(8,128)S(1)} %collective-permute-done.11.refs_14_) | copy-start | bytes 1622020
  62.5 29.1 %collective-permute-start.13 = (f32[136,512]{1,0:T(8,128)S(1)}, f32[136,512]{1,0:T(8,128)S(1)}, u32[]{:S(2)}, u32[]{:S(2)}) collective-permute-start(f32[136,512]{1,0:T(8,128)S(1)} %slice.131), channel_id=1, source_target_pairs={{0,2},{1,3},{2,0},{3,1},{4,6},{5,7},{6,4},{7,5},{8,10},{9,11},{10,... | collective-permute-start | bytes 835592 | tf_op jit(solution)/shard_map/ppermute | solution.py:262
  65.6 27.4 %copy-start.4 = (f32[264,512]{1,0:T(8,128)}, f32[264,512]{1,0:T(8,128)S(1)}, u32[]{:S(2)}) copy-start(f32[264,512]{1,0:T(8,128)S(1)} %collective-permute-done.8.refs_10_) | copy-start | bytes 1622020
  65.6 56.8 %collective-permute-start.16 = (f32[128,512]{1,0:T(8,128)S(1)}, f32[128,512]{1,0:T(8,128)S(1)}, u32[]{:S(2)}, u32[]{:S(2)}) collective-permute-start(f32[128,512]{1,0:T(8,128)S(1)} %slice.137), channel_id=1, source_target_pairs={{0,4},{1,5},{2,6},{3,7},{4,0},{5,1},{6,2},{7,3},{8,12},{9,13},{10,... | collective-permute-start | bytes 786440 | tf_op jit(solution)/shard_map/ppermute | solution.py:262
  66.8 44.0 %copy-start.9 = (s32[16,256]{1,0:T(8,128)S(1)}, s32[16,256]{1,0:T(8,128)}, u32[]{:S(2)}) copy-start(s32[16,256]{1,0:T(8,128)} %constant.162) | copy-start | bytes 49156
  74.1 35.5 %copy-start.7 = (f32[264,512]{1,0:T(8,128)}, f32[264,512]{1,0:T(8,128)S(1)}, u32[]{:S(2)}) copy-start(f32[264,512]{1,0:T(8,128)S(1)} %collective-permute-done.7.refs_9_) | copy-start | bytes 1622020
  74.1 23.5 %collective-permute-start.9 = (f32[136,512]{1,0:T(8,128)S(1)}, f32[136,512]{1,0:T(8,128)S(1)}, u32[]{:S(2)}, u32[]{:S(2)}) collective-permute-start(f32[136,512]{1,0:T(8,128)S(1)} %slice.126), channel_id=1, source_target_pairs={{0,2},{1,3},{2,0},{3,1},{4,6},{5,7},{6,4},{7,5},{8,10},{9,11},{10,... | collective-permute-start | bytes 835592 | tf_op jit(solution)/shard_map/ppermute | solution.py:262
  77.1 32.5 %copy-start.5 = (f32[264,512]{1,0:T(8,128)}, f32[264,512]{1,0:T(8,128)S(1)}, u32[]{:S(2)}) copy-start(f32[264,512]{1,0:T(8,128)S(1)} %collective-permute-done.4.refs_5_) | copy-start | bytes 1622020
  77.1 45.3 %collective-permute-start.15 = (f32[128,512]{1,0:T(8,128)S(1)}, f32[128,512]{1,0:T(8,128)}, u32[]{:S(2)}, u32[]{:S(2)}) collective-permute-start(f32[128,512]{1,0:T(8,128)S(1)} %slice.136), channel_id=1, source_target_pairs={{0,4},{1,5},{2,6},{3,7},{4,0},{5,1},{6,2},{7,3},{8,12},{9,13},{10,... | collective-permute-start | bytes 786440 | tf_op jit(solution)/shard_map/ppermute | solution.py:262
  85.7 24.0 %copy-start.8 = (f32[264,512]{1,0:T(8,128)}, f32[264,512]{1,0:T(8,128)S(1)}, u32[]{:S(2)}) copy-start(f32[264,512]{1,0:T(8,128)S(1)} %collective-permute-done.2.refs_3_) | copy-start | bytes 1622020
  85.7 23.9 %collective-permute-start.5 = (f32[272,512]{1,0:T(8,128)S(1)}, f32[272,512]{1,0:T(8,128)S(1)}, u32[]{:S(2)}, u32[]{:S(2)}) collective-permute-start(f32[272,512]{1,0:T(8,128)S(1)} %pad_maximum_fusion), channel_id=1, source_target_pairs={{0,2},{1,3},{2,0},{3,1},{4,6},{5,7},{6,4},{7,5},{8,10},{9,11},{10,... | collective-permute-start | bytes 1671176 | tf_op jit(solution)/shard_map/ppermute | solution.py:262
  91.7 30.8 %copy-start.11 = (f32[136,512]{1,0:T(8,128)}, f32[136,512]{1,0:T(8,128)S(1)}, u32[]{:S(2)}) copy-start(f32[136,512]{1,0:T(8,128)S(1)} %collective-permute-done.13.refs_17_) | copy-start | bytes 835588
  91.7 30.7 %collective-permute-start.14 = (f32[256,512]{1,0:T(8,128)S(1)}, f32[256,512]{1,0:T(8,128)}, u32[]{:S(2)}, u32[]{:S(2)}) collective-permute-start(f32[256,512]{1,0:T(8,128)S(1)} %pad_maximum_fusion.2), channel_id=1, source_target_pairs={{0,4},{1,5},{2,6},{3,7},{4,0},{5,1},{6,2},{7,3},{8,12},{9,13},{10,... | collective-permute-start | bytes 1572872 | tf_op jit(solution)/shard_map/ppermute | solution.py:262
  97.6 12.0 %copy-start.12 = (f32[136,512]{1,0:T(8,128)}, f32[136,512]{1,0:T(8,128)S(1)}, u32[]{:S(2)}) copy-start(f32[136,512]{1,0:T(8,128)S(1)} %collective-permute-done.9.refs_12_) | copy-start | bytes 835588
  109.6 0.8 copy-start.10
  122.4 0.7 copy-start.15
  273.1 71.1 %collective-permute-start.17 = (f32[2,96,64,256]{3,2,1,0:T(8,128)}, f32[2,96,64,256]{3,2,1,0:T(8,128)}, u32[]{:S(2)}, u32[]{:S(2)}) collective-permute-start(f32[2,96,64,256]{3,2,1,0:T(8,128)} %get-tuple-element.13), channel_id=1, source_target_pairs={{0,1},{1,0},{2,3},{3,2},{4,5},{5,4},{6,7},{7,6},{8,9},{9,8},{10,11... | collective-permute-start | bytes 37748744 | tf_op jit(solution)/shard_map/ppermute | solution.py:336
  336.7 7.4 %collective-permute-start.18 = (f32[2,32,64,256]{3,2,1,0:T(8,128)}, f32[2,32,64,256]{3,2,1,0:T(8,128)S(1)}, u32[]{:S(2)}, u32[]{:S(2)}) collective-permute-start(f32[2,32,64,256]{3,2,1,0:T(8,128)} %get-tuple-element.15), channel_id=1, source_target_pairs={{0,1},{1,0},{2,3},{3,2},{4,5},{5,4},{6,7},{7,6},{8,9},{9,8},{10,11... | collective-permute-start | bytes 12582920 | tf_op jit(solution)/shard_map/ppermute | solution.py:336
  344.2 1.9 copy-start

commit v5 on v4

--- a/solution.py
+++ b/solution.py
@@ -273,7 +273,7 @@
         tails.append(u[rows:])
 
     columns = [v] + [flip(v, "px", n_px, m) for m in range(1, n_px)]
-    for members in ([0, 1], [2], [3]):
+    for members in ([0], [1], [2], [3]):
         one = [across(columns[m], 2) for m in members]
         two = [across(columns[m], 4) for m in members]
         upper = across(jnp.concatenate([u[:half] for u in one], 0), 4)
@@ -329,7 +329,7 @@
     matrix_y = dft_matrix(res_y, n_py, width_y, NY, 1.0 / math.sqrt(NX * NY))
     matrix_x = dft_matrix(res_x, n_px, width_x, NX, 1.0)
     swap = [(i, i ^ 1) for i in range(n_py)]
-    last = max(1, tiles_x // 4)
+    last = max(1, tiles_x // 8)
     halves = []
     for first, each in ((0, tiles_x - last), (tiles_x - last, last)):
         own, other = deposit(plan, blocks, coef, first, each, tiles_y, classes, STEP_ROWS, DEPTH)

time: 378 us -> 368 us (0.974)
  starting transfers between devices: 23.7 us -> 16.7 us
    ppermute x17 -> x19, starting transfers between devices: 18.8 us -> 14.2 us  [gather_rows(): lax.ppermute(u, axis, [(i, i ^ m) for i in range(n)])]
    ppermute x17 -> x19, waiting for transfers between devices: 83.1 us -> 83.8 us  [gather_rows(): lax.ppermute(u, axis, [(i, i ^ m) for i in range(n)])]
  transfers between devices with their start and end apart: 19 -> 21, of which waited for: 11 -> 12; matrix products, arithmetic and copies ran while one was open for 5% -> 5% of each run, Pallas kernels for 16% -> 9%
where the time goes in v5:
time: 368 us; the launch traced here: 364 us
  Pallas kernels  238 us (65%)
  waiting for transfers between devices  85.5 us (23%)
  starting transfers between devices  16.7 us (5%)
  other arithmetic  16.6 us (5%)
  local copies, waits for them, and re-layouts  6.36 us (2%)
    pallas_call x2, Pallas kernels, deposit(): pl.pallas_call(functools.partial(deposit_kernel, classes=classes, ch=ch,...  208 us
    ppermute x19, waiting for transfers between devices, gather_rows(): lax.ppermute(u, axis, [(i, i ^ m) for i in range(n)])  83.8 us
    pallas_call x1, Pallas kernels, transform(): pl.pallas_call(functools.partial(transform_kernel, counts=counts), grid=(...  30.1 us
    ppermute x19, starting transfers between devices, gather_rows(): lax.ppermute(u, axis, [(i, i ^ m) for i in range(n)])  14.2 us
  transfers between devices with their start and end apart: 21, of which 12 were waited for; matrix products, arithmetic and copies ran while one was open for 5% of the time, Pallas kernels for 9%

profile of v5, /device:TPU:17, one launch (start us, length us, event | category | flops | bytes accessed | tf_op | source)
XLA Modules:
  0.0 364.0 jit_solution(13458619531308943328)
XLA Ops:
  0.0 0.7 broadcast_multiply_fusion
  0.7 0.7 add_convert_fusion
  1.4 1.2 copy.10
  2.7 1.0 fusion.2
  3.8 1.3 collective-permute-start.1
  5.3 3.2 collective-permute-start.7
  8.5 1.2 collective-permute-start
  9.7 0.6 pad_maximum_fusion.2.coef
  10.3 6.7 %collective-permute-done.1.refs_2_ = f32[264,512]{1,0:T(8,128)S(1)} collective-permute-done((f32[264,512]{1,0:T(8,128)S(1)}, f32[264,512]{1,0:T(8,128)S(1)}, u32[]{:S(2)}, u32[]{:S(2)}) %collective-permute-start.1) | collective-permute-done | bytes 540704 | tf_op jit(solution)/shard_map/ppermute | solution.py:262
  17.0 1.3 collective-permute-start.2
  18.3 22.9 %collective-permute-done.11.refs_15_ = f32[264,512]{1,0:T(8,128)S(1)} collective-permute-done((f32[264,512]{1,0:T(8,128)S(1)}, f32[264,512]{1,0:T(8,128)S(1)}, u32[]{:S(2)}, u32[]{:S(2)}) %collective-permute-start.11) | collective-permute-done | bytes 540704 | tf_op jit(solution)/shard_map/ppermute | solution.py:262
  41.4 9.7 %collective-permute-done.7.refs_10_ = f32[264,512]{1,0:T(8,128)} collective-permute-done((f32[264,512]{1,0:T(8,128)S(1)}, f32[264,512]{1,0:T(8,128)}, u32[]{:S(2)}, u32[]{:S(2)}) %collective-permute-start.7) | collective-permute-done | bytes 540704 | tf_op jit(solution)/shard_map/ppermute | solution.py:262
  51.1 1.2 collective-permute-start.12
  52.3 0.7 slice_bitcast_fusion.7
  53.0 0.7 slice_bitcast_fusion.11
  54.0 0.3 collective-permute-start.15
  54.2 1.2 collective-permute-start.9
  55.5 0.3 collective-permute-start.8
  55.8 0.3 collective-permute-start.5
  56.1 7.5 %collective-permute-done.12.refs_16_ = f32[264,512]{1,0:T(8,128)S(1)} collective-permute-done((f32[264,512]{1,0:T(8,128)S(1)}, f32[264,512]{1,0:T(8,128)S(1)}, u32[]{:S(2)}, u32[]{:S(2)}) %collective-permute-start.12) | collective-permute-done | bytes 540704 | tf_op jit(solution)/shard_map/ppermute | solution.py:262
  63.6 1.2 collective-permute-start.4
  64.8 6.9 %collective-permute-done.9.refs_12_ = f32[264,512]{1,0:T(8,128)S(1)} collective-permute-done((f32[264,512]{1,0:T(8,128)}, f32[264,512]{1,0:T(8,128)S(1)}, u32[]{:S(2)}, u32[]{:S(2)}) %collective-permute-start.9) | collective-permute-done | bytes 540704 | tf_op jit(solution)/shard_map/ppermute | solution.py:262
  71.7 0.3 collective-permute-start.14
  72.0 3.0 collective-permute-done.8.refs_11_
  75.3 8.0 %collective-permute-done.5.refs_7_ = f32[264,512]{1,0:T(8,128)S(1)} collective-permute-done((f32[264,512]{1,0:T(8,128)}, f32[264,512]{1,0:T(8,128)S(1)}, u32[]{:S(2)}, u32[]{:S(2)}) %collective-permute-start.5) | collective-permute-done | bytes 540704 | tf_op jit(solution)/shard_map/ppermute | solution.py:262
  83.6 3.1 collective-permute-done.4.refs_6_
  87.1 5.6 %collective-permute-done.14.refs_19_ = f32[136,512]{1,0:T(8,128)S(1)} collective-permute-done((f32[136,512]{1,0:T(8,128)S(1)}, f32[136,512]{1,0:T(8,128)S(1)}, u32[]{:S(2)}, u32[]{:S(2)}) %collective-permute-start.14) | collective-permute-done | bytes 278560 | tf_op jit(solution)/shard_map/ppermute | solution.py:262
  92.7 1.1 collective-permute-start.6
  93.9 4.7 %collective-permute-done.10.refs_14_ = f32[136,512]{1,0:T(8,128)S(1)} collective-permute-done((f32[136,512]{1,0:T(8,128)S(1)}, f32[136,512]{1,0:T(8,128)S(1)}, u32[]{:S(2)}, u32[]{:S(2)}) %collective-permute-start.10) | collective-permute-done | bytes 278560 | tf_op jit(solution)/shard_map/ppermute | solution.py:262
  98.9 5.7 %collective-permute-done.6.refs_9_ = f32[136,512]{1,0:T(8,128)S(1)} collective-permute-done((f32[136,512]{1,0:T(8,128)S(1)}, f32[136,512]{1,0:T(8,128)S(1)}, u32[]{:S(2)}, u32[]{:S(2)}) %collective-permute-start.6) | collective-permute-done | bytes 278560 | tf_op jit(solution)/shard_map/ppermute | solution.py:262
  104.7 0.4 stack.66
  105.2 5.8 %sort.14 = (s32[4096]{0:T(1024)S(1)}, s32[4096]{0:T(1024)}) sort(s32[4096]{0:T(1024)S(1)} %bitcast.83, s32[4096]{0:T(1024)S(1)} %iota.57), dimensions={0}, to_apply=%region_0.1 | sort | flops 49152 | bytes 65536 | tf_op jit(solution)/shard_map/sort | solution.py:321
  110.9 0.6 convert_reduce_fusion
  111.9 0.6 slice.109
  112.5 2.3 select_reduce_fusion
  114.8 1.3 pad_add_fusion.span
  116.1 0.6 add_select_fusion.2.order
  116.7 0.7 copy-done.16
  117.4 176.0 %shard_map.64 = (f32[2,112,64,256]{3,2,1,0:T(8,128)}, f32[2,112,64,256]{3,2,1,0:T(8,128)}) custom-call(s32[2304]{0:T(1024)} %get-tuple-element.18.groups_of, s32[2304]{0:T(1024)} %get-tuple-element.17.firsts, s32[2304]{0:T(1024)} %get-tuple-element.16.ends, s32[4096]{0:T(1024)} %add_select_fusion.2.order, s32[9]{0:T(128)} %pad_add_fusion.span, ...), custom_call_target="tpu_custom_call" | custom-call | flops 93012885504 | bytes 8650752 | tf_op jit(solution)/shard_map/pallas_call | solution.py:143
  293.4 2.4 collective-permute-start.19
  295.8 32.3 %shard_map.65 = (f32[2,16,64,256]{3,2,1,0:T(8,128)}, f32[2,16,64,256]{3,2,1,0:T(8,128)}) custom-call(s32[2304]{0:T(1024)} %get-tuple-element.18.groups_of, s32[2304]{0:T(1024)} %get-tuple-element.17.firsts, s32[2304]{0:T(1024)} %get-tuple-element.16.ends, s32[4096]{0:T(1024)} %add_select_fusion.2.order, s32[9]{0:T(128)} %pad_add_fusion.span, ...), custom_call_target="tpu_custom_call" | custom-call | flops 13287555072 | bytes 8650752 | tf_op jit(solution)/shard_map/pallas_call | solution.py:143
  328.4 0.7 fusion.3
  329.2 0.6 pad_maximum_fusion.1.yh
  329.8 0.3 fusion.13
  330.1 0.7 fusion.1
  330.8 1.7 collective-permute-done.20.refs_3_
  332.6 1.3 copy-done
  333.9 30.1 %shard_map.66 = f32[2,128,64,256]{3,2,1,0:T(8,128)} custom-call(bf16[128,256]{1,0:T(8,128)(2,1)} %pad_maximum_fusion.1.yh, bf16[128,128]{1,0:T(8,128)(2,1)} %get-tuple-element.21.yl, bf16[256,256]{1,0:T(8,128)(2,1)} %get-tuple-element.20.xh, bf16[256,256]{1,0:T(8,128)(2,1)} %get-tuple-element.19.xl, f32[2,112,64,256]{3,2,1,0:T(8,128)} %get-tuple-element.12.refs_0_, ...), custom_call_target="tpu_custom_call" | custom-call | tf_op jit(solution)/shard_map/pallas_call | solution.py:226
  (101 shorter events, 2.9 us)
Async XLA Ops:
  3.8 83.3 %copy-start.1 = (f32[264,512]{1,0:T(8,128)}, f32[264,512]{1,0:T(8,128)S(1)}, u32[]{:S(2)}) copy-start(f32[264,512]{1,0:T(8,128)S(1)} %pad_maximum_fusion.refs_0_) | copy-start | bytes 1622020
  3.8 13.2 %collective-permute-start.1 = (f32[264,512]{1,0:T(8,128)S(1)}, f32[264,512]{1,0:T(8,128)S(1)}, u32[]{:S(2)}, u32[]{:S(2)}) collective-permute-start(f32[264,512]{1,0:T(8,128)S(1)} %pad_maximum_fusion.refs_0_), channel_id=1, source_target_pairs={{0,4},{1,5},{2,6},{3,7},{4,0},{5,1},{6,2},{7,3},{8,12},{9,13},{10,... | collective-permute-start | bytes 1622024 | tf_op jit(solution)/shard_map/ppermute | solution.py:262
  5.1 36.1 %collective-permute-start.11 = (f32[264,512]{1,0:T(8,128)S(1)}, f32[264,512]{1,0:T(8,128)S(1)}, u32[]{:S(2)}, u32[]{:S(2)}) collective-permute-start(f32[264,512]{1,0:T(8,128)S(1)} %pad_maximum_fusion.refs_0_), channel_id=1, source_target_pairs={{0,24},{8,16},{16,8},{24,0},{1,25},{9,17},{17,9},{25,1},{2,26},{10... | collective-permute-start | bytes 1622024 | tf_op jit(solution)/shard_map/ppermute | solution.py:262
  5.3 45.9 %collective-permute-start.7 = (f32[264,512]{1,0:T(8,128)S(1)}, f32[264,512]{1,0:T(8,128)}, u32[]{:S(2)}, u32[]{:S(2)}) collective-permute-start(f32[264,512]{1,0:T(8,128)S(1)} %pad_maximum_fusion.refs_0_), channel_id=1, source_target_pairs={{0,16},{8,24},{16,0},{24,8},{1,17},{9,25},{17,1},{25,9},{2,18},{10... | collective-permute-start | bytes 1622024 | tf_op jit(solution)/shard_map/ppermute | solution.py:262
  8.5 44.6 %collective-permute-start.3 = (f32[264,512]{1,0:T(8,128)S(1)}, f32[264,512]{1,0:T(8,128)}, u32[]{:S(2)}, u32[]{:S(2)}) collective-permute-start(f32[264,512]{1,0:T(8,128)S(1)} %pad_maximum_fusion.refs_0_), channel_id=1, source_target_pairs={{0,8},{8,0},{16,24},{24,16},{1,9},{9,1},{17,25},{25,17},{2,10},{10... | collective-permute-start | bytes 1622024 | tf_op jit(solution)/shard_map/ppermute | solution.py:262
  8.5 45.3 %collective-permute-start = (f32[264,512]{1,0:T(8,128)S(1)}, f32[264,512]{1,0:T(8,128)S(1)}, u32[]{:S(2)}, u32[]{:S(2)}) collective-permute-start(f32[264,512]{1,0:T(8,128)S(1)} %pad_maximum_fusion.refs_0_), channel_id=1, source_target_pairs={{0,2},{1,3},{2,0},{3,1},{4,6},{5,7},{6,4},{7,5},{8,10},{9,11},{10,... | collective-permute-start | bytes 1622024 | tf_op jit(solution)/shard_map/ppermute | solution.py:262
  17.0 70.1 %copy-start.2 = (f32[264,512]{1,0:T(8,128)}, f32[264,512]{1,0:T(8,128)S(1)}, u32[]{:S(2)}) copy-start(f32[264,512]{1,0:T(8,128)S(1)} %collective-permute-done.1.refs_2_) | copy-start | bytes 1622020
  17.0 38.5 %collective-permute-start.2 = (f32[136,512]{1,0:T(8,128)S(1)}, f32[136,512]{1,0:T(8,128)S(1)}, u32[]{:S(2)}, u32[]{:S(2)}) collective-permute-start(f32[136,512]{1,0:T(8,128)S(1)} %slice.116), channel_id=1, source_target_pairs={{0,2},{1,3},{2,0},{3,1},{4,6},{5,7},{6,4},{7,5},{8,10},{9,11},{10,... | collective-permute-start | bytes 835592 | tf_op jit(solution)/shard_map/ppermute | solution.py:262
  41.2 22.4 %copy-start.15 = (f32[264,512]{1,0:T(8,128)}, f32[264,512]{1,0:T(8,128)S(1)}, u32[]{:S(2)}) copy-start(f32[264,512]{1,0:T(8,128)S(1)} %collective-permute-done.11.refs_15_) | copy-start | bytes 1622020
  41.2 14.6 %collective-permute-start.13 = (f32[264,512]{1,0:T(8,128)S(1)}, f32[264,512]{1,0:T(8,128)S(1)}, u32[]{:S(2)}, u32[]{:S(2)}) collective-permute-start(f32[264,512]{1,0:T(8,128)S(1)} %collective-permute-done.11.refs_15_), channel_id=1, source_target_pairs={{0,4},{1,5},{2,6},{3,7},{4,0},{5,1},{6,2},{7,3},{8,12},{9,13},{10,... | collective-permute-start | bytes 1622024 | tf_op jit(solution)/shard_map/ppermute | solution.py:262
  51.1 12.5 %collective-permute-start.12 = (f32[264,512]{1,0:T(8,128)S(1)}, f32[264,512]{1,0:T(8,128)S(1)}, u32[]{:S(2)}, u32[]{:S(2)}) collective-permute-start(f32[264,512]{1,0:T(8,128)S(1)} %collective-permute-done.11.refs_15_), channel_id=1, source_target_pairs={{0,2},{1,3},{2,0},{3,1},{4,6},{5,7},{6,4},{7,5},{8,10},{9,11},{10,... | collective-permute-start | bytes 1622024 | tf_op jit(solution)/shard_map/ppermute | solution.py:262
  53.8 18.2 %copy-start.6 = (f32[264,512]{1,0:T(8,128)}, f32[264,512]{1,0:T(8,128)S(1)}, u32[]{:S(2)}) copy-start(f32[264,512]{1,0:T(8,128)S(1)} %collective-permute-done.refs_1_) | copy-start | bytes 1622020
  53.9 51.1 %copy-start.10 = (s32[16,256]{1,0:T(8,128)S(1)}, s32[16,256]{1,0:T(8,128)}, u32[]{:S(2)}) copy-start(s32[16,256]{1,0:T(8,128)} %constant.162) | copy-start | bytes 49156
  54.0 62.7 %collective-permute-start.15 = (f32[128,512]{1,0:T(8,128)S(1)}, f32[128,512]{1,0:T(8,128)}, u32[]{:S(2)}, u32[]{:S(2)}) collective-permute-start(f32[128,512]{1,0:T(8,128)S(1)} %slice.134), channel_id=1, source_target_pairs={{0,4},{1,5},{2,6},{3,7},{4,0},{5,1},{6,2},{7,3},{8,12},{9,13},{10,... | collective-permute-start | bytes 786440 | tf_op jit(solution)/shard_map/ppermute | solution.py:262
  54.2 17.5 %collective-permute-start.9 = (f32[264,512]{1,0:T(8,128)}, f32[264,512]{1,0:T(8,128)S(1)}, u32[]{:S(2)}, u32[]{:S(2)}) collective-permute-start(f32[264,512]{1,0:T(8,128)} %collective-permute-done.7.refs_10_), channel_id=1, source_target_pairs={{0,4},{1,5},{2,6},{3,7},{4,0},{5,1},{6,2},{7,3},{8,12},{9,13},{10,... | collective-permute-start | bytes 1622024 | tf_op jit(solution)/shard_map/ppermute | solution.py:262
  55.5 61.2 %copy-start.11 = (f32[136,512]{1,0:T(8,128)}, f32[136,512]{1,0:T(8,128)S(1)}, u32[]{:S(2)}) copy-start(f32[136,512]{1,0:T(8,128)S(1)} %collective-permute-done.2.refs_4_) | copy-start | bytes 835588
  55.5 19.6 %collective-permute-start.8 = (f32[264,512]{1,0:T(8,128)}, f32[264,512]{1,0:T(8,128)S(1)}, u32[]{:S(2)}, u32[]{:S(2)}) collective-permute-start(f32[264,512]{1,0:T(8,128)} %collective-permute-done.7.refs_10_), channel_id=1, source_target_pairs={{0,2},{1,3},{2,0},{3,1},{4,6},{5,7},{6,4},{7,5},{8,10},{9,11},{10,... | collective-permute-start | bytes 1622024 | tf_op jit(solution)/shard_map/ppermute | solution.py:262
  55.8 60.9 %copy-start.3 = (f32[264,512]{1,0:T(8,128)}, f32[264,512]{1,0:T(8,128)S(1)}, u32[]{:S(2)}) copy-start(f32[264,512]{1,0:T(8,128)S(1)} %collective-permute-done.13.refs_17_) | copy-start | bytes 1622020
  55.8 27.5 %collective-permute-start.5 = (f32[264,512]{1,0:T(8,128)}, f32[264,512]{1,0:T(8,128)S(1)}, u32[]{:S(2)}, u32[]{:S(2)}) collective-permute-start(f32[264,512]{1,0:T(8,128)} %collective-permute-done.3.refs_5_), channel_id=1, source_target_pairs={{0,4},{1,5},{2,6},{3,7},{4,0},{5,1},{6,2},{7,3},{8,12},{9,13},{10,... | collective-permute-start | bytes 1622024 | tf_op jit(solution)/shard_map/ppermute | solution.py:262
  63.6 41.0 %copy-start.7 = (f32[264,512]{1,0:T(8,128)}, f32[264,512]{1,0:T(8,128)S(1)}, u32[]{:S(2)}) copy-start(f32[264,512]{1,0:T(8,128)S(1)} %collective-permute-done.12.refs_16_) | copy-start | bytes 1622020
  63.6 23.1 %collective-permute-start.4 = (f32[264,512]{1,0:T(8,128)}, f32[264,512]{1,0:T(8,128)S(1)}, u32[]{:S(2)}, u32[]{:S(2)}) collective-permute-start(f32[264,512]{1,0:T(8,128)} %collective-permute-done.3.refs_5_), channel_id=1, source_target_pairs={{0,2},{1,3},{2,0},{3,1},{4,6},{5,7},{6,4},{7,5},{8,10},{9,11},{10,... | collective-permute-start | bytes 1622024 | tf_op jit(solution)/shard_map/ppermute | solution.py:262
  71.7 15.3 %copy-start.4 = (f32[264,512]{1,0:T(8,128)}, f32[264,512]{1,0:T(8,128)S(1)}, u32[]{:S(2)}) copy-start(f32[264,512]{1,0:T(8,128)S(1)} %collective-permute-done.9.refs_12_) | copy-start | bytes 1622020
  71.7 21.0 %collective-permute-start.14 = (f32[136,512]{1,0:T(8,128)S(1)}, f32[136,512]{1,0:T(8,128)S(1)}, u32[]{:S(2)}, u32[]{:S(2)}) collective-permute-start(f32[136,512]{1,0:T(8,128)S(1)} %slice.131), channel_id=1, source_target_pairs={{0,2},{1,3},{2,0},{3,1},{4,6},{5,7},{6,4},{7,5},{8,10},{9,11},{10,... | collective-permute-start | bytes 835592 | tf_op jit(solution)/shard_map/ppermute | solution.py:262
  75.1 29.5 %copy-start.8 = (f32[264,512]{1,0:T(8,128)}, f32[264,512]{1,0:T(8,128)S(1)}, u32[]{:S(2)}) copy-start(f32[264,512]{1,0:T(8,128)S(1)} %collective-permute-done.8.refs_11_) | copy-start | bytes 1622020
  75.1 41.6 %collective-permute-start.18 = (f32[128,512]{1,0:T(8,128)S(1)}, f32[128,512]{1,0:T(8,128)}, u32[]{:S(2)}, u32[]{:S(2)}) collective-permute-start(f32[128,512]{1,0:T(8,128)S(1)} %slice.137), channel_id=1, source_target_pairs={{0,4},{1,5},{2,6},{3,7},{4,0},{5,1},{6,2},{7,3},{8,12},{9,13},{10,... | collective-permute-start | bytes 786440 | tf_op jit(solution)/shard_map/ppermute | solution.py:262
  83.3 21.3 %copy-start.5 = (f32[264,512]{1,0:T(8,128)}, f32[264,512]{1,0:T(8,128)S(1)}, u32[]{:S(2)}) copy-start(f32[264,512]{1,0:T(8,128)S(1)} %collective-permute-done.5.refs_7_) | copy-start | bytes 1622020
  83.3 15.3 %collective-permute-start.10 = (f32[136,512]{1,0:T(8,128)S(1)}, f32[136,512]{1,0:T(8,128)S(1)}, u32[]{:S(2)}, u32[]{:S(2)}) collective-permute-start(f32[136,512]{1,0:T(8,128)S(1)} %slice.126), channel_id=1, source_target_pairs={{0,2},{1,3},{2,0},{3,1},{4,6},{5,7},{6,4},{7,5},{8,10},{9,11},{10,... | collective-permute-start | bytes 835592 | tf_op jit(solution)/shard_map/ppermute | solution.py:262
  86.7 18.0 %copy-start.9 = (f32[264,512]{1,0:T(8,128)}, f32[264,512]{1,0:T(8,128)S(1)}, u32[]{:S(2)}) copy-start(f32[264,512]{1,0:T(8,128)S(1)} %collective-permute-done.4.refs_6_) | copy-start | bytes 1622020
  86.7 30.0 %collective-permute-start.17 = (f32[128,512]{1,0:T(8,128)S(1)}, f32[128,512]{1,0:T(8,128)}, u32[]{:S(2)}, u32[]{:S(2)}) collective-permute-start(f32[128,512]{1,0:T(8,128)S(1)} %slice.136), channel_id=1, source_target_pairs={{0,4},{1,5},{2,6},{3,7},{4,0},{5,1},{6,2},{7,3},{8,12},{9,13},{10,... | collective-permute-start | bytes 786440 | tf_op jit(solution)/shard_map/ppermute | solution.py:262
  92.7 11.9 %copy-start.12 = (f32[136,512]{1,0:T(8,128)}, f32[136,512]{1,0:T(8,128)S(1)}, u32[]{:S(2)}) copy-start(f32[136,512]{1,0:T(8,128)S(1)} %collective-permute-done.14.refs_19_) | copy-start | bytes 835588
  92.7 11.8 %collective-permute-start.6 = (f32[136,512]{1,0:T(8,128)S(1)}, f32[136,512]{1,0:T(8,128)S(1)}, u32[]{:S(2)}, u32[]{:S(2)}) collective-permute-start(f32[136,512]{1,0:T(8,128)S(1)} %slice.121), channel_id=1, source_target_pairs={{0,2},{1,3},{2,0},{3,1},{4,6},{5,7},{6,4},{7,5},{8,10},{9,11},{10,... | collective-permute-start | bytes 835592 | tf_op jit(solution)/shard_map/ppermute | solution.py:262
  98.6 6.0 %copy-start.13 = (f32[136,512]{1,0:T(8,128)}, f32[136,512]{1,0:T(8,128)S(1)}, u32[]{:S(2)}) copy-start(f32[136,512]{1,0:T(8,128)S(1)} %collective-permute-done.10.refs_14_) | copy-start | bytes 835588
  98.6 18.1 %collective-permute-start.16 = (f32[128,512]{1,0:T(8,128)S(1)}, f32[128,512]{1,0:T(8,128)S(1)}, u32[]{:S(2)}, u32[]{:S(2)}) collective-permute-start(f32[128,512]{1,0:T(8,128)S(1)} %slice.135), channel_id=1, source_target_pairs={{0,4},{1,5},{2,6},{3,7},{4,0},{5,1},{6,2},{7,3},{8,12},{9,13},{10,... | collective-permute-start | bytes 786440 | tf_op jit(solution)/shard_map/ppermute | solution.py:262
  104.6 12.2 %copy-start.14 = (f32[136,512]{1,0:T(8,128)}, f32[136,512]{1,0:T(8,128)S(1)}, u32[]{:S(2)}) copy-start(f32[136,512]{1,0:T(8,128)S(1)} %collective-permute-done.6.refs_9_) | copy-start | bytes 835588
  116.7 0.7 copy-start.16
  293.4 39.1 %collective-permute-start.19 = (f32[2,112,64,256]{3,2,1,0:T(8,128)}, f32[2,112,64,256]{3,2,1,0:T(8,128)}, u32[]{:S(2)}, u32[]{:S(2)}) collective-permute-start(f32[2,112,64,256]{3,2,1,0:T(8,128)} %get-tuple-element.13), channel_id=1, source_target_pairs={{0,1},{1,0},{2,3},{3,2},{4,5},{5,4},{6,7},{7,6},{8,9},{9,8},{10,11... | collective-permute-start | bytes 44040200 | tf_op jit(solution)/shard_map/ppermute | solution.py:336
  328.1 4.4 %collective-permute-start.20 = (f32[2,16,64,256]{3,2,1,0:T(8,128)}, f32[2,16,64,256]{3,2,1,0:T(8,128)S(1)}, u32[]{:S(2)}, u32[]{:S(2)}) collective-permute-start(f32[2,16,64,256]{3,2,1,0:T(8,128)} %get-tuple-element.15), channel_id=1, source_target_pairs={{0,1},{1,0},{2,3},{3,2},{4,5},{5,4},{6,7},{7,6},{8,9},{9,8},{10,11... | collective-permute-start | bytes 6291464 | tf_op jit(solution)/shard_map/ppermute | solution.py:336
  332.6 1.3 copy-start
